TPU v7x, 32 devices: a whole 2x2x4 slice. The times are simulated.
32 devices in a mesh: dp: 4 (over x, core), fsdp: 8 (over z, y).
Axes of the slice: x: 2, y: 2, z: 4, core: 2. Of those that a mesh axis runs over, the one named last changes fastest.
Arguments:
- block_input: bfloat16 [8192, 2048], P(('dp', 'fsdp')), may hold values from -6 to 6
- segment_ids: int32 [8192], P(('dp', 'fsdp')), may hold values from -1 to 3, as said below
- w_query: bfloat16 [2048, 2048], P('fsdp'), may hold values from -0.125 to 0.125
- w_key: bfloat16 [2048, 2048], P('fsdp'), may hold values from -0.125 to 0.125
- w_value: bfloat16 [2048, 2048], P('fsdp'), may hold values from -0.125 to 0.125
- w_out: bfloat16 [2048, 2048], P('fsdp'), may hold values from -0.125 to 0.125
- gain_query: bfloat16 [2048], P('fsdp'), may hold values from 0.25 to 1.75
- gain_key: bfloat16 [2048], P('fsdp'), may hold values from 0.25 to 1.75
- gain_attn: bfloat16 [2048], P('fsdp'), may hold values from 0.25 to 1.75
- w_gate: bfloat16 [2048, 8192], P('fsdp'), may hold values from -0.125 to 0.125
- w_up: bfloat16 [2048, 8192], P('fsdp'), may hold values from -0.125 to 0.125
- w_down: bfloat16 [8192, 2048], P('fsdp'), may hold values from -0.0625 to 0.0625
- gain_mlp: bfloat16 [2048], P('fsdp'), may hold values from 0.25 to 1.75
- out_cotangent: bfloat16 [8192, 2048], P(('dp', 'fsdp')), may hold values from -6 to 6
Outputs:
- block_output: bfloat16 [8192, 2048], P(('dp', 'fsdp'))
- input_grad: float32 [8192, 2048], P(('dp', 'fsdp'))
- grad_w_query: float32 [2048, 2048], P('fsdp')
- grad_w_key: float32 [2048, 2048], P('fsdp')
- grad_w_value: float32 [2048, 2048], P('fsdp')
- grad_w_out: float32 [2048, 2048], P('fsdp')
- grad_gain_query: float32 [2048], P('fsdp')
- grad_gain_key: float32 [2048], P('fsdp')
- grad_gain_attn: float32 [2048], P('fsdp')
- grad_w_gate: float32 [2048, 8192], P('fsdp')
- grad_w_up: float32 [2048, 8192], P('fsdp')
- grad_w_down: float32 [8192, 2048], P('fsdp')
- grad_gain_mlp: float32 [2048], P('fsdp')
Inputs may be any that keep to these rules, and one draw needn't show every extreme that they name: `segment_ids`: each aligned block of 128 rows is one micro-batch: its live rows come first with segment ids 0, 1, ... that never fall, each segment contiguous, followed by padding rows of id -1; a micro-batch has 64 or more live rows and at most 4 segments; some micro-batches have no padding.
All inputs are finite; a program needn't handle non-finite values.
Results may differ from a plain program's by a relative error of at most 0.02.
Values may be sent and summed in bfloat16 or wider, within the bound.
No kernel may reach another device: no remote copies, remote signals or barrier semaphores. Data moves between devices by JAX's collectives and lax.ppermute only.
A program may use at most 512 MiB of HBM per device.

v0:
```python
import jax
import jax.numpy as jnp
from jax import lax
from jax.sharding import PartitionSpec as P

D = 2048
HEADS = 16
HEAD_DIM = 128
MB = 128


EPS = 1e-06
THETA = 500000.0
NEG = -1e30


def rms_norm(values, gain_vec):
    return values * lax.rsqrt(jnp.mean(values * values, axis=-1, keepdims=True) + EPS) * gain_vec


def rotate(values, cosine, sine_table):
    half_dim = values.shape[-1] // 2
    first_half = values[..., :half_dim]
    second = values[..., half_dim:]
    return jnp.concatenate(
        [first_half * cosine - second * sine_table, second * cosine + first_half * sine_table],
        axis=-1,
    )


def mask_tables(segments, head_dim):
    row_total = segments.shape[1]
    row_index = jnp.arange(row_total, dtype=jnp.int32)
    same_seg = segments[:, :, None] == segments[:, None, :]
    allowed = jnp.logical_and(same_seg, row_index[:, None] >= row_index[None, :])
    position = jnp.sum(allowed.astype(jnp.int32), axis=2) - 1
    half_dim = head_dim // 2
    frequency = THETA ** (-2.0 * jnp.arange(half_dim, dtype=jnp.float32) / head_dim)
    angles = position.astype(jnp.float32)[:, :, None, None] * frequency
    return (allowed, jnp.cos(angles), jnp.sin(angles))


def product(left_rows, right_rows):
    return jnp.dot(left_rows, right_rows, preferred_element_type=jnp.float32)


def product_nt(left_rows, right_rows):
    return lax.dot_general(
        left_rows, right_rows, (((1,), (1,)), ((), ())), preferred_element_type=jnp.float32
    )


def product_tn(left_rows, right_rows):
    return lax.dot_general(
        left_rows, right_rows, (((0,), (0,)), ((), ())), preferred_element_type=jnp.float32
    )


def swiglu(gate_vals, up_vals):
    return jax.nn.silu(gate_vals) * up_vals


def body(
    block_input,
    segment_ids,
    w_query,
    w_key,
    w_value,
    w_out,
    gain_query,
    gain_key,
    gain_attn,
    w_gate,
    w_up,
    w_down,
    gain_mlp,
    out_cotangent,
):
    row_count = block_input.shape[0]
    micro_count = row_count // MB
    segments = segment_ids.reshape(micro_count, MB)
    allowed, cosine, sine_table = mask_tables(segments, HEAD_DIM)
    live_rows = (segment_ids >= 0).astype(jnp.float32)[:, None]
    scaling = HEAD_DIM ** (-0.5)
    input_full = block_input.astype(jnp.float32)

    def heads(values):
        return values.reshape(micro_count, MB, HEADS, HEAD_DIM)

    def prepare(raw_rows, gain_vec):
        return rotate(heads(rms_norm(raw_rows, gain_vec)), cosine, sine_table)

    def owner_grad(left_rows, right_rows):
        return lax.psum_scatter(
            product_tn(left_rows, right_rows).astype(jnp.bfloat16),
            "fsdp",
            scatter_dimension=0,
            tiled=True,
        ).astype(jnp.float32)

    pieces = (
        lax.all_gather(w_query, "fsdp", axis=0, tiled=True),
        lax.all_gather(w_key, "fsdp", axis=0, tiled=True),
        lax.all_gather(w_value, "fsdp", axis=0, tiled=True),
        lax.all_gather(gain_query, "fsdp", axis=0, tiled=True),
        lax.all_gather(gain_key, "fsdp", axis=0, tiled=True),
    )
    columns = block_input
    q_raw = product(columns, pieces[0])
    k_raw = product(columns, pieces[1])
    v_raw = product(columns, pieces[2])
    gain_q_full = pieces[3]
    gain_k_full = pieces[4]
    query_rot, pull_query = jax.vjp(prepare, q_raw, gain_q_full.astype(jnp.float32))
    key_rot, pull_key = jax.vjp(prepare, k_raw, gain_k_full.astype(jnp.float32))
    query_low = query_rot.astype(jnp.bfloat16)
    key_low = key_rot.astype(jnp.bfloat16)
    value_low = heads(v_raw.astype(jnp.bfloat16))

    def masked_scores():
        raw_scores = (
            jnp.einsum("gqhd,gkhd->ghqk", query_low, key_low, preferred_element_type=jnp.float32)
            * scaling
        )
        return jnp.where(allowed[:, None], raw_scores, NEG)

    scores = masked_scores()
    row_top = jnp.max(scores, axis=-1, keepdims=True)
    exp_scores = jnp.exp(scores - row_top)
    row_sum = jnp.sum(exp_scores, axis=-1, keepdims=True)
    log_total = row_top + jnp.log(row_sum)
    probs_low = (exp_scores / row_sum).astype(jnp.bfloat16)
    attended = (
        jnp.einsum("ghqk,gkhd->gqhd", probs_low, value_low, preferred_element_type=jnp.float32)
        .reshape(row_count, D)
        .astype(jnp.bfloat16)
    )
    pieces = (
        lax.all_gather(w_out, "fsdp", axis=0, tiled=True),
        lax.all_gather(gain_attn, "fsdp", axis=0, tiled=True),
    )
    columns = attended
    branch = product(columns, pieces[0])
    gain_a_full = pieces[1]
    attn_normed, pull_attn = jax.vjp(rms_norm, branch, gain_a_full.astype(jnp.float32))
    middle = input_full + attn_normed
    middle_low = middle.astype(jnp.bfloat16)
    pieces = (
        lax.all_gather(w_gate, "fsdp", axis=0, tiled=True),
        lax.all_gather(w_up, "fsdp", axis=0, tiled=True),
    )
    columns = middle_low
    gate = product(columns, pieces[0])
    up_proj = product(columns, pieces[1])
    hidden_f32, pull_swiglu = jax.vjp(swiglu, gate, up_proj)
    hidden_low = hidden_f32.astype(jnp.bfloat16)
    pieces = (
        lax.all_gather(w_down, "fsdp", axis=0, tiled=True),
        lax.all_gather(gain_mlp, "fsdp", axis=0, tiled=True),
    )
    columns = hidden_low
    mixed = product(columns, pieces[0])
    gain_m_full = pieces[1]
    mlp_normed, pull_mlp = jax.vjp(rms_norm, mixed, gain_m_full.astype(jnp.float32))
    block_output = ((middle + mlp_normed) * live_rows).astype(jnp.bfloat16)
    grad_rows = out_cotangent.astype(jnp.float32) * live_rows
    d_mixed, d_gain_mlp = pull_mlp(grad_rows)
    d_mixed_low = d_mixed.astype(jnp.bfloat16)
    grad_down = owner_grad(hidden_low, d_mixed_low)
    d_hidden = product_nt(d_mixed_low, lax.all_gather(w_down, "fsdp", axis=0, tiled=True))
    d_gate, d_up = pull_swiglu(d_hidden)
    d_gate_low = d_gate.astype(jnp.bfloat16)
    d_up_low = d_up.astype(jnp.bfloat16)
    grad_gate = owner_grad(middle_low, d_gate_low)
    grad_up = owner_grad(middle_low, d_up_low)
    pieces = lax.all_gather((w_gate, w_up), "fsdp", axis=0, tiled=True)
    d_middle = grad_rows + (product_nt(d_gate_low, pieces[0]) + product_nt(d_up_low, pieces[1]))
    d_branch, d_gain_attn = pull_attn(d_middle)
    d_branch_low = d_branch.astype(jnp.bfloat16)
    grad_out = owner_grad(attended, d_branch_low)
    d_attended = product_nt(d_branch_low, lax.all_gather(w_out, "fsdp", axis=0, tiled=True))
    d_att_low = heads(d_attended.astype(jnp.bfloat16))
    probs = jnp.exp(masked_scores() - log_total)
    probs_back = probs.astype(jnp.bfloat16)
    d_probs = jnp.einsum(
        "gqhd,gkhd->ghqk", d_att_low, value_low, preferred_element_type=jnp.float32
    )
    d_value_low = (
        jnp.einsum("ghqk,gqhd->gkhd", probs_back, d_att_low, preferred_element_type=jnp.float32)
        .reshape(row_count, D)
        .astype(jnp.bfloat16)
    )
    row_dot = jnp.sum(probs * d_probs, axis=-1, keepdims=True)
    d_scores = (probs * (d_probs - row_dot)).astype(jnp.bfloat16)
    d_query = (
        jnp.einsum("ghqk,gkhd->gqhd", d_scores, key_low, preferred_element_type=jnp.float32)
        * scaling
    )
    d_key = (
        jnp.einsum("ghqk,gqhd->gkhd", d_scores, query_low, preferred_element_type=jnp.float32)
        * scaling
    )
    d_q_raw, d_gain_query = pull_query(d_query)
    d_k_raw, d_gain_key = pull_key(d_key)
    d_q_low = d_q_raw.astype(jnp.bfloat16)
    d_k_low = d_k_raw.astype(jnp.bfloat16)
    grad_query = owner_grad(block_input, d_q_low)
    grad_key = owner_grad(block_input, d_k_low)
    grad_value = owner_grad(block_input, d_value_low)
    pieces = lax.all_gather((w_query, w_key, w_value), "fsdp", axis=0, tiled=True)
    d_input = d_middle + (
        product_nt(d_q_low, pieces[0])
        + product_nt(d_k_low, pieces[1])
        + product_nt(d_value_low, pieces[2])
    )
    part_q, part_k, part_a, part_m = (
        lax.psum_scatter(
            d_gain_query.astype(jnp.bfloat16), "fsdp", scatter_dimension=0, tiled=True
        ).astype(jnp.float32),
        lax.psum_scatter(
            d_gain_key.astype(jnp.bfloat16), "fsdp", scatter_dimension=0, tiled=True
        ).astype(jnp.float32),
        lax.psum_scatter(
            d_gain_attn.astype(jnp.bfloat16), "fsdp", scatter_dimension=0, tiled=True
        ).astype(jnp.float32),
        lax.psum_scatter(
            d_gain_mlp.astype(jnp.bfloat16), "fsdp", scatter_dimension=0, tiled=True
        ).astype(jnp.float32),
    )
    shards = (
        lax.psum(grad_query.astype(jnp.bfloat16), "dp").astype(jnp.float32),
        lax.psum(grad_key.astype(jnp.bfloat16), "dp").astype(jnp.float32),
        lax.psum(grad_value.astype(jnp.bfloat16), "dp").astype(jnp.float32),
        lax.psum(grad_out.astype(jnp.bfloat16), "dp").astype(jnp.float32),
        lax.psum(part_q.astype(jnp.bfloat16), "dp").astype(jnp.float32),
        lax.psum(part_k.astype(jnp.bfloat16), "dp").astype(jnp.float32),
        lax.psum(part_a.astype(jnp.bfloat16), "dp").astype(jnp.float32),
        lax.psum(grad_gate.astype(jnp.bfloat16), "dp").astype(jnp.float32),
        lax.psum(grad_up.astype(jnp.bfloat16), "dp").astype(jnp.float32),
        lax.psum(grad_down.astype(jnp.bfloat16), "dp").astype(jnp.float32),
        lax.psum(part_m.astype(jnp.bfloat16), "dp").astype(jnp.float32),
    )
    return (
        block_output,
        d_input,
        shards[0],
        shards[1],
        shards[2],
        shards[3],
        shards[4],
        shards[5],
        shards[6],
        shards[7],
        shards[8],
        shards[9],
        shards[10],
    )


def solution(mesh):
    in_specs = (
        P(("dp", "fsdp"), None),
        P(("dp", "fsdp")),
        P("fsdp", None),
        P("fsdp", None),
        P("fsdp", None),
        P("fsdp", None),
        P("fsdp"),
        P("fsdp"),
        P("fsdp"),
        P("fsdp", None),
        P("fsdp", None),
        P("fsdp", None),
        P("fsdp"),
        P(("dp", "fsdp"), None),
    )
    out_specs = (
        P(("dp", "fsdp"), None),
        P(("dp", "fsdp"), None),
        P("fsdp", None),
        P("fsdp", None),
        P("fsdp", None),
        P("fsdp", None),
        P("fsdp"),
        P("fsdp"),
        P("fsdp"),
        P("fsdp", None),
        P("fsdp", None),
        P("fsdp", None),
        P("fsdp"),
    )
    return jax.shard_map(body, mesh=mesh, in_specs=in_specs, out_specs=out_specs, check_vma=False)
```

profile of v0, /device:TPU:0, one launch (start us, length us, event | category | flops | bytes accessed | tf_op | source)
XLA Modules:
  0.0 5084.2 jit_solution(18411725040498475680)
XLA Ops:
  12.1 22.3 all-gather.3
  34.4 16.5 all-gather.2
  50.9 18.6 all-gather.1
  69.5 16.6 all-gather
  87.0 51.2 %all-gather.12.cloned.1.call-done = bf16[2048,2048]{1,0:T(8,128)(2,1)} async-done(((bf16[256,2048]{1,0:T(8,128)(2,1)}), bf16[2048,2048]{1,0:T(8,128)(2,1)}) %all-gather.12.cloned.1.call-update) | async-done | bytes 8388624 | tf_op jit(solution)/shard_map/all_gather | solution.py:104
  145.1 118.3 %all-gather.16.cloned.1.call-done = bf16[2048,2048]{1,0:T(8,128)(2,1)} async-done(((bf16[256,2048]{1,0:T(8,128)(2,1)}), bf16[2048,2048]{1,0:T(8,128)(2,1)}) %all-gather.16.cloned.1.call-update) | async-done | bytes 8388624 | tf_op jit(solution)/shard_map/all_gather | solution.py:103
  270.9 117.8 %all-gather.14.cloned.1.call-done = bf16[2048,2048]{1,0:T(8,128)(2,1)} async-done(((bf16[256,2048]{1,0:T(8,128)(2,1)}), bf16[2048,2048]{1,0:T(8,128)(2,1)}) %all-gather.14.cloned.1.call-update) | async-done | bytes 8388624 | tf_op jit(solution)/shard_map/all_gather | solution.py:102
  406.9 106.9 %all-gather.18.cloned.1.call-done = bf16[2048,2048]{1,0:T(8,128)(2,1)} async-done(((bf16[256,2048]{1,0:T(8,128)(2,1)}), bf16[2048,2048]{1,0:T(8,128)(2,1)}) %all-gather.18.cloned.1.call-update) | async-done | bytes 8388624 | tf_op jit(solution)/shard_map/all_gather | solution.py:139
  521.3 629.8 %all-gather.20.cloned.1.call-done = bf16[2048,8192]{1,0:T(8,128)(2,1)} async-done(((bf16[256,8192]{1,0:T(8,128)(2,1)}), bf16[2048,8192]{1,0:T(8,128)(2,1)}) %all-gather.20.cloned.1.call-update) | async-done | bytes 33554448 | tf_op jit(solution)/shard_map/all_gather | solution.py:149
  1151.1 19.3 fusion.48
  1170.4 619.9 %all-gather.22.cloned.1.call-done = bf16[2048,8192]{1,0:T(8,128)(2,1)} async-done(((bf16[256,8192]{1,0:T(8,128)(2,1)}), bf16[2048,8192]{1,0:T(8,128)(2,1)}) %all-gather.22.cloned.1.call-update) | async-done | bytes 33554448 | tf_op jit(solution)/shard_map/all_gather | solution.py:150
  1790.2 24.4 multiply_convert_fusion.1
  1814.7 614.8 %all-gather.24.cloned.1.call-done = bf16[8192,2048]{1,0:T(8,128)(2,1)} async-done(((bf16[1024,2048]{1,0:T(8,128)(2,1)}), bf16[8192,2048]{1,0:T(8,128)(2,1)}) %all-gather.24.cloned.1.call-update) | async-done | bytes 33554448 | tf_op jit(solution)/shard_map/all_gather | solution.py:158
  2429.5 16.6 multiply_reduce_fusion.7
  2449.3 23.9 multiply_convert_fusion
  2473.2 16.9 fusion.49
  2490.1 16.2 multiply_reduce_fusion.1
  2530.8 7.0 convert_bitcast_fusion
  2571.6 16.8 convolution_convert_fusion
  2589.6 16.1 convolution_convert_fusion.1
  2606.0 16.3 convolution_convert_fusion.2
  2622.3 41.1 reduce-scatter.14.cloned.1.call-done
  2663.5 153.1 %reduce-scatter.12.cloned.1.call-done = bf16[256,2048]{0,1:T(8,128)(2,1)} async-done(((bf16[2048,2048]{0,1:T(8,128)(2,1)}), bf16[256,2048]{0,1:T(8,128)(2,1)}) %reduce-scatter.12.cloned.1.call-update) | async-done | bytes 1048592 | tf_op jit(solution)/shard_map/reduce_scatter | solution.py:94
  2816.5 152.5 %reduce-scatter.10.cloned.1.call-done = bf16[256,2048]{0,1:T(8,128)(2,1)} async-done(((bf16[2048,2048]{0,1:T(8,128)(2,1)}), bf16[256,2048]{0,1:T(8,128)(2,1)}) %reduce-scatter.10.cloned.1.call-update) | async-done | bytes 1048592 | tf_op jit(solution)/shard_map/reduce_scatter | solution.py:94
  2969.0 153.0 %reduce-scatter.8.cloned.1.call-done = bf16[256,2048]{0,1:T(8,128)(2,1)} async-done(((bf16[2048,2048]{0,1:T(8,128)(2,1)}), bf16[256,2048]{0,1:T(8,128)(2,1)}) %reduce-scatter.8.cloned.1.call-update) | async-done | bytes 1048592 | tf_op jit(solution)/shard_map/reduce_scatter | solution.py:94
  3122.0 545.9 %reduce-scatter.20.cloned.1.call-done = bf16[1024,2048]{1,0:T(8,128)(2,1)} async-done(((bf16[8192,2048]{1,0:T(8,128)(2,1)}), bf16[1024,2048]{1,0:T(8,128)(2,1)}) %reduce-scatter.20.cloned.1.call-update) | async-done | bytes 4194320 | tf_op jit(solution)/shard_map/reduce_scatter | solution.py:94
  3667.9 546.4 %reduce-scatter.18.cloned.1.call-done = bf16[256,8192]{1,0:T(8,128)(2,1)} async-done(((bf16[2048,8192]{1,0:T(8,128)(2,1)}), bf16[256,8192]{1,0:T(8,128)(2,1)}) %reduce-scatter.18.cloned.1.call-update) | async-done | bytes 4194320 | tf_op jit(solution)/shard_map/reduce_scatter | solution.py:94
  4214.3 545.9 %reduce-scatter.16.cloned.1.call-done = bf16[256,8192]{1,0:T(8,128)(2,1)} async-done(((bf16[2048,8192]{1,0:T(8,128)(2,1)}), bf16[256,8192]{1,0:T(8,128)(2,1)}) %reduce-scatter.16.cloned.1.call-update) | async-done | bytes 4194320 | tf_op jit(solution)/shard_map/reduce_scatter | solution.py:94
  4762.1 35.3 all-reduce.8
  4797.7 6.5 all-reduce.9
  4822.7 231.4 %all-reduce.13.cloned.1.call-done = (bf16[256,2048]{0,1:T(8,128)(2,1)}, bf16[256,2048]{0,1:T(8,128)(2,1)}, bf16[256,2048]{0,1:T(8,128)(2,1)}, bf16[256,2048]{1,0...) async-done(((bf16[256,2048]{0,1:T(8,128)(2,1)}, bf16[256,2048]{0,1:T(8,128)(2,1)}, bf16[256,2048]{0,1:T(8,128)(2,1)}, ...) | async-done | bytes 16777232 | tf_op jit(solution)/shard_map/psum | solution.py:231
  5061.7 6.7 convert_element_type.237
  (230 shorter events, 144.6 us)
Async XLA Ops:
  7.2 130.9 %all-gather.12.cloned.1.call-start = ((), (), s32[]{:S(2)}) async-start(), calls=%async_computation.7 | async-start | bytes 9437184 | tf_op jit(solution)/shard_map/all_gather | solution.py:104
  7.9 255.5 %all-gather.16.cloned.1.call-start = ((), (), s32[]{:S(2)}) async-start(), calls=%async_computation.9 | async-start | bytes 9437184 | tf_op jit(solution)/shard_map/all_gather | solution.py:103
  8.7 380.0 %all-gather.14.cloned.1.call-start = ((), (), s32[]{:S(2)}) async-start(), calls=%async_computation.8 | async-start | bytes 9437184 | tf_op jit(solution)/shard_map/all_gather | solution.py:102
  9.4 504.4 %all-gather.18.cloned.1.call-start = ((), (), s32[]{:S(2)}) async-start(), calls=%async_computation.10 | async-start | bytes 9437184 | tf_op jit(solution)/shard_map/all_gather | solution.py:139
  10.0 1141.1 %all-gather.20.cloned.1.call-start = ((), (), s32[]{:S(2)}) async-start(), calls=%async_computation.11 | async-start | bytes 37748736 | tf_op jit(solution)/shard_map/all_gather | solution.py:149
  10.6 1779.7 %all-gather.22.cloned.1.call-start = ((), (), s32[]{:S(2)}) async-start(), calls=%async_computation.12 | async-start | bytes 37748736 | tf_op jit(solution)/shard_map/all_gather | solution.py:150
  11.2 75.0 %copy-start.42 = (s32[256]{0:T(256)S(1)}, s32[256]{0:T(256)}, u32[]{:S(2)}) copy-start(s32[256]{0:T(256)} %param.15) | copy-start | bytes 3076
  11.2 126.9 %copy-start.2 = (bf16[256,2048]{1,0:T(8,128)(2,1)S(1)}, bf16[256,2048]{1,0:T(8,128)(2,1)}, u32[]{:S(2)}) copy-start(bf16[256,2048]{1,0:T(8,128)(2,1)} %param.14) | copy-start | bytes 3145732
  11.2 2418.3 %all-gather.24.cloned.1.call-start = ((), (), s32[]{:S(2)}) async-start(), calls=%async_computation.13 | async-start | bytes 37748736 | tf_op jit(solution)/shard_map/all_gather | solution.py:158
  11.9 2651.5 %reduce-scatter.14.cloned.1.call-start = ((), (), s32[]{:S(2)}) async-start(), calls=%async_computation.17 | async-start | bytes 9437184 | tf_op jit(solution)/shard_map/reduce_scatter | solution.py:94
  69.5 199.7 %copy-start.40 = (f32[8,1,256]{2,1,0:T(1,128)}, f32[8,1,256]{2,1,0:T(1,128)S(1)}, u32[]{:S(2)}) copy-start(f32[8,1,256]{2,1,0:T(1,128)S(1)} %convert_element_type.245) | copy-start | bytes 24580
  86.1 308.4 %copy-start.38 = (f32[8,1,256]{2,1,0:T(1,128)}, f32[8,1,256]{2,1,0:T(1,128)S(1)}, u32[]{:S(2)}) copy-start(f32[8,1,256]{2,1,0:T(1,128)S(1)} %convert_element_type.244) | copy-start | bytes 24580
  86.9 310.7 %copy-start.31 = (f32[2,128,64]{2,1,0:T(8,128)}, f32[2,128,64]{2,1,0:T(8,128)S(1)}, u32[]{:S(2)}) copy-start(f32[2,128,64]{2,1,0:T(8,128)S(1)} %get-tuple-element.94) | copy-start | bytes 196612
  86.9 310.7 %copy-start.33 = (f32[2,128,64]{2,1,0:T(8,128)}, f32[2,128,64]{2,1,0:T(8,128)S(1)}, u32[]{:S(2)}) copy-start(f32[2,128,64]{2,1,0:T(8,128)S(1)} %get-tuple-element.95) | copy-start | bytes 196612
  2429.5 16.6 copy-start.24
  2446.1 3.2 copy-start.16
  2473.2 16.9 copy-start.25
  2514.3 302.2 %reduce-scatter.12.cloned.1.call-start = ((), (), s32[]{:S(2)}) async-start(), calls=%async_computation.16 | async-start | bytes 9437184 | tf_op jit(solution)/shard_map/reduce_scatter | solution.py:94
  2521.3 3.9 copy-start.1
  2537.9 431.1 %reduce-scatter.10.cloned.1.call-start = ((), (), s32[]{:S(2)}) async-start(), calls=%async_computation.15 | async-start | bytes 9437184 | tf_op jit(solution)/shard_map/reduce_scatter | solution.py:94
  2558.2 563.8 %reduce-scatter.8.cloned.1.call-start = ((), (), s32[]{:S(2)}) async-start(), calls=%async_computation.14 | async-start | bytes 9437184 | tf_op jit(solution)/shard_map/reduce_scatter | solution.py:94
  2570.1 1097.9 %reduce-scatter.20.cloned.1.call-start = ((), (), s32[]{:S(2)}) async-start(), calls=%async_computation.20 | async-start | bytes 37748736 | tf_op jit(solution)/shard_map/reduce_scatter | solution.py:94
  2588.4 1625.9 %reduce-scatter.18.cloned.1.call-start = ((), (), s32[]{:S(2)}) async-start(), calls=%async_computation.19 | async-start | bytes 37748736 | tf_op jit(solution)/shard_map/reduce_scatter | solution.py:94
  2605.7 2154.4 %reduce-scatter.16.cloned.1.call-start = ((), (), s32[]{:S(2)}) async-start(), calls=%async_computation.18 | async-start | bytes 37748736 | tf_op jit(solution)/shard_map/reduce_scatter | solution.py:94
  2622.3 2431.7 %all-reduce.13.cloned.1.call-start = ((), (), s32[]{:S(2)}) async-start(), calls=%async_computation.21 | async-start | bytes 33554432 | tf_op jit(solution)/shard_map/psum | solution.py:231
  4806.5 6.2 copy-start.21
  4806.5 12.3 slice-start
  4812.7 6.1 copy-start.18
  4812.7 6.1 copy-start.30
  4812.8 6.2 slice-start.1
  5061.7 6.7 copy-start.23
  5068.4 4.4 copy-start.22
  (42 other events, 58.5 us)
Sparse Core Ops, SparseCore 0:
  10.1 127.9 all-gather.11
  140.3 123.0 all-gather.15
  265.5 123.1 all-gather.13
  390.7 123.1 all-gather.17
  515.2 635.8 all-gather.19
  1152.5 637.6 all-gather.21
  1791.8 637.6 all-gather.23
  2514.5 148.9 reduce-scatter.13
  2668.1 148.3 reduce-scatter.11
  2820.6 148.3 reduce-scatter.9
  2973.6 148.3 reduce-scatter.7
  3125.7 542.2 reduce-scatter.19
  3671.7 542.5 reduce-scatter.17
  4217.9 542.2 reduce-scatter.15
  4763.3 290.7 all-reduce.12
where the time goes:
time: 5090 us; the launch traced here: 5080 us
  waiting for transfers between devices  4630 us (91%)
  matrix products  245 us (5%)
  blocking collectives  116 us (2%)
    reduce_scatter x7, waiting for transfers between devices, owner_grad(): lax.psum_scatter(product_tn(left_rows, right_rows).astype(jnp.bfloat16),...  2140 us
    all_gather x1, waiting for transfers between devices, body(): lax.all_gather(w_gate, 'fsdp', axis=0, tiled=True)  630 us
    all_gather x1, waiting for transfers between devices, body(): lax.all_gather(w_up, 'fsdp', axis=0, tiled=True)  620 us
    all_gather x1, waiting for transfers between devices, body(): lax.all_gather(w_down, 'fsdp', axis=0, tiled=True)  615 us
    psum x1, waiting for transfers between devices, body(): lax.psum(grad_query.astype(jnp.bfloat16), 'dp').astype(jnp.float32)  231 us
    all_gather x1, waiting for transfers between devices, body(): lax.all_gather(w_key, 'fsdp', axis=0, tiled=True)  118 us
    all_gather x1, waiting for transfers between devices, body(): lax.all_gather(w_query, 'fsdp', axis=0, tiled=True)  118 us
    all_gather x1, waiting for transfers between devices, body(): lax.all_gather(w_out, 'fsdp', axis=0, tiled=True)  107 us
  transfers between devices with their start and end apart: 15, of which 15 were waited for; matrix products, arithmetic and copies ran while one was open for 4% of the time, Pallas kernels for 0%

commit v1 on v0

v1 whole, which is shorter than its diff:
```python
import jax
import jax.numpy as jnp
from jax import lax
from jax.experimental import pallas as pl
from jax.experimental.pallas import tpu as pltpu
from jax.sharding import Mesh, PartitionSpec as P

D = 2048
HEADS = 16
HEAD_DIM = 128
MB = 128
EPS = 1e-06
THETA = 500000.0
NEG = -1e30
BF = jnp.bfloat16
F32 = jnp.float32
SWAP = [(0, 1), (1, 0)]
BLOCK = 256
PARTS = ((0, 2), (2, 4), (6, 2))
HALVES = (slice(0, D // 2), slice(D // 2, D))


def product(left_rows, right_rows):
    return jnp.dot(left_rows, right_rows, preferred_element_type=F32)


def product_nt(left_rows, right_rows):
    return lax.dot_general(left_rows, right_rows, (((1,), (1,)), ((), ())), preferred_element_type=F32)


def product_tn(left_rows, right_rows):
    return lax.dot_general(left_rows, right_rows, (((0,), (0,)), ((), ())), preferred_element_type=F32)


def swap(values, axis):
    return lax.ppermute(values, axis, SWAP)


def plane_gather(rows):
    half = rows.shape[0] // 2
    by_a = swap(rows, "a")
    by_y = swap(rows, "y")
    top = swap(by_y[:half], "a")
    bottom = swap(by_a[half:], "y")
    far_a, far_y, far_top, far_bottom = (swap(piece, "c") for piece in (by_a, by_y, top, bottom))
    return jnp.concatenate(
        [top, bottom, far_top, far_bottom, by_a, far_a, by_y, far_y, rows, swap(rows, "c")], axis=0
    )


def plane_gather_small(values):
    values = jnp.concatenate([values, swap(values, "c")], axis=0)
    for axis in ("y", "a"):
        values = jnp.concatenate([swap(values, axis), values], axis=0)
    return values


def resident(shape):
    return pl.BlockSpec(shape, lambda i: (0,) * len(shape), pipeline_mode=pl.Buffered(1))


def row_block(columns, first=0):
    return pl.BlockSpec((BLOCK, columns), lambda i: (first + i, 0))


def stat_block(first=0):
    return pl.BlockSpec((2, BLOCK), lambda i: (0, first + i))


def call(kernel, grid, in_specs, out_specs, out_shape, flops, args, after=(), **more):
    extra = len(after)
    known = len(args)
    moved = sum(v.size * v.dtype.itemsize for v in args)
    moved += sum(v.size * v.dtype.itemsize for v in jax.tree.leaves(out_shape))

    def body(*refs):
        kernel(*refs[:known], *refs[known + extra :])

    return pl.pallas_call(
        body,
        grid=grid,
        in_specs=list(in_specs) + [pl.BlockSpec(memory_space=pl.ANY)] * extra,
        out_specs=out_specs,
        out_shape=out_shape,
        compiler_params=pltpu.CompilerParams(vmem_limit_bytes=44 * 1024 * 1024),
        cost_estimate=pl.CostEstimate(flops=flops, bytes_accessed=moved, transcendentals=0),
        **more,
    )(*args, *after)


def eye():
    shape = (MB, MB)
    return lax.broadcasted_iota(jnp.int32, shape, 0) == lax.broadcasted_iota(jnp.int32, shape, 1)


def as_column(row):
    return jnp.sum(jnp.where(eye(), row, 0.0), axis=1, keepdims=True)


def as_row(column):
    return jnp.sum(jnp.where(eye(), column, 0.0), axis=0, keepdims=True)


def allowed_pairs(segment_row):
    shape = (MB, MB)
    earlier = lax.broadcasted_iota(jnp.int32, shape, 0) >= lax.broadcasted_iota(jnp.int32, shape, 1)
    return jnp.logical_and(as_column(segment_row) == segment_row, earlier)


def qkv_kernel(x_ref, w_ref, qkv_ref, squares_ref):
    width = w_ref.shape[1] // 3
    qkv = product(x_ref[...], w_ref[...])
    qkv_ref[...] = qkv
    for kind in range(2):
        part = qkv[:, kind * width : (kind + 1) * width]
        total = jnp.sum(part * part, axis=1, keepdims=True)
        for m in range(BLOCK // MB):
            squares_ref[kind : kind + 1, m * MB : (m + 1) * MB] = as_row(total[m * MB : (m + 1) * MB])


def attention_kernel(qkv_ref, squares_ref, seg_ref, cos_ref, sin_ref, gain_ref, out_ref, low_ref, att_ref, part_ref):
    width = gain_ref.shape[1]
    scales = lax.rsqrt(squares_ref[...] / D + EPS)
    for m in range(BLOCK // MB):
        rows = slice(m * MB, (m + 1) * MB)
        allowed = allowed_pairs(seg_ref[:, rows])
        cosine, sine = cos_ref[rows, :], sin_ref[rows, :]
        row_scale = [as_column(scales[kind : kind + 1, rows]) for kind in range(2)]
        for h in range(width // HEAD_DIM):
            cols = slice(h * HEAD_DIM, (h + 1) * HEAD_DIM)
            turned = []
            for kind in range(2):
                at = slice(kind * width + h * HEAD_DIM, kind * width + (h + 1) * HEAD_DIM)
                u = qkv_ref[rows, at] * row_scale[kind] * gain_ref[kind : kind + 1, cols]
                u = (u * cosine + pltpu.roll(u, HEAD_DIM // 2, 1) * sine).astype(BF)
                low_ref[rows, at] = u
                turned.append(u)
            at = slice(2 * width + h * HEAD_DIM, 2 * width + (h + 1) * HEAD_DIM)
            value = qkv_ref[rows, at].astype(BF)
            low_ref[rows, at] = value
            scores = jnp.where(allowed, product_nt(turned[0], turned[1]) * HEAD_DIM**-0.5, NEG)
            e = jnp.exp(scores - jnp.max(scores, axis=1, keepdims=True))
            probs = (e / jnp.sum(e, axis=1, keepdims=True)).astype(BF)
            att_ref[rows, cols] = product(probs, value).astype(BF)
    part_ref[...] = product(att_ref[...], out_ref[...]).astype(BF)


def attention_back_kernel(
    low_ref, qkv_ref, squares_ref, seg_ref, cos_ref, sin_ref, gain_ref, out_ref, db_ref,
    n_ref, dv_ref, dots_ref, gain_part_ref,
):
    width = gain_ref.shape[1]
    scales = lax.rsqrt(squares_ref[...] / D + EPS)
    d_att = product_nt(db_ref[...], out_ref[...]).astype(BF)
    terms = [[jnp.zeros((1, HEAD_DIM), F32) for _ in range(width // HEAD_DIM)] for _ in range(2)]
    for m in range(BLOCK // MB):
        rows = slice(m * MB, (m + 1) * MB)
        allowed = allowed_pairs(seg_ref[:, rows])
        cosine, sine = cos_ref[rows, :], sin_ref[rows, :]
        dots = [jnp.zeros((MB, 1), F32), jnp.zeros((MB, 1), F32)]
        for h in range(width // HEAD_DIM):
            cols = slice(h * HEAD_DIM, (h + 1) * HEAD_DIM)
            query, key, value = (
                low_ref[rows, kind * width + h * HEAD_DIM : kind * width + (h + 1) * HEAD_DIM] for kind in range(3)
            )
            scores = jnp.where(allowed, product_nt(query, key) * HEAD_DIM**-0.5, NEG)
            e = jnp.exp(scores - jnp.max(scores, axis=1, keepdims=True))
            probs = e / jnp.sum(e, axis=1, keepdims=True)
            d_out = d_att[rows, cols]
            d_probs = product_nt(d_out, value)
            dv_ref[rows, cols] = product_tn(probs.astype(BF), d_out).astype(BF)
            inner = jnp.sum(probs * d_probs, axis=1, keepdims=True)
            d_scores = (probs * (d_probs - inner)).astype(BF)
            grads = (product(d_scores, key), product_tn(d_scores, query))
            for kind in range(2):
                at = slice(kind * width + h * HEAD_DIM, kind * width + (h + 1) * HEAD_DIM)
                u = grads[kind] * HEAD_DIM**-0.5
                u = u * cosine - pltpu.roll(u, HEAD_DIM // 2, 1) * sine
                raw = qkv_ref[rows, at]
                n = u * gain_ref[kind : kind + 1, cols]
                n_ref[rows, at] = n
                dots[kind] += jnp.sum(n * raw, axis=1, keepdims=True)
                scaled = raw * as_column(scales[kind : kind + 1, rows])
                terms[kind][h] += jnp.sum(u * scaled, axis=0, keepdims=True)
        for kind in range(2):
            dots_ref[kind : kind + 1, rows] = as_row(dots[kind])
    for kind in range(2):
        for h in range(width // HEAD_DIM):
            gain_part_ref[0, kind : kind + 1, h * HEAD_DIM : (h + 1) * HEAD_DIM] = terms[kind][h]


def qkv_back_kernel(n_ref, qkv_ref, squares_ref, dots_ref, dv_ref, out_ref):
    width = dv_ref.shape[1]
    scales = lax.rsqrt(squares_ref[...] / D + EPS)
    factors = scales * scales * scales * dots_ref[...] / D
    for m in range(BLOCK // MB):
        rows = slice(m * MB, (m + 1) * MB)
        for kind in range(2):
            at = slice(kind * width, (kind + 1) * width)
            near = as_column(scales[kind : kind + 1, rows])
            far = as_column(factors[kind : kind + 1, rows])
            out_ref[rows, at] = (near * n_ref[rows, at] - far * qkv_ref[rows, at]).astype(BF)
    out_ref[:, 2 * width :] = dv_ref[...]


def gate_up_kernel(mid_ref, w_ref, gate_up_ref, hidden_ref):
    half = hidden_ref.shape[1]
    both = product(mid_ref[...], w_ref[...])
    gate, up = both[:, :half], both[:, half:]
    gate_up_ref[...] = both.astype(BF)
    hidden_ref[...] = (gate / (1.0 + jnp.exp(-gate)) * up).astype(BF)


def hidden_back_kernel(dm0_ref, dm1_ref, w0_ref, w1_ref, gate_up_ref, out_ref):
    half = w0_ref.shape[0]
    d_hidden = product_nt(dm0_ref[...], w0_ref[...]) + product_nt(dm1_ref[...], w1_ref[...])
    gate = gate_up_ref[:, :half].astype(F32)
    up = gate_up_ref[:, half:].astype(F32)
    sig = 1.0 / (1.0 + jnp.exp(-gate))
    out_ref[:, :half] = (d_hidden * up * sig * (1.0 + gate * (1.0 - sig))).astype(BF)
    out_ref[:, half:] = (d_hidden * gate * sig).astype(BF)


def block_product(left, right, first, count, transposed=False, after=()):
    columns = right.shape[0] if transposed else right.shape[1]

    def kernel(left_ref, right_ref, out_ref):
        out_ref[...] = (product_nt if transposed else product)(left_ref[...], right_ref[...]).astype(BF)

    return call(
        kernel, (count,), [row_block(left.shape[1], first), resident(right.shape)], row_block(columns),
        jax.ShapeDtypeStruct((count * BLOCK, columns), BF), 2 * count * BLOCK * left.shape[1] * columns,
        (left, right), after,
    )


def plane_product(left, right, transposed=False, after=()):
    return tuple(block_product(left, right, first, count, transposed, after) for first, count in PARTS)


def assemble(pieces, out_shape, rows, columns, steps, spots, place, scalars):
    count = len(pieces)
    outs = len(out_shape)

    def in_map(k, o):
        def index(j, s, scalars):
            at = spots(o, jnp.where(j == k, s, jnp.where(j < k, 0, steps - 1)))
            return at

        return index

    def out_map(o):
        return lambda j, s, scalars: place(o, j, s, scalars)

    def kernel(scalar_ref, *refs):
        j = pl.program_id(0)
        for k in range(count):

            @pl.when(j == k)
            def _():
                for o in range(outs):
                    refs[count * outs + o][...] = refs[k * outs + o][...].astype(F32)

    moved = sum(6 * p.size for p in pieces)
    return pl.pallas_call(
        kernel,
        grid_spec=pltpu.PrefetchScalarGridSpec(
            num_scalar_prefetch=1,
            grid=(count, steps),
            in_specs=[pl.BlockSpec((rows, columns), in_map(k, o)) for k in range(count) for o in range(outs)],
            out_specs=[pl.BlockSpec((rows, columns), out_map(o)) for o in range(outs)],
        ),
        out_shape=out_shape,
        compiler_params=pltpu.CompilerParams(vmem_limit_bytes=44 * 1024 * 1024),
        cost_estimate=pl.CostEstimate(flops=0, bytes_accessed=moved, transcendentals=0),
    )(scalars, *[p for p in pieces for _ in range(outs)])


def plane_scatter(parts):
    corner_part, next_part, own_part = parts
    rows = own_part.shape[0] // 2
    half = rows // 2
    corner = (corner_part[:rows].astype(F32) + swap(corner_part[rows:], "c").astype(F32)).astype(BF)
    from_a = swap(corner[:half], "a").astype(F32)
    from_y = swap(corner[half:], "y").astype(F32)
    a_near = next_part[:rows].astype(F32) + swap(next_part[rows : 2 * rows], "c").astype(F32)
    y_near = next_part[2 * rows : 3 * rows].astype(F32) + swap(next_part[3 * rows :], "c").astype(F32)
    to_a = jnp.concatenate([a_near[:half], a_near[half:] + from_y], axis=0).astype(BF)
    to_y = jnp.concatenate([y_near[:half] + from_a, y_near[half:]], axis=0).astype(BF)
    own = own_part[:rows].astype(F32) + swap(own_part[rows:], "c").astype(F32)
    return own + swap(to_a, "a").astype(F32) + swap(to_y, "y").astype(F32)


def plane_sum_tokens(stats):
    kinds, _, count = stats.shape
    values = stats.reshape(kinds, 2, 2, 2, count)
    for axis, dim in (("a", 1), ("y", 2), ("c", 3)):
        values = values + jnp.flip(swap(values, axis), dim)
    return values.reshape(kinds, 8, count)


def sum_everywhere(values, planes):
    for axis in ("a", "c", "y"):
        values = values + swap(values, axis)
    step = 1
    while step < planes:
        values = values + lax.ppermute(values, "z", [(i, i ^ step) for i in range(planes)])
        step *= 2
    return values


def gather_owners(values, planes):
    z = lax.axis_index("z")
    values = ordered_pair(values, swap(values, "y"), lax.axis_index("y"))
    step = 1
    while step < planes:
        other = lax.ppermute(values, "z", [(i, i ^ step) for i in range(planes)])
        pair = ordered_pair(values, other, (z // step) % 2)
        values = pair.reshape((-1,) + pair.shape[2:])
        step *= 2
    return values


def spread(pieces):
    both = list(pieces) + [swap(piece, "a") for piece in pieces]
    return both + [swap(piece, "c") for piece in both]


def ordered_pair(mine, other, index, axis=0):
    return jnp.where(index == 0, jnp.stack([mine, other], axis=axis), jnp.stack([other, mine], axis=axis))


def rotation_tables(segments):
    row_index = jnp.arange(MB, dtype=jnp.int32)
    same_seg = segments[:, :, None] == segments[:, None, :]
    allowed = jnp.logical_and(same_seg, row_index[:, None] >= row_index[None, :])
    position = jnp.sum(allowed.astype(jnp.int32), axis=2) - 1
    half_dim = HEAD_DIM // 2
    frequency = THETA ** (-2.0 * jnp.arange(half_dim, dtype=F32) / HEAD_DIM)
    angles = position.astype(F32).reshape(-1, 1) * frequency
    cosine, sine = jnp.cos(angles), jnp.sin(angles)
    return jnp.concatenate([cosine, cosine], axis=1), jnp.concatenate([-sine, sine], axis=1)


def make_body(planes):
    def body(
        block_input, segment_ids, w_query, w_key, w_value, w_out, gain_query, gain_key, gain_attn,
        w_gate, w_up, w_down, gain_mlp, out_cotangent,
    ):
        a = lax.axis_index("a")
        c = lax.axis_index("c")
        z = lax.axis_index("z")
        y = lax.axis_index("y")
        member = a * 2 + c
        pair = member * 2 + y
        own_rows = block_input.shape[0]
        all_rows = own_rows * 8
        shard_rows = w_query.shape[0]
        width = D // 8
        ff_shard = w_down.shape[0]
        quarter = ff_shard // 4
        ff_here = planes * quarter
        blocks = all_rows // BLOCK

        gains = gather_owners(jnp.stack([gain_query, gain_key, gain_attn, gain_mlp]).astype(F32), planes)
        gains = jnp.transpose(gains, (1, 0, 2)).reshape(4, D)
        gain_q = lax.dynamic_slice(gains[0], (pair * width,), (width,))
        gain_k = lax.dynamic_slice(gains[1], (pair * width,), (width,))
        gain_a, gain_m = gains[2], gains[3]
        segments = plane_gather_small(segment_ids.reshape(own_rows // MB, MB))
        live = (segment_ids >= 0).astype(F32)[:, None]

        def columns_of(which_y):
            at = (member * 2 + which_y) * width
            return jnp.concatenate(
                [lax.dynamic_slice(w, (0, at), (shard_rows, width)) for w in (w_query, w_key, w_value)], axis=1
            )

        def hidden_columns_of(which_y):
            starts = [((plane * 2 + which_y) * 4 + member) * quarter for plane in range(planes)]
            return jnp.concatenate(
                [lax.dynamic_slice(w, (0, at), (shard_rows, quarter)) for w in (w_gate, w_up) for at in starts], axis=1
            )

        def column_weights(mine, given):
            both = ordered_pair(mine, swap(given, "y"), y)
            return lax.all_gather(both.reshape(2 * shard_rows, -1), "z", axis=0, tiled=True)

        if planes == 4:
            out_piece = lax.dynamic_slice(w_out, (member * (shard_rows // 4), 0), (shard_rows // 4, D))
            out_pieces = lax.all_gather(out_piece, "z", axis=0, tiled=True)
            out_rows = lax.all_to_all(out_pieces, ("a", "c"), split_axis=0, concat_axis=0, tiled=True)
        else:
            out_rows = lax.dynamic_slice(
                lax.all_gather(w_out, ("z", "y"), axis=0, tiled=True), (pair * width, 0), (width, D)
            )
        qkv_w = column_weights(columns_of(y), columns_of(1 - y))
        gu_w = column_weights(hidden_columns_of(y), hidden_columns_of(1 - y))
        down_piece = lax.dynamic_slice(w_down, (member * quarter, 0), (quarter, D))
        down_w = [lax.all_gather(down_piece[:, cut], "z", axis=0, tiled=True) for cut in HALVES]

        x_all = plane_gather(block_input)
        shaped = jax.ShapeDtypeStruct
        qkv, squares = call(
            qkv_kernel, (blocks,), [row_block(D), resident((D, 3 * width))], [row_block(3 * width), stat_block()],
            [shaped((all_rows, 3 * width), F32), shaped((2, all_rows), F32)], 2 * all_rows * D * 3 * width,
            (x_all, qkv_w),
        )
        squares = plane_sum_tokens(squares.reshape(2, 8, own_rows)).reshape(2, all_rows)
        cosine, sine = rotation_tables(segments)
        seg_row = segments.astype(F32).reshape(1, all_rows)
        gain_qk = jnp.stack([gain_q, gain_k])

        def attention(first, count):
            return call(
                attention_kernel, (count,),
                [
                    row_block(3 * width, first), stat_block(first), pl.BlockSpec((1, BLOCK), lambda i: (0, first + i)),
                    row_block(HEAD_DIM, first), row_block(HEAD_DIM, first), resident((2, width)), resident((width, D)),
                ],
                [row_block(3 * width), row_block(width), row_block(D)],
                [shaped((count * BLOCK, cols), BF) for cols in (3 * width, width, D)],
                2 * count * BLOCK * width * (D + 2 * MB),
                (qkv, squares, seg_row, cosine, sine, gain_qk, out_rows),
            )

        lows, atts, branch_parts = zip(*[attention(first, count) for first, count in PARTS])
        attended = jnp.concatenate(atts, axis=0)
        low = jnp.concatenate(lows, axis=0)
        branch = plane_scatter(branch_parts)

        def row_scale(values):
            return lax.rsqrt(jnp.mean(values * values, axis=-1, keepdims=True) + EPS)

        def norm_back(values, scale_here, gain, upstream):
            n = upstream * gain
            grad = scale_here * n - scale_here**3 * values * jnp.mean(n * values, axis=-1, keepdims=True)
            return grad, jnp.sum(upstream * values * scale_here, axis=0)

        branch_scale = row_scale(branch)
        middle = block_input.astype(F32) + branch * branch_scale * gain_a
        mid_all = plane_gather(middle.astype(BF))

        gate_up, hidden = call(
            gate_up_kernel, (blocks,), [row_block(D), resident((D, 2 * ff_here))],
            [row_block(2 * ff_here), row_block(ff_here)],
            [shaped((all_rows, 2 * ff_here), BF), shaped((all_rows, ff_here), BF)], 4 * all_rows * D * ff_here,
            (mid_all, gu_w),
        )
        mixed0 = plane_scatter(plane_product(hidden, down_w[0]))
        mixed1 = plane_scatter(plane_product(hidden, down_w[1], after=(mixed0,)))
        mixed = jnp.concatenate([mixed0, mixed1], axis=1)
        mixed_scale = row_scale(mixed)
        block_output = ((middle + mixed * mixed_scale * gain_m) * live).astype(BF)

        grad_rows = out_cotangent.astype(F32) * live
        d_mixed, d_gain_mlp = norm_back(mixed, mixed_scale, gain_m, grad_rows)
        dm_all = [plane_gather(d_mixed[:, cut].astype(BF)) for cut in HALVES]

        def plane_sum(values):
            return lax.psum_scatter(values.astype(BF), "z", scatter_dimension=0, tiled=True)

        grad_down_parts = [product_tn(hidden, cut).astype(BF) for cut in dm_all]
        grad_down = [plane_sum(part) for part in grad_down_parts]
        d_gu = call(
            hidden_back_kernel, (blocks,),
            [row_block(D // 2), row_block(D // 2), resident((ff_here, D // 2)), resident((ff_here, D // 2)),
             row_block(2 * ff_here)],
            row_block(2 * ff_here), shaped((all_rows, 2 * ff_here), BF), 2 * all_rows * D * ff_here,
            (*dm_all, *down_w, gate_up), grad_down_parts,
        )
        grad_gu = plane_sum(product_tn(mid_all, d_gu))
        d_middle = grad_rows + plane_scatter(plane_product(d_gu, gu_w, True))

        d_branch, d_gain_attn = norm_back(branch, branch_scale, gain_a, d_middle)
        db_all = plane_gather(d_branch.astype(BF))
        grad_out = product_tn(attended, db_all).astype(BF)
        n_qk, d_value, dots, gain_part = call(
            attention_back_kernel, (blocks,),
            [
                row_block(3 * width), row_block(2 * width), stat_block(), pl.BlockSpec((1, BLOCK), lambda i: (0, i)),
                row_block(HEAD_DIM), row_block(HEAD_DIM), resident((2, width)), resident((width, D)), row_block(D),
            ],
            [row_block(2 * width), row_block(width), stat_block(), pl.BlockSpec((1, 2, width), lambda i: (i, 0, 0))],
            [
                shaped((all_rows, 2 * width), F32), shaped((all_rows, width), BF), shaped((2, all_rows), F32),
                shaped((blocks, 2, width), F32),
            ],
            2 * all_rows * width * (D + 5 * MB),
            (low, qkv, squares, seg_row, cosine, sine, gain_qk, out_rows, db_all),
        )
        d_gain_query, d_gain_key = jnp.sum(gain_part, axis=0)
        dots = plane_sum_tokens(dots.reshape(2, 8, own_rows)).reshape(2, all_rows)
        d_qkv = call(
            qkv_back_kernel, (blocks,),
            [row_block(2 * width), row_block(2 * width), stat_block(), stat_block(), row_block(width)],
            row_block(3 * width), shaped((all_rows, 3 * width), BF), 0, (n_qk, qkv, squares, dots, d_value),
        )
        grad_qkv_part = product_tn(x_all, d_qkv).astype(BF)
        grad_qkv = plane_sum(grad_qkv_part)
        d_input = d_middle + plane_scatter(plane_product(d_qkv, qkv_w, True, after=(grad_qkv_part,)))

        scalars = jnp.stack([a, c, y]).astype(jnp.int32)

        def member_of(j_a, j_c, scalars):
            return (scalars[0] ^ j_a) * 2 + (scalars[1] ^ j_c)

        down_pieces = [piece for pair_ in zip(*[spread([cut]) for cut in grad_down]) for piece in pair_]
        (grad_down,) = assemble(
            down_pieces, [shaped((ff_shard, D), F32)], quarter, D // 2, 1, lambda o, s: (0, 0),
            lambda o, j, s, scalars: (member_of((j // 2) % 2, j // 4, scalars), j % 2), scalars,
        )

        def column_pieces(summed):
            split = summed.reshape(2, shard_rows, -1)
            mine = lax.dynamic_index_in_dim(split, y, 0, keepdims=False)
            given = lax.dynamic_index_in_dim(split, 1 - y, 0, keepdims=False)
            return spread([mine, swap(given, "y")])

        def column_pair(j, scalars):
            return member_of((j // 2) % 2, j // 4, scalars), scalars[2] ^ (j % 2)

        def gu_place(o, j, s, scalars):
            owner, which_y = column_pair(j, scalars)
            return 0, (s * 2 + which_y) * 4 + owner

        gu_pieces = column_pieces(grad_gu)
        if quarter % 128 == 0:
            grad_gate, grad_up = assemble(
                gu_pieces, [shaped((shard_rows, 8 * ff_here), F32)] * 2, shard_rows, quarter, planes,
                lambda o, s: (0, o * planes + s), gu_place, scalars,
            )
        else:
            filled = jnp.zeros((shard_rows, 2, planes, 2, 4, quarter), F32)
            for j, piece in enumerate(gu_pieces):
                owner, which_y = column_pair(j, scalars)
                piece = piece.astype(F32).reshape(shard_rows, 2, planes, 1, 1, quarter)
                filled = lax.dynamic_update_slice(filled, piece, (0, 0, 0, which_y, owner, 0))
            grad_gate, grad_up = (filled[:, o].reshape(shard_rows, 8 * ff_here) for o in range(2))

        def qkv_place(o, j, s, scalars):
            owner, which_y = column_pair(j, scalars)
            return 0, owner * 2 + which_y

        grad_query, grad_key, grad_value = assemble(
            column_pieces(grad_qkv), [shaped((shard_rows, D), F32)] * 3, shard_rows, width, 1,
            lambda o, s: (0, o), qkv_place, scalars,
        )
        if planes == 4:
            grad_out = lax.all_to_all(grad_out, ("a", "c"), split_axis=0, concat_axis=0, tiled=True)
            (grad_out,) = assemble(
                spread([plane_sum(grad_out)]), [shaped((shard_rows, D), F32)], shard_rows // 4, D, 1,
                lambda o, s: (0, 0), lambda o, j, s, scalars: (member_of(j % 2, j // 2, scalars), 0), scalars,
            )
        else:
            whole = lax.dynamic_update_slice(jnp.zeros((D, D), BF), grad_out, (pair * width, 0))
            whole = lax.psum_scatter(whole, ("z", "y"), scatter_dimension=0, tiled=True)
            grad_out = lax.psum(whole, ("a", "c")).astype(F32)

        zero = jnp.zeros((D,), F32)
        gain_terms = jnp.stack(
            [
                lax.dynamic_update_slice(zero, d_gain_query, (pair * width,)),
                lax.dynamic_update_slice(zero, d_gain_key, (pair * width,)),
                d_gain_attn,
                d_gain_mlp,
            ]
        )
        gain_terms = sum_everywhere(gain_terms, planes)
        own_gains = lax.dynamic_slice(gain_terms, (0, (z * 2 + y) * shard_rows), (4, shard_rows))
        return (
            block_output,
            d_input,
            grad_query,
            grad_key,
            grad_value,
            grad_out,
            own_gains[0],
            own_gains[1],
            own_gains[2],
            grad_gate,
            grad_up,
            grad_down,
            own_gains[3],
        )

    return body


def solution(mesh):
    replicas, shards = mesh.shape["dp"], mesh.shape["fsdp"]
    planes = shards // 2
    fine = Mesh(mesh.devices.reshape(replicas // 2, 2, planes, 2), ("a", "c", "z", "y"))
    tokens = ("a", "c", "z", "y")
    owner = ("z", "y")
    rows, row, wide, vec = P(tokens, None), P(tokens), P(owner, None), P(owner)
    in_specs = (rows, row, wide, wide, wide, wide, vec, vec, vec, wide, wide, wide, vec, rows)
    out_specs = (rows, rows, wide, wide, wide, wide, vec, vec, vec, wide, wide, wide, vec)
    return jax.shard_map(make_body(planes), mesh=fine, in_specs=in_specs, out_specs=out_specs, check_vma=False)
```

time: 5090 us -> 941 us (0.18)
  waiting for transfers between devices: 4630 us -> 397 us
  Pallas kernels: 0 us -> 191 us
  matrix products: 245 us -> 56.3 us
  blocking collectives: 116 us -> 0 us
  starting transfers between devices: 1.39 us -> 101 us
  local copies, waits for them, and re-layouts: 34.7 us -> 127 us
    all_gather x7 -> x5, waiting for transfers between devices: 2260 us -> 29.5 us  [the longest x2 29.5 us: body(): lax.all_gather(down_piece[:, cut], 'z', axis=0, tiled=True)]
    reduce_scatter x7 -> x5, waiting for transfers between devices: 2140 us -> 0.03 us  [plane_sum(): lax.psum_scatter(values.astype(BF), 'z', scatter_dimension=0, tiled=True)]
    ppermute x0 -> x127, waiting for transfers between devices: none -> 348 us  [the longest x123 345 us: swap(): return lax.ppermute(values, axis, SWAP)]
    psum x1 -> x0, waiting for transfers between devices: 231 us -> none  [body(): lax.psum(grad_query.astype(jnp.bfloat16), 'dp').astype(jnp.float32)]
    pallas_call x0 -> x24, Pallas kernels: none -> 191 us  [the longest x20 153 us: call(): pl.pallas_call(body, grid=grid, in_specs=list(in_specs) + [pl.BlockSpec(m...]
    dot_general x20 -> x0, matrix products: 172 us -> none  [the longest x7 83.7 us: product(): return jnp.dot(left_rows, right_rows, preferred_element_type=jnp.float32)]
    ppermute x0 -> x127, starting transfers between devices: none -> 92.7 us  [the longest x123 89.2 us: swap(): return lax.ppermute(values, axis, SWAP)]
    all_gather x4 -> x0, blocking collectives: 74 us -> none  [the longest x1 22.3 us: body(): lax.all_gather(gain_mlp, 'fsdp', axis=0, tiled=True)]
  transfers between devices with their start and end apart: 15 -> 139, of which waited for: 15 -> 53; matrix products, arithmetic and copies ran while one was open for 4% -> 18% of each run, Pallas kernels for 0% -> 18%
where the time goes in v1:
time: 941 us; the launch traced here: 930 us
  waiting for transfers between devices  397 us (42%)
  Pallas kernels  191 us (20%)
  local copies, waits for them, and re-layouts  127 us (13%)
  starting transfers between devices  101 us (11%)
  matrix products  56.3 us (6%)
  other arithmetic  41.5 us (4%)
  between operations  16.4 us (2%)
    ppermute x123, waiting for transfers between devices, swap(): return lax.ppermute(values, axis, SWAP)  345 us
    pallas_call x20, Pallas kernels, call(): pl.pallas_call(body, grid=grid, in_specs=list(in_specs) + [pl.BlockSpec(m...  153 us
    unnamed x233, local copies, waits for them, and re-layouts  94 us
    ppermute x123, starting transfers between devices, swap(): return lax.ppermute(values, axis, SWAP)  89.2 us
    dot_general x5, matrix products, product_tn(): lax.dot_general(left_rows, right_rows, (((0,), (0,)), ((), ())), preferre...  56.3 us
    pallas_call x4, Pallas kernels, assemble(): pl.pallas_call(kernel, grid_spec=pltpu.PrefetchScalarGridSpec(num_scalar_...  38.5 us
    all_gather x2, waiting for transfers between devices, body(): lax.all_gather(down_piece[:, cut], 'z', axis=0, tiled=True)  29.5 us
  transfers between devices with their start and end apart: 139, of which 53 were waited for; matrix products, arithmetic and copies ran while one was open for 18% of the time, Pallas kernels for 18%

profile of v1, /device:TPU:0, one launch (start us, length us, event | category | flops | bytes accessed | tf_op | source)
XLA Modules:
  0.0 930.3 jit_solution(9371116139670720134)
XLA Ops:
  12.6 9.1 collective-permute-done.9
  36.2 22.6 %collective-permute-done.36 = bf16[256,2048]{1,0:T(8,128)(2,1)S(1)} collective-permute-done((bf16[256,2048]{1,0:T(8,128)(2,1)S(1)}, bf16[256,2048]{1,0:T(8,128)(2,1)S(1)}, u32[]{:S(2)}, u32[]{:S(2)}) %collective-permute-start.36) | collective-permute-done | bytes 1048608 | tf_op jit(solution)/shard_map/ppermute | solution.py:36
  66.3 17.8 %collective-permute-done.14 = s32[4,128]{1,0:T(4,128)S(1)} collective-permute-done((s32[4,128]{1,0:T(4,128)S(1)}, s32[4,128]{1,0:T(4,128)S(1)}, u32[]{:S(2)}, u32[]{:S(2)}) %collective-permute-start.14) | collective-permute-done | bytes 2080 | tf_op jit(solution)/shard_map/ppermute | solution.py:36
  114.9 10.4 %shard_map.237 = (f32[2048,768]{1,0:T(8,128)S(1)}, f32[2,2048]{1,0:T(2,128)S(1)}) custom-call(bf16[2048,2048]{1,0:T(8,128)(2,1)} %constant_dynamic-update-slice_fusion.refs_0_, bf16[2048,768]{1,0:T(8,128)(2,1)S(1)} %copy-done.13), custom_call_target="tpu_custom_call" | custom-call | flops 6442450944 | bytes 17842176 | tf_op jit(solution)/shard_map/pallas_call | solution.py:79
  139.1 8.9 all-to-all-done
  154.6 9.3 %shard_map.239 = (bf16[1024,768]{1,0:T(8,128)(2,1)S(1)}, bf16[1024,256]{1,0:T(8,128)(2,1)S(1)}, bf16[1024,2048]{1,0:T(8,128)(2,1)S(1)}) custom-call(f32[2048,768]{1,0:T(8,128)} %copy-done.2, f32[2,2048]{1,0:T(2,128)S(1)} %reshape_reshape.13.refs_1_.refs_2_, f32[1,2048]{1,0:T(1,128)S(1)} %bitcast.65, f32[2048,128]{1,0:T(8,128)S(1)} %get-tuple-element.140.refs_3_.refs_4_, ...), custom_call_target="tpu_custom_call" | custom-call | flops 1207959552 | bytes 15755264 | tf_op jit(solution)/shard_map/pallas_call | solution.py:79
  175.7 11.4 %collective-permute-done.25 = bf16[128,2048]{1,0:T(8,128)(2,1)S(1)} collective-permute-done((bf16[128,2048]{1,0:T(8,128)(2,1)S(1)}, bf16[128,2048]{1,0:T(8,128)(2,1)S(1)}, u32[]{:S(2)}, u32[]{:S(2)}) %collective-permute-start.25) | collective-permute-done | bytes 524320 | tf_op jit(solution)/shard_map/ppermute | solution.py:36
  193.7 19.8 %collective-permute-done.26 = bf16[256,2048]{1,0:T(8,128)(2,1)} collective-permute-done((bf16[256,2048]{1,0:T(8,128)(2,1)}, bf16[256,2048]{1,0:T(8,128)(2,1)}, u32[]{:S(2)}, u32[]{:S(2)}) %collective-permute-start.26) | collective-permute-done | bytes 1048608 | tf_op jit(solution)/shard_map/ppermute | solution.py:36
  221.7 22.2 %collective-permute-done.27 = bf16[256,2048]{1,0:T(8,128)(2,1)S(1)} collective-permute-done((bf16[256,2048]{1,0:T(8,128)(2,1)S(1)}, bf16[256,2048]{1,0:T(8,128)(2,1)S(1)}, u32[]{:S(2)}, u32[]{:S(2)}) %collective-permute-start.27) | collective-permute-done | bytes 1048608 | tf_op jit(solution)/shard_map/ppermute | solution.py:36
  270.6 23.5 %shard_map.241 = (bf16[2048,2048]{1,0:T(8,128)(2,1)}, bf16[2048,1024]{1,0:T(8,128)(2,1)S(1)}) custom-call(bf16[2048,2048]{1,0:T(8,128)(2,1)} %constant_dynamic-update-slice_fusion.10.refs_0_, bf16[2048,2048]{1,0:T(8,128)(2,1)} %all-gather.10.cloned.1.call-done.refs_1_), custom_call_target="tpu_custom_call" | custom-call | flops 17179869184 | bytes 29360128 | tf_op jit(solution)/shard_map/pallas_call | solution.py:79
  296.1 18.1 %all-gather.12.cloned.1.call-done.refs_1_.refs_2_ = bf16[1024,1024]{1,0:T(8,128)(2,1)} async-done(((bf16[256,1024]{1,0:T(8,128)(2,1)}), bf16[1024,1024]{1,0:T(8,128)(2,1)}) %all-gather.12.cloned.1.call-update) | async-done | bytes 2097168 | tf_op jit(solution)/shard_map/all_gather | solution.py:400
  337.1 10.0 %collective-permute-done.44 = bf16[256,1024]{1,0:T(8,128)(2,1)S(1)} collective-permute-done((bf16[256,1024]{1,0:T(8,128)(2,1)S(1)}, bf16[256,1024]{1,0:T(8,128)(2,1)S(1)}, u32[]{:S(2)}, u32[]{:S(2)}) %collective-permute-start.44) | collective-permute-done | bytes 524320 | tf_op jit(solution)/shard_map/ppermute | solution.py:36
  348.8 11.4 %all-gather.14.cloned.1.call-done.refs_1_.refs_3_ = bf16[1024,1024]{1,0:T(8,128)(2,1)} async-done(((bf16[256,1024]{1,0:T(8,128)(2,1)}), bf16[1024,1024]{1,0:T(8,128)(2,1)}) %all-gather.14.cloned.1.call-update) | async-done | bytes 2097168 | tf_op jit(solution)/shard_map/all_gather | solution.py:400
  383.2 10.0 %collective-permute-done.52 = bf16[256,1024]{1,0:T(8,128)(2,1)S(1)} collective-permute-done((bf16[256,1024]{1,0:T(8,128)(2,1)S(1)}, bf16[256,1024]{1,0:T(8,128)(2,1)S(1)}, u32[]{:S(2)}, u32[]{:S(2)}) %collective-permute-start.52) | collective-permute-done | bytes 524320 | tf_op jit(solution)/shard_map/ppermute | solution.py:36
  400.7 10.8 %collective-permute-done.62 = bf16[256,1024]{1,0:T(8,128)(2,1)S(1)} collective-permute-done((bf16[256,1024]{1,0:T(8,128)(2,1)S(1)}, bf16[256,1024]{1,0:T(8,128)(2,1)S(1)}, u32[]{:S(2)}, u32[]{:S(2)}) %collective-permute-start.62) | collective-permute-done | bytes 524320 | tf_op jit(solution)/shard_map/ppermute | solution.py:36
  413.8 8.8 collective-permute-done.53
  450.9 9.7 %convolution_convert_fusion.3.refs_6_ = bf16[1024,1024]{1,0:T(8,128)(2,1)} fusion(bf16[2048,1024]{1,0:T(8,128)(2,1)} %copy-done.3, bf16[2048,1024]{1,0:T(8,128)(2,1)} %constant_dynamic-update-slice_fusion.46.refs_1_), kind=kOutput, calls=%fused_computation.30 | convolution fusion | flops 4296015872 | bytes 10485760 | tf_op jit(solution)/shard_map/dot_general | solution.py:32
  467.1 16.8 %shard_map.248.refs_0_ = bf16[2048,2048]{1,0:T(8,128)(2,1)} custom-call(bf16[2048,1024]{1,0:T(8,128)(2,1)} %copy-done.74, bf16[2048,1024]{1,0:T(8,128)(2,1)} %constant_dynamic-update-slice_fusion.46.refs_1_, bf16[1024,1024]{1,0:T(8,128)(2,1)S(1)} %copy-done.10, bf16[1024,1024]{1,0:T(8,128)(2,1)S(1)} %copy-done.12, ...), custom_call_target="tpu_custom_call" | custom-call | flops 8589934592 | bytes 29360128 | tf_op jit(solution)/shard_map/pallas_call | solution.py:79
  483.9 23.7 %convolution_convert_fusion = bf16[2048,2048]{1,0:T(8,128)(2,1)} fusion(bf16[2048,2048]{1,0:T(8,128)(2,1)} %constant_dynamic-update-slice_fusion.10.refs_0_, bf16[2048,2048]{1,0:T(8,128)(2,1)} %shard_map.248.refs_0_), kind=kOutput, calls=%fused_computation | convolution fusion | flops 17184063488 | bytes 25165824 | tf_op jit(solution)/shard_map/dot_general | solution.py:32
  507.6 8.5 shard_map.251
  516.5 13.3 %shard_map.250 = bf16[1024,2048]{1,0:T(8,128)(2,1)S(1)} custom-call(bf16[2048,2048]{1,0:T(8,128)(2,1)} %shard_map.248.refs_0_, bf16[2048,2048]{1,0:T(8,128)(2,1)} %all-gather.10.cloned.1.call-done.refs_1_), custom_call_target="tpu_custom_call" | custom-call | flops 8589934592 | bytes 20971520 | tf_op jit(solution)/shard_map/pallas_call | solution.py:79
  530.6 8.9 shard_map.249
  543.7 10.9 %collective-permute-done.77 = bf16[128,2048]{1,0:T(8,128)(2,1)S(1)} collective-permute-done((bf16[128,2048]{1,0:T(8,128)(2,1)S(1)}, bf16[128,2048]{1,0:T(8,128)(2,1)S(1)}, u32[]{:S(2)}, u32[]{:S(2)}) %collective-permute-start.77) | collective-permute-done | bytes 524320 | tf_op jit(solution)/shard_map/ppermute | solution.py:36
  557.6 21.8 %collective-permute-done.78 = bf16[256,2048]{1,0:T(8,128)(2,1)S(1)} collective-permute-done((bf16[256,2048]{1,0:T(8,128)(2,1)S(1)}, bf16[256,2048]{1,0:T(8,128)(2,1)S(1)}, u32[]{:S(2)}, u32[]{:S(2)}) %collective-permute-start.78) | collective-permute-done | bytes 1048608 | tf_op jit(solution)/shard_map/ppermute | solution.py:36
  587.1 21.6 %collective-permute-done.79 = bf16[256,2048]{1,0:T(8,128)(2,1)} collective-permute-done((bf16[256,2048]{1,0:T(8,128)(2,1)}, bf16[256,2048]{1,0:T(8,128)(2,1)}, u32[]{:S(2)}, u32[]{:S(2)}) %collective-permute-start.79) | collective-permute-done | bytes 1048608 | tf_op jit(solution)/shard_map/ppermute | solution.py:36
  647.0 25.0 %shard_map.252 = (f32[2048,512]{1,0:T(8,128)}, bf16[2048,256]{1,0:T(8,128)(2,1)S(1)}, f32[2,2048]{1,0:T(2,128)S(1)}, f32[8,2,256]{2,1,0:T(2,128)S(1)}) custom-call(bf16[2048,768]{1,0:T(8,128)(2,1)S(1)} %copy-done.19, f32[2048,768]{1,0:T(8,128)} %copy-done.2, f32[2,2048]{1,0:T(2,128)S(1)} %copy-done.41, f32[1,2048]{1,0:T(1,128)S(1)} %bitcast.67, ...), custom_call_target="tpu_custom_call" | custom-call | flops 2818572288 | bytes 26273792 | tf_op jit(solution)/shard_map/pallas_call | solution.py:79
  686.7 10.4 %all-to-all-done.1 = bf16[4,64,2048]{2,1,0:T(8,128)(2,1)S(1)} async-done(((bf16[4,64,2048]{2,1,0:T(8,128)(2,1)}), bf16[4,64,2048]{2,1,0:T(8,128)(2,1)S(1)}, u32[]{:S(2)}, u32[]{:S(2)}) %all-to-all-start.1) | async-done | bytes 1048608 | tf_op jit(solution)/shard_map/all_to_all | solution.py:550
  706.7 10.4 %convolution_convert_fusion.1.refs_2_ = bf16[2048,768]{1,0:T(8,128)(2,1)} fusion(bf16[2048,2048]{1,0:T(8,128)(2,1)} %constant_dynamic-update-slice_fusion.refs_0_, bf16[2048,768]{1,0:T(8,128)(2,1)S(1)} %shard_map.253.refs_0_), kind=kOutput, calls=%fused_computation.1 | convolution fusion | flops 6444023808 | bytes 14680064 | tf_op jit(solution)/shard_map/dot_general | solution.py:32
  752.0 16.2 %collective-permute-done.97 = bf16[128,2048]{1,0:T(8,128)(2,1)S(1)} collective-permute-done((bf16[128,2048]{1,0:T(8,128)(2,1)S(1)}, bf16[128,2048]{1,0:T(8,128)(2,1)S(1)}, u32[]{:S(2)}, u32[]{:S(2)}) %collective-permute-start.97) | collective-permute-done | bytes 524320 | tf_op jit(solution)/shard_map/ppermute | solution.py:36
  801.0 20.1 %collective-permute-done.98 = bf16[256,2048]{1,0:T(8,128)(2,1)} collective-permute-done((bf16[256,2048]{1,0:T(8,128)(2,1)}, bf16[256,2048]{1,0:T(8,128)(2,1)}, u32[]{:S(2)}, u32[]{:S(2)}) %collective-permute-start.98) | collective-permute-done | bytes 1048608 | tf_op jit(solution)/shard_map/ppermute | solution.py:36
  835.4 34.2 %collective-permute-done.100.refs_6_.refs_7_.refs_8_ = bf16[256,768]{1,0:T(8,128)(2,1)} collective-permute-done((bf16[256,768]{1,0:T(8,128)(2,1)S(1)}, bf16[256,768]{1,0:T(8,128)(2,1)}, u32[]{:S(2)}, u32[]{:S(2)}) %collective-permute-start.100) | collective-permute-done | bytes 393248 | tf_op jit(solution)/shard_map/ppermute | solution.py:36
  900.8 22.5 %shard_map.259 = (f32[256,8192]{1,0:T(8,128)}, f32[256,8192]{1,0:T(8,128)}) custom-call(s32[3]{0:T(128)S(1)} %pad_add_fusion.3.scalar_ref, bf16[256,2048]{1,0:T(8,128)(2,1)S(1)} %get-tuple-element.88.refs_0_.refs_1_, bf16[256,2048]{1,0:T(8,128)(2,1)S(1)} %get-tuple-element.88.refs_0_.refs_1_, bf16[256,2048]{1,0:T(8,128)(2,1)S(1)} %collective-permute-done.114.refs_2_.refs_3_, ...), custom_call_target="tpu_custom_call" | custom-call | bytes 25165824 | tf_op jit(solution)/shard_map/pallas_call | solution.py:265
  (674 shorter events, 415.6 us)
Async XLA Ops:
  7.2 105.8 %all-gather.6.cloned.1.call-start = ((), (), s32[]{:S(2)}) async-start(), calls=%async_computation.7 | async-start | bytes 3932160 | tf_op jit(solution)/shard_map/all_gather | solution.py:387
  22.7 107.3 %all-gather.8.cloned.1.call-start = ((), (), s32[]{:S(2)}) async-start(), calls=%async_computation.8 | async-start | bytes 1310720 | tf_op jit(solution)/shard_map/all_gather | solution.py:391
  23.5 247.1 %all-gather.10.cloned.1.call-start = ((), (), s32[]{:S(2)}) async-start(), calls=%async_computation.9 | async-start | bytes 10485760 | tf_op jit(solution)/shard_map/all_gather | solution.py:387
  60.4 28.0 %collective-permute-start = (bf16[256,2048]{1,0:T(8,128)(2,1)S(1)}, bf16[256,2048]{1,0:T(8,128)(2,1)S(1)}, u32[]{:S(2)}, u32[]{:S(2)}) collective-permute-start(bf16[256,2048]{1,0:T(8,128)(2,1)S(1)} %copy-done.70), channel_id=1, source_target_pairs={{0,1},{1,0},{2,3},{3,2},{4,5},{5,4},{6,7},{7,6},{8,9},{9,8},{10,11... | collective-permute-start | bytes 3145736 | tf_op jit(solution)/shard_map/ppermute | solution.py:36
  61.9 27.8 %collective-permute-start.2 = (bf16[256,2048]{1,0:T(8,128)(2,1)S(1)}, bf16[256,2048]{1,0:T(8,128)(2,1)S(1)}, u32[]{:S(2)}, u32[]{:S(2)}) collective-permute-start(bf16[256,2048]{1,0:T(8,128)(2,1)S(1)} %copy-done.70), channel_id=1, source_target_pairs={{0,16},{16,0},{1,17},{17,1},{2,18},{18,2},{3,19},{19,3},{4,20},{20... | collective-permute-start | bytes 3145736 | tf_op jit(solution)/shard_map/ppermute | solution.py:36
  63.4 47.3 %collective-permute-start.8 = (bf16[256,2048]{1,0:T(8,128)(2,1)S(1)}, bf16[256,2048]{1,0:T(8,128)(2,1)}, u32[]{:S(2)}, u32[]{:S(2)}) collective-permute-start(bf16[256,2048]{1,0:T(8,128)(2,1)S(1)} %copy-done.70), channel_id=1, source_target_pairs={{0,8},{8,0},{1,9},{9,1},{2,10},{10,2},{3,11},{11,3},{4,12},{12,4},... | collective-permute-start | bytes 3145736 | tf_op jit(solution)/shard_map/ppermute | solution.py:36
  99.4 30.6 %collective-permute-start.18 = (f32[4,4,256]{2,1,0:T(4,128)S(1)}, f32[4,4,256]{2,1,0:T(4,128)S(1)}, u32[]{:S(2)}, u32[]{:S(2)}) collective-permute-start(f32[4,4,256]{2,1,0:T(4,128)S(1)} %bitcast.91), channel_id=1, source_target_pairs={{0,4},{2,6},{4,0},{6,2},{1,5},{3,7},{5,1},{7,3},{8,12},{10,14},{12... | collective-permute-start | bytes 49160 | tf_op jit(solution)/shard_map/ppermute | solution.py:317
  133.6 180.7 %all-gather.12.cloned.1.call-start = ((), (), s32[]{:S(2)}) async-start(), calls=%async_computation.10 | async-start | bytes 2621440 | tf_op jit(solution)/shard_map/all_gather | solution.py:400
  188.3 25.2 %collective-permute-start.26 = (bf16[256,2048]{1,0:T(8,128)(2,1)}, bf16[256,2048]{1,0:T(8,128)(2,1)}, u32[]{:S(2)}, u32[]{:S(2)}) collective-permute-start(bf16[256,2048]{1,0:T(8,128)(2,1)} %pad_maximum_fusion.5), channel_id=1, source_target_pairs={{0,1},{1,0},{2,3},{3,2},{4,5},{5,4},{6,7},{7,6},{8,9},{9,8},{10,11... | collective-permute-start | bytes 3145736 | tf_op jit(solution)/shard_map/ppermute | solution.py:36
  191.0 24.9 %collective-permute-start.23 = (bf16[256,2048]{1,0:T(8,128)(2,1)}, bf16[256,2048]{1,0:T(8,128)(2,1)}, u32[]{:S(2)}, u32[]{:S(2)}) collective-permute-start(bf16[256,2048]{1,0:T(8,128)(2,1)} %pad_maximum_fusion.4), channel_id=1, source_target_pairs={{0,16},{16,0},{1,17},{17,1},{2,18},{18,2},{3,19},{19,3},{4,20},{20... | collective-permute-start | bytes 3145736 | tf_op jit(solution)/shard_map/ppermute | solution.py:36
  193.6 166.6 %all-gather.14.cloned.1.call-start = ((), (), s32[]{:S(2)}) async-start(), calls=%async_computation.11 | async-start | bytes 2621440 | tf_op jit(solution)/shard_map/all_gather | solution.py:400
  255.8 374.1 %reduce-scatter.12.cloned.1.call-start = ((), (), s32[]{:S(2)}) async-start(), calls=%async_computation.15 | async-start | bytes 2621440 | tf_op jit(solution)/shard_map/reduce_scatter | solution.py:461
  447.8 294.7 %reduce-scatter.14.cloned.1.call-start = ((), (), s32[]{:S(2)}) async-start(), calls=%async_computation.16 | async-start | bytes 2621440 | tf_op jit(solution)/shard_map/reduce_scatter | solution.py:461
  460.6 309.9 %reduce-scatter.10.cloned.1.call-start = ((), (), s32[]{:S(2)}) async-start(), calls=%async_computation.14 | async-start | bytes 10485760 | tf_op jit(solution)/shard_map/reduce_scatter | solution.py:461
  586.5 25.7 %collective-permute-start.81 = (bf16[256,2048]{1,0:T(8,128)(2,1)}, bf16[256,2048]{1,0:T(8,128)(2,1)}, u32[]{:S(2)}, u32[]{:S(2)}) collective-permute-start(bf16[256,2048]{1,0:T(8,128)(2,1)} %subtract_convert_fusion), channel_id=1, source_target_pairs={{0,16},{16,0},{1,17},{17,1},{2,18},{18,2},{3,19},{19,3},{4,20},{20... | collective-permute-start | bytes 3145736 | tf_op jit(solution)/shard_map/ppermute | solution.py:36
  629.9 122.1 %collective-permute-start.121 = (bf16[256,1024]{1,0:T(8,128)(2,1)}, bf16[256,1024]{1,0:T(8,128)(2,1)}, u32[]{:S(2)}, u32[]{:S(2)}) collective-permute-start(bf16[256,1024]{1,0:T(8,128)(2,1)} %reduce-scatter.12.cloned.1.call-done.refs_0_), channel_id=1, source_target_pairs={{0,16},{16,0},{1,17},{17,1},{2,18},{18,2},{3,19},{19,3},{4,20},{20... | collective-permute-start | bytes 1572872 | tf_op jit(solution)/shard_map/ppermute | solution.py:36
  682.7 106.5 %reduce-scatter.8.cloned.1.call-start = ((), (), s32[]{:S(2)}) async-start(), calls=%async_computation.13 | async-start | bytes 1310720 | tf_op jit(solution)/shard_map/reduce_scatter | solution.py:461
  698.1 123.1 %reduce-scatter.6.cloned.1.call-start = ((), (), s32[]{:S(2)}) async-start(), calls=%async_computation.12 | async-start | bytes 3932160 | tf_op jit(solution)/shard_map/reduce_scatter | solution.py:461
  742.3 34.5 %collective-permute-start.123 = (bf16[256,1024]{1,0:T(8,128)(2,1)S(1)}, bf16[256,1024]{1,0:T(8,128)(2,1)}, u32[]{:S(2)}, u32[]{:S(2)}) collective-permute-start(bf16[256,1024]{1,0:T(8,128)(2,1)S(1)} %copy-done.42), channel_id=1, source_target_pairs={{0,8},{8,0},{1,9},{9,1},{2,10},{10,2},{3,11},{11,3},{4,12},{12,4},... | collective-permute-start | bytes 1572872 | tf_op jit(solution)/shard_map/ppermute | solution.py:36
  742.5 30.8 %collective-permute-start.122 = (bf16[256,1024]{1,0:T(8,128)(2,1)}, bf16[256,1024]{1,0:T(8,128)(2,1)}, u32[]{:S(2)}, u32[]{:S(2)}) collective-permute-start(bf16[256,1024]{1,0:T(8,128)(2,1)} %reduce-scatter.14.cloned.1.call-done.refs_1_), channel_id=1, source_target_pairs={{0,16},{16,0},{1,17},{17,1},{2,18},{18,2},{3,19},{19,3},{4,20},{20... | collective-permute-start | bytes 1572872 | tf_op jit(solution)/shard_map/ppermute | solution.py:36
  752.0 24.8 %collective-permute-start.124 = (bf16[256,1024]{1,0:T(8,128)(2,1)S(1)}, bf16[256,1024]{1,0:T(8,128)(2,1)}, u32[]{:S(2)}, u32[]{:S(2)}) collective-permute-start(bf16[256,1024]{1,0:T(8,128)(2,1)S(1)} %copy-done.44), channel_id=1, source_target_pairs={{0,8},{8,0},{1,9},{9,1},{2,10},{10,2},{3,11},{11,3},{4,12},{12,4},... | collective-permute-start | bytes 1572872 | tf_op jit(solution)/shard_map/ppermute | solution.py:36
  773.3 26.2 %collective-permute-start.114 = (bf16[256,2048]{1,0:T(8,128)(2,1)}, bf16[256,2048]{1,0:T(8,128)(2,1)S(1)}, u32[]{:S(2)}, u32[]{:S(2)}) collective-permute-start(bf16[256,2048]{1,0:T(8,128)(2,1)} %get-tuple-element.87), channel_id=1, source_target_pairs={{0,1},{1,0},{2,3},{3,2},{4,5},{5,4},{6,7},{7,6},{8,9},{9,8},{10,11... | collective-permute-start | bytes 3145736 | tf_op jit(solution)/shard_map/ppermute | solution.py:36
  776.8 44.4 %collective-permute-start.98 = (bf16[256,2048]{1,0:T(8,128)(2,1)}, bf16[256,2048]{1,0:T(8,128)(2,1)}, u32[]{:S(2)}, u32[]{:S(2)}) collective-permute-start(bf16[256,2048]{1,0:T(8,128)(2,1)} %pad_maximum_fusion.9), channel_id=1, source_target_pairs={{0,1},{1,0},{2,3},{3,2},{4,5},{5,4},{6,7},{7,6},{8,9},{9,8},{10,11... | collective-permute-start | bytes 3145736 | tf_op jit(solution)/shard_map/ppermute | solution.py:36
  782.9 39.5 %collective-permute-start.95 = (bf16[256,2048]{1,0:T(8,128)(2,1)}, bf16[256,2048]{1,0:T(8,128)(2,1)}, u32[]{:S(2)}, u32[]{:S(2)}) collective-permute-start(bf16[256,2048]{1,0:T(8,128)(2,1)} %pad_maximum_fusion.8), channel_id=1, source_target_pairs={{0,16},{16,0},{1,17},{17,1},{2,18},{18,2},{3,19},{19,3},{4,20},{20... | collective-permute-start | bytes 3145736 | tf_op jit(solution)/shard_map/ppermute | solution.py:36
  789.2 34.6 %collective-permute-start.106 = (bf16[64,2048]{1,0:T(8,128)(2,1)}, bf16[64,2048]{1,0:T(8,128)(2,1)S(1)}, u32[]{:S(2)}, u32[]{:S(2)}) collective-permute-start(bf16[64,2048]{1,0:T(8,128)(2,1)} %reduce-scatter.8.cloned.1.call-done.refs_0_), channel_id=1, source_target_pairs={{0,16},{16,0},{1,17},{17,1},{2,18},{18,2},{3,19},{19,3},{4,20},{20... | collective-permute-start | bytes 786440 | tf_op jit(solution)/shard_map/ppermute | solution.py:36
  789.2 86.9 %collective-permute-start.115 = (bf16[256,2048]{1,0:T(8,128)(2,1)S(1)}, bf16[256,2048]{1,0:T(8,128)(2,1)}, u32[]{:S(2)}, u32[]{:S(2)}) collective-permute-start(bf16[256,2048]{1,0:T(8,128)(2,1)S(1)} %get-tuple-element.88.refs_0_.refs_1_), channel_id=1, source_target_pairs={{0,16},{16,0},{1,17},{17,1},{2,18},{18,2},{3,19},{19,3},{4,20},{20... | collective-permute-start | bytes 3145736 | tf_op jit(solution)/shard_map/ppermute | solution.py:36
  799.6 76.6 %collective-permute-start.116 = (bf16[256,2048]{1,0:T(8,128)(2,1)S(1)}, bf16[256,2048]{1,0:T(8,128)(2,1)}, u32[]{:S(2)}, u32[]{:S(2)}) collective-permute-start(bf16[256,2048]{1,0:T(8,128)(2,1)S(1)} %collective-permute-done.114.refs_2_.refs_3_), channel_id=1, source_target_pairs={{0,16},{16,0},{1,17},{17,1},{2,18},{18,2},{3,19},{19,3},{4,20},{20... | collective-permute-start | bytes 3145736 | tf_op jit(solution)/shard_map/ppermute | solution.py:36
  823.7 45.9 %collective-permute-start.100 = (bf16[256,768]{1,0:T(8,128)(2,1)S(1)}, bf16[256,768]{1,0:T(8,128)(2,1)}, u32[]{:S(2)}, u32[]{:S(2)}) collective-permute-start(bf16[256,768]{1,0:T(8,128)(2,1)S(1)} %get-tuple-element.114.refs_0_.refs_1_.refs_2_), channel_id=1, source_target_pairs={{0,16},{16,0},{1,17},{17,1},{2,18},{18,2},{3,19},{19,3},{4,20},{20... | collective-permute-start | bytes 1179656 | tf_op jit(solution)/shard_map/ppermute | solution.py:36
  828.2 42.2 %collective-permute-start.102 = (bf16[256,768]{1,0:T(8,128)(2,1)S(1)}, bf16[256,768]{1,0:T(8,128)(2,1)S(1)}, u32[]{:S(2)}, u32[]{:S(2)}) collective-permute-start(bf16[256,768]{1,0:T(8,128)(2,1)S(1)} %get-tuple-element.114.refs_0_.refs_1_.refs_2_), channel_id=1, source_target_pairs={{0,8},{8,0},{1,9},{9,1},{2,10},{10,2},{3,11},{11,3},{4,12},{12,4},... | collective-permute-start | bytes 1179656 | tf_op jit(solution)/shard_map/ppermute | solution.py:36
  833.9 40.9 %collective-permute-start.101 = (bf16[256,768]{1,0:T(8,128)(2,1)S(1)}, bf16[256,768]{1,0:T(8,128)(2,1)S(1)}, u32[]{:S(2)}, u32[]{:S(2)}) collective-permute-start(bf16[256,768]{1,0:T(8,128)(2,1)S(1)} %collective-permute-done.99.refs_3_.refs_4_.refs_5_), channel_id=1, source_target_pairs={{0,16},{16,0},{1,17},{17,1},{2,18},{18,2},{3,19},{19,3},{4,20},{20... | collective-permute-start | bytes 1179656 | tf_op jit(solution)/shard_map/ppermute | solution.py:36
  874.8 25.9 %collective-permute-start.117 = (bf16[256,2048]{1,0:T(8,128)(2,1)S(1)}, bf16[256,2048]{1,0:T(8,128)(2,1)}, u32[]{:S(2)}, u32[]{:S(2)}) collective-permute-start(bf16[256,2048]{1,0:T(8,128)(2,1)S(1)} %get-tuple-element.88.refs_0_.refs_1_), channel_id=1, source_target_pairs={{0,8},{8,0},{1,9},{9,1},{2,10},{10,2},{3,11},{11,3},{4,12},{12,4},... | collective-permute-start | bytes 3145736 | tf_op jit(solution)/shard_map/ppermute | solution.py:36
  875.6 25.1 %collective-permute-start.118 = (bf16[256,2048]{1,0:T(8,128)(2,1)S(1)}, bf16[256,2048]{1,0:T(8,128)(2,1)}, u32[]{:S(2)}, u32[]{:S(2)}) collective-permute-start(bf16[256,2048]{1,0:T(8,128)(2,1)S(1)} %collective-permute-done.114.refs_2_.refs_3_), channel_id=1, source_target_pairs={{0,8},{8,0},{1,9},{9,1},{2,10},{10,2},{3,11},{11,3},{4,12},{12,4},... | collective-permute-start | bytes 3145736 | tf_op jit(solution)/shard_map/ppermute | solution.py:36
  (197 other events, 2295.9 us)
Sparse Core Ops, SparseCore 0:
  22.8 64.9 all-gather.5
  90.0 27.9 all-gather.7
  120.1 148.4 all-gather.9
  270.0 44.1 all-gather.11
  315.7 44.5 all-gather.13
  447.9 41.7 reduce-scatter.11
  492.7 43.1 reduce-scatter.13
  538.8 143.7 reduce-scatter.9
  698.2 24.7 reduce-scatter.7
  725.9 60.2 reduce-scatter.5

commit v2 on v1

v2 whole, which is shorter than its diff:
```python
import jax
import jax.numpy as jnp
from jax import lax
from jax.experimental import pallas as pl
from jax.experimental.pallas import tpu as pltpu
from jax.sharding import Mesh, PartitionSpec as P

D = 2048
HEADS = 16
HEAD_DIM = 128
MB = 128
EPS = 1e-06
THETA = 500000.0
NEG = -1e30
BF = jnp.bfloat16
F32 = jnp.float32
SWAP = [(0, 1), (1, 0)]
BLOCK = 256
PARTS = ((0, 2), (2, 4), (6, 2))
VMEM_LIMIT = 40 * 1024 * 1024


def cost(flops, *arrays):
    moved = sum(v.size * v.dtype.itemsize for v in arrays)
    return pl.CostEstimate(flops=flops, bytes_accessed=moved, transcendentals=0)
HALVES = (slice(0, D // 2), slice(D // 2, D))


def product(left_rows, right_rows):
    return jnp.dot(left_rows, right_rows, preferred_element_type=F32)


def product_nt(left_rows, right_rows):
    return lax.dot_general(left_rows, right_rows, (((1,), (1,)), ((), ())), preferred_element_type=F32)


def product_tn(left_rows, right_rows):
    return lax.dot_general(left_rows, right_rows, (((0,), (0,)), ((), ())), preferred_element_type=F32)


def swap(values, axis):
    return lax.ppermute(values, axis, SWAP)


def plane_gather(rows, early=None, hold=()):
    half = rows.shape[0] // 2
    by_a = swap(rows, "a")
    by_y = swap(rows, "y")
    if early is not None:
        early.extend((by_a, by_y))
    top, bottom = by_y[:half], by_a[half:]
    if hold:
        top, bottom = ordered(top, hold), ordered(bottom, hold)
    top = swap(top, "a")
    bottom = swap(bottom, "y")
    far_a, far_y, far_top, far_bottom = (swap(piece, "c") for piece in (by_a, by_y, top, bottom))
    pieces = [top, bottom, far_top, far_bottom, by_a, far_a, by_y, far_y, rows, swap(rows, "c")]
    return jnp.concatenate(pieces, axis=0)


def plane_gather_small(values):
    values = jnp.concatenate([values, swap(values, "c")], axis=0)
    for axis in ("y", "a"):
        values = jnp.concatenate([swap(values, axis), values], axis=0)
    return values


def assemble_hidden(pieces, columns, places, quarter, planes):
    rows, width = pieces[0].shape
    count = len(pieces)
    parts = 2 * planes

    def kernel(places_ref, *refs):
        ins, outs, held, sems = refs[:count], refs[count : count + 2], refs[count + 2], refs[count + 3]

        def copies(k):
            for n in range(parts):
                at = pl.multiple_of(places_ref[k, n % planes] * quarter, quarter)
                yield pltpu.make_async_copy(
                    held.at[k % 2, :, n * quarter : (n + 1) * quarter],
                    outs[n // planes].at[:, pl.ds(at, quarter)],
                    sems.at[k % 2, n],
                )

        for k in range(count):
            if k >= 2:
                for copy in copies(k - 2):
                    copy.wait()
            held[k % 2] = ins[k][...].astype(F32)
            for copy in copies(k):
                copy.start()
        for k in range(count - 2, count):
            for copy in copies(k):
                copy.wait()

    return pl.pallas_call(
        kernel,
        grid_spec=pltpu.PrefetchScalarGridSpec(
            num_scalar_prefetch=1,
            grid=(1,),
            in_specs=[pl.BlockSpec((rows, width), lambda i, s: (0, 0), pipeline_mode=pl.Buffered(1))] * count,
            out_specs=[pl.BlockSpec(memory_space=pl.ANY)] * 2,
            scratch_shapes=[pltpu.VMEM((2, rows, width), F32), pltpu.SemaphoreType.DMA((2, parts))],
        ),
        out_shape=[jax.ShapeDtypeStruct((rows, columns), F32)] * 2,
        compiler_params=pltpu.CompilerParams(vmem_limit_bytes=VMEM_LIMIT),
        cost_estimate=cost(0, *pieces, *pieces, *pieces),
    )(places, *pieces)


def resident(shape):
    return pl.BlockSpec(shape, lambda i: (0,) * len(shape), pipeline_mode=pl.Buffered(1))


def resident_view(view):
    array, rows, columns = view
    return resident((array.shape[0], rows, columns))


def flat(ref):
    value = ref[...]
    return value.reshape(-1, value.shape[-1]) if value.ndim == 3 else value


def row_block(columns, first=0):
    return pl.BlockSpec((BLOCK, columns), lambda i: (first + i, 0))


def stat_block(first=0):
    return pl.BlockSpec((2, BLOCK), lambda i: (0, first + i))


def call(kernel, grid, in_specs, out_specs, out_shape, flops, args, after=(), through=()):
    outs = isinstance(out_shape, (list, tuple))
    out_shape = list(out_shape) if outs else [out_shape]
    out_specs = list(out_specs) if outs else [out_specs]
    extra = len(after) + len(through)
    known = len(args)
    results = len(out_shape)

    def body(*refs):
        kernel(*refs[:known], *refs[known + extra : known + extra + results])

    anywhere = pl.BlockSpec(memory_space=pl.ANY)
    given = pl.pallas_call(
        body,
        grid=grid,
        in_specs=list(in_specs) + [anywhere] * extra,
        out_specs=out_specs + [anywhere] * len(through),
        out_shape=out_shape + [jax.ShapeDtypeStruct(v.shape, v.dtype) for v in through],
        input_output_aliases={known + len(after) + k: results + k for k in range(len(through))},
        compiler_params=pltpu.CompilerParams(vmem_limit_bytes=VMEM_LIMIT),
        cost_estimate=cost(flops, *args, *out_shape),
    )(*args, *after, *through)
    own = given[:results] if outs else given[0]
    return (own, *given[results:]) if through else own


def eye():
    shape = (MB, MB)
    return lax.broadcasted_iota(jnp.int32, shape, 0) == lax.broadcasted_iota(jnp.int32, shape, 1)


def as_column(row):
    return jnp.sum(jnp.where(eye(), row, 0.0), axis=1, keepdims=True)


def as_row(column):
    return jnp.sum(jnp.where(eye(), column, 0.0), axis=0, keepdims=True)


def allowed_pairs(segment_row):
    shape = (MB, MB)
    earlier = lax.broadcasted_iota(jnp.int32, shape, 0) >= lax.broadcasted_iota(jnp.int32, shape, 1)
    return jnp.logical_and(as_column(segment_row) == segment_row, earlier)


def qkv_kernel(x_ref, w_ref, qkv_ref, squares_ref):
    width = w_ref.shape[2] // 3
    qkv = product(x_ref[...], flat(w_ref))
    qkv_ref[...] = qkv
    for kind in range(2):
        part = qkv[:, kind * width : (kind + 1) * width]
        total = jnp.sum(part * part, axis=1, keepdims=True)
        for m in range(BLOCK // MB):
            squares_ref[kind : kind + 1, m * MB : (m + 1) * MB] = as_row(total[m * MB : (m + 1) * MB])


def head_slots(width):
    for m in range(BLOCK // MB):
        for h in range(width // HEAD_DIM):
            starts = [kind * width + h * HEAD_DIM for kind in range(3)]
            yield m, h, slice(m * MB, (m + 1) * MB), [slice(at, at + HEAD_DIM) for at in starts]


def masked_softmax(queries, keys, allowed):
    scores = [product_nt(query, key) * HEAD_DIM**-0.5 for query, key in zip(queries, keys)]
    scores = [jnp.where(mask, score, NEG) for mask, score in zip(allowed, scores)]
    tops = [jnp.max(score, axis=1, keepdims=True) for score in scores]
    powers = [jnp.exp(score - top) for score, top in zip(scores, tops)]
    sums = [jnp.sum(power, axis=1, keepdims=True) for power in powers]
    return [power / total for power, total in zip(powers, sums)]


def attention_kernel(qkv_ref, squares_ref, seg_ref, cos_ref, sin_ref, gain_ref, out_ref, low_ref, att_ref, part_ref):
    width = gain_ref.shape[1]
    scales = lax.rsqrt(squares_ref[...] / D + EPS)
    slots = list(head_slots(width))
    masks, columns = [], []
    for m in range(BLOCK // MB):
        rows = slice(m * MB, (m + 1) * MB)
        masks.append(allowed_pairs(seg_ref[:, rows]))
        columns.append([as_column(scales[kind : kind + 1, rows]) for kind in range(2)])
    lows = [[], [], []]
    for kind in range(2):
        for m, h, rows, ats in slots:
            gain = gain_ref[kind : kind + 1, h * HEAD_DIM : (h + 1) * HEAD_DIM]
            u = qkv_ref[rows, ats[kind]] * columns[m][kind] * gain
            lows[kind].append((u * cos_ref[rows, :] + pltpu.roll(u, HEAD_DIM // 2, 1) * sin_ref[rows, :]).astype(BF))
    lows[2] = [qkv_ref[rows, ats[2]].astype(BF) for m, h, rows, ats in slots]
    probs = masked_softmax(lows[0], lows[1], [masks[m] for m, *_ in slots])
    outs = [product(prob.astype(BF), value).astype(BF) for prob, value in zip(probs, lows[2])]
    for n, (m, h, rows, ats) in enumerate(slots):
        for kind in range(3):
            low_ref[rows, ats[kind]] = lows[kind][n]
        att_ref[rows, h * HEAD_DIM : (h + 1) * HEAD_DIM] = outs[n]
    part_ref[...] = product(att_ref[...], out_ref[...]).astype(BF)


def attention_back_kernel(
    low_ref, qkv_ref, squares_ref, seg_ref, cos_ref, sin_ref, gain_ref, out_ref, db_ref,
    n_ref, dv_ref, dots_ref, gain_part_ref,
):
    width = gain_ref.shape[1]
    scales = lax.rsqrt(squares_ref[...] / D + EPS)
    slots = list(head_slots(width))
    masks, columns = [], []
    for m in range(BLOCK // MB):
        rows = slice(m * MB, (m + 1) * MB)
        masks.append(allowed_pairs(seg_ref[:, rows]))
        columns.append([as_column(scales[kind : kind + 1, rows]) for kind in range(2)])
    queries, keys, values = ([low_ref[rows, ats[kind]] for m, h, rows, ats in slots] for kind in range(3))
    d_att = product_nt(db_ref[...], out_ref[...]).astype(BF)
    d_outs = [d_att[rows, h * HEAD_DIM : (h + 1) * HEAD_DIM] for m, h, rows, ats in slots]
    d_probs = [product_nt(d_out, value) for d_out, value in zip(d_outs, values)]
    probs = masked_softmax(queries, keys, [masks[m] for m, *_ in slots])
    d_values = [product_tn(prob.astype(BF), d_out).astype(BF) for prob, d_out in zip(probs, d_outs)]
    inner = [jnp.sum(prob * d_prob, axis=1, keepdims=True) for prob, d_prob in zip(probs, d_probs)]
    d_scores = [(prob * (d_prob - dot)).astype(BF) for prob, d_prob, dot in zip(probs, d_probs, inner)]
    grads = [
        [product(score, key) for score, key in zip(d_scores, keys)],
        [product_tn(score, query) for score, query in zip(d_scores, queries)],
    ]
    dots = [[jnp.zeros((MB, 1), F32) for _ in range(2)] for _ in range(BLOCK // MB)]
    terms = [[jnp.zeros((1, HEAD_DIM), F32) for _ in range(width // HEAD_DIM)] for _ in range(2)]
    for kind in range(2):
        for n, (m, h, rows, ats) in enumerate(slots):
            u = grads[kind][n] * HEAD_DIM**-0.5
            u = u * cos_ref[rows, :] - pltpu.roll(u, HEAD_DIM // 2, 1) * sin_ref[rows, :]
            raw = qkv_ref[rows, ats[kind]]
            grad = u * gain_ref[kind : kind + 1, h * HEAD_DIM : (h + 1) * HEAD_DIM]
            n_ref[rows, ats[kind]] = grad
            dots[m][kind] += jnp.sum(grad * raw, axis=1, keepdims=True)
            terms[kind][h] += jnp.sum(u * (raw * columns[m][kind]), axis=0, keepdims=True)
    for n, (m, h, rows, ats) in enumerate(slots):
        dv_ref[rows, h * HEAD_DIM : (h + 1) * HEAD_DIM] = d_values[n]
    for kind in range(2):
        for m in range(BLOCK // MB):
            dots_ref[kind : kind + 1, m * MB : (m + 1) * MB] = as_row(dots[m][kind])
        for h in range(width // HEAD_DIM):
            gain_part_ref[0, kind : kind + 1, h * HEAD_DIM : (h + 1) * HEAD_DIM] = terms[kind][h]


def qkv_back_kernel(n_ref, qkv_ref, squares_ref, dots_ref, dv_ref, out_ref):
    width = dv_ref.shape[1]
    scales = lax.rsqrt(squares_ref[...] / D + EPS)
    factors = scales * scales * scales * dots_ref[...] / D
    for m in range(BLOCK // MB):
        rows = slice(m * MB, (m + 1) * MB)
        for kind in range(2):
            at = slice(kind * width, (kind + 1) * width)
            near = as_column(scales[kind : kind + 1, rows])
            far = as_column(factors[kind : kind + 1, rows])
            out_ref[rows, at] = (near * n_ref[rows, at] - far * qkv_ref[rows, at]).astype(BF)
    out_ref[:, 2 * width :] = dv_ref[...]


def gate_up_kernel(mid_ref, w_ref, gate_up_ref, hidden_ref):
    half = hidden_ref.shape[1]
    both = product(mid_ref[...], flat(w_ref))
    gate, up = both[:, :half], both[:, half:]
    gate_up_ref[...] = both.astype(BF)
    hidden_ref[...] = (gate / (1.0 + jnp.exp(-gate)) * up).astype(BF)


def hidden_back_kernel(dm0_ref, dm1_ref, w0_ref, w1_ref, gate_up_ref, out_ref):
    half = w1_ref.shape[0]
    d_hidden = product_nt(dm0_ref[...], flat(w0_ref)) + product_nt(dm1_ref[...], w1_ref[...])
    gate = gate_up_ref[:, :half].astype(F32)
    up = gate_up_ref[:, half:].astype(F32)
    sig = 1.0 / (1.0 + jnp.exp(-gate))
    out_ref[:, :half] = (d_hidden * up * sig * (1.0 + gate * (1.0 - sig))).astype(BF)
    out_ref[:, half:] = (d_hidden * gate * sig).astype(BF)


def block_product(left, right, first, count, transposed=False, after=()):
    view = isinstance(right, tuple)
    shape = (right[0].shape[0] * right[1], right[2]) if view else right.shape
    columns = shape[0] if transposed else shape[1]

    def kernel(left_ref, right_ref, out_ref):
        out_ref[...] = (product_nt if transposed else product)(left_ref[...], flat(right_ref)).astype(BF)

    return call(
        kernel, (count,),
        [row_block(left.shape[1], first), resident_view(right) if view else resident(right.shape)], row_block(columns),
        jax.ShapeDtypeStruct((count * BLOCK, columns), BF), 2 * count * BLOCK * left.shape[1] * columns,
        (left, right[0] if view else right), after,
    )


def weight_grad(left, right, after=(), parts=1, spare=0):
    rows, columns = left.shape[1] // parts, right.shape[1]
    size = min(BLOCK, rows)
    steps = rows // size

    def kernel(left_ref, right_ref, out_ref):
        out_ref[0] = product_tn(left_ref[...], right_ref[...]).astype(BF)

    return call(
        kernel, (parts * steps,),
        [pl.BlockSpec((left.shape[0], size), lambda i: (0, i)), resident(right.shape)],
        pl.BlockSpec((1, size, columns), lambda i: (i // steps, i % steps, 0)),
        jax.ShapeDtypeStruct((parts, rows + spare, columns), BF), 2 * left.shape[0] * left.shape[1] * columns,
        (left, right), after,
    )


def ordered(values, after):
    def kernel(in_ref, out_ref):
        out_ref[...] = in_ref[...]

    whole = pl.BlockSpec(values.shape, lambda i: (0,) * values.ndim)
    return call(kernel, (1,), [whole], whole, jax.ShapeDtypeStruct(values.shape, values.dtype), 0, (values,), after)


def beside(left, right, after):
    columns = left.shape[1]

    def kernel(left_ref, right_ref, out_ref):
        out_ref[:, :columns] = left_ref[...]
        out_ref[:, columns:] = right_ref[...]

    whole = [pl.BlockSpec(shape, lambda i: (0, 0)) for shape in (left.shape, right.shape)]
    shape = (left.shape[0], columns + right.shape[1])
    return call(
        kernel, (1,), whole, pl.BlockSpec(shape, lambda i: (0, 0)), jax.ShapeDtypeStruct(shape, left.dtype), 0,
        (left, right), after,
    )


def split_rows(values, which, rows, after=()):
    columns = values.shape[1]
    extra = len(after)

    def kernel(which_ref, mine_ref, given_ref, *refs):
        refs[extra][...] = mine_ref[...]
        refs[extra + 1][...] = given_ref[...]

    width = columns // 2
    return pl.pallas_call(
        kernel,
        grid_spec=pltpu.PrefetchScalarGridSpec(
            num_scalar_prefetch=1,
            grid=(2,),
            in_specs=[
                pl.BlockSpec((rows, width), lambda i, w: (w[0], i)),
                pl.BlockSpec((rows, width), lambda i, w: (1 - w[0], i)),
            ]
            + [pl.BlockSpec(memory_space=pl.ANY)] * extra,
            out_specs=[pl.BlockSpec((rows, width), lambda i, w: (0, i))] * 2,
        ),
        out_shape=[jax.ShapeDtypeStruct((rows, columns), values.dtype)] * 2,
        cost_estimate=cost(0, values, values),
    )(jnp.reshape(which, (1,)).astype(jnp.int32), values, values, *after)


def assemble(pieces, out_shape, rows, columns, steps, spots, place, scalars):
    count = len(pieces)
    outs = len(out_shape)

    def in_map(k, o):
        def index(j, s, scalars):
            at = spots(o, jnp.where(j == k, s, jnp.where(j < k, 0, steps - 1)))
            return at

        return index

    def out_map(o):
        return lambda j, s, scalars: place(o, j, s, scalars)

    def kernel(scalar_ref, *refs):
        j = pl.program_id(0)
        for k in range(count):

            @pl.when(j == k)
            def _():
                for o in range(outs):
                    refs[count * outs + o][...] = refs[k * outs + o][...].astype(F32)

    return pl.pallas_call(
        kernel,
        grid_spec=pltpu.PrefetchScalarGridSpec(
            num_scalar_prefetch=1,
            grid=(count, steps),
            in_specs=[pl.BlockSpec((rows, columns), in_map(k, o)) for k in range(count) for o in range(outs)],
            out_specs=[pl.BlockSpec((rows, columns), out_map(o)) for o in range(outs)],
        ),
        out_shape=out_shape,
        compiler_params=pltpu.CompilerParams(vmem_limit_bytes=VMEM_LIMIT),
        cost_estimate=cost(0, *pieces, *out_shape),
    )(scalars, *[p for p in pieces for _ in range(outs)])


def plane_scatter(make, between=None, lean=False):
    corner_part = make(*PARTS[0], ())
    rows = corner_part.shape[0] // 2
    half = rows // 2
    next_part = make(*PARTS[1], (corner_part,))
    corner = (corner_part[:rows].astype(F32) + swap(corner_part[rows:], "c").astype(F32)).astype(BF)
    if between is not None:
        between((corner, next_part))
    if lean:
        from_a, from_y = None, swap(corner, "y").astype(F32)
    else:
        from_a, from_y = swap(corner[:half], "a").astype(F32), swap(corner[half:], "y").astype(F32)
    a_near = next_part[:rows].astype(F32) + swap(next_part[rows : 2 * rows], "c").astype(F32)
    y_near = next_part[2 * rows : 3 * rows].astype(F32) + swap(next_part[3 * rows :], "c").astype(F32)
    if lean:
        to_a, to_y = (a_near + from_y).astype(BF), y_near.astype(BF)
    else:
        to_a = jnp.concatenate([a_near[:half], a_near[half:] + from_y], axis=0).astype(BF)
        to_y = jnp.concatenate([y_near[:half] + from_a, y_near[half:]], axis=0).astype(BF)
    own_part = make(*PARTS[2], (corner, next_part))
    own = own_part[:rows].astype(F32) + swap(own_part[rows:], "c").astype(F32)
    return own + swap(to_a, "a").astype(F32) + swap(to_y, "y").astype(F32), (to_a, to_y)


def plane_sum_tokens(stats):
    kinds, _, count = stats.shape
    values = stats.reshape(kinds, 2, 2, 2, count)
    for axis, dim in (("a", 1), ("y", 2), ("c", 3)):
        values = values + jnp.flip(swap(values, axis), dim)
    return values.reshape(kinds, 8, count)


def exchange_members(blocks, a, c):
    return exchange_last(*exchange_first(blocks, a), a, c)


def exchange_first(blocks, a):
    both = blocks.reshape((2, 2) + blocks.shape[1:])
    mine = lax.dynamic_index_in_dim(both, a, 0, keepdims=False)
    return mine, swap(lax.dynamic_index_in_dim(both, 1 - a, 0, keepdims=False), "a")


def exchange_last(mine, other, a, c):
    blocks = jax.ShapeDtypeStruct((4,) + mine.shape[1:], mine.dtype)
    both = ordered_pair(mine, other, a)
    mine = lax.dynamic_index_in_dim(both, c, 1, keepdims=False)
    other = swap(lax.dynamic_index_in_dim(both, 1 - c, 1, keepdims=False), "c")
    return ordered_pair(mine, other, c, 1).reshape(blocks.shape)


def spread(pieces):
    both = list(pieces) + [swap(piece, "a") for piece in pieces]
    return both + [swap(piece, "c") for piece in both]


def ordered_pair(mine, other, index, axis=0):
    return jnp.where(index == 0, jnp.stack([mine, other], axis=axis), jnp.stack([other, mine], axis=axis))


def rotation_tables(segments):
    row_index = jnp.arange(MB, dtype=jnp.int32)
    same_seg = segments[:, :, None] == segments[:, None, :]
    allowed = jnp.logical_and(same_seg, row_index[:, None] >= row_index[None, :])
    position = jnp.sum(allowed.astype(jnp.int32), axis=2) - 1
    half_dim = HEAD_DIM // 2
    frequency = THETA ** (-2.0 * jnp.arange(half_dim, dtype=F32) / HEAD_DIM)
    angles = position.astype(F32).reshape(-1, 1) * frequency
    cosine, sine = jnp.cos(angles), jnp.sin(angles)
    return jnp.concatenate([cosine, cosine], axis=1), jnp.concatenate([-sine, sine], axis=1)


def make_body(planes):
    def body(
        block_input, segment_ids, w_query, w_key, w_value, w_out, gain_query, gain_key, gain_attn,
        w_gate, w_up, w_down, gain_mlp, out_cotangent,
    ):
        a = lax.axis_index("a")
        c = lax.axis_index("c")
        z = lax.axis_index("z")
        y = lax.axis_index("y")
        member = a * 2 + c
        pair = member * 2 + y
        own_rows = block_input.shape[0]
        all_rows = own_rows * 8
        shard_rows = w_query.shape[0]
        width = D // 8
        ff_shard = w_down.shape[0]
        quarter = ff_shard // 4
        ff_here = planes * quarter
        blocks = all_rows // BLOCK

        segments = plane_gather_small(segment_ids.reshape(own_rows // MB, MB))
        live = (segment_ids >= 0).astype(F32)[:, None]

        def columns_of(which_y):
            at = (member * 2 + which_y) * width
            return jnp.concatenate(
                [lax.dynamic_slice(w, (0, at), (shard_rows, width)) for w in (w_query, w_key, w_value)], axis=1
            )

        def hidden_columns_of(which_y):
            starts = [((plane * 2 + which_y) * 4 + member) * quarter for plane in range(planes)]
            return jnp.concatenate(
                [lax.dynamic_slice(w, (0, at), (shard_rows, quarter)) for w in (w_gate, w_up) for at in starts], axis=1
            )

        def column_weights(mine, given, more, next_to=()):
            both = ordered_pair(mine, swap(given, "y"), y).reshape(2 * shard_rows, -1)
            return jnp.concatenate([jnp.concatenate([both] + list(next_to), axis=1), more], axis=0)

        def gather_planes(piece):
            return lax.all_gather(piece, "z", axis=0, tiled=False)

        own_gains = jnp.stack([gain_query, gain_key, gain_attn, gain_mlp]).reshape(2, 2 * shard_rows)
        more, next_to = own_gains, []
        if planes == 4:
            out_piece = lax.dynamic_slice(w_out, (member * (shard_rows // 4), 0), (shard_rows // 4, D))
            next_to = [out_piece.reshape(2 * shard_rows, -1)]
        more = jnp.pad(own_gains, ((0, 14), (0, (3 + len(next_to)) * width - 2 * shard_rows)))
        qkv_array = gather_planes(column_weights(columns_of(y), columns_of(1 - y), more, next_to))
        x_near = []
        x_all = plane_gather(block_input, x_near)
        down_pieces = [lax.dynamic_slice(w_down, (member * quarter, n * D // 2), (quarter, D // 2)) for n in range(2)]
        gu_given = ordered(hidden_columns_of(1 - y), x_near)
        gu_array = gather_planes(
            column_weights(
                hidden_columns_of(y), gu_given,
                jnp.concatenate([down_pieces[0][: quarter // 2], down_pieces[0][quarter // 2 :]], axis=1),
            )
        )
        last_down = gather_planes(down_pieces[1]).reshape(ff_here, D // 2)
        qkv_w = (qkv_array, 2 * shard_rows, 3 * width)
        gains = qkv_array[:, 2 * shard_rows : 2 * shard_rows + 2, : 2 * shard_rows].reshape(planes, 4, shard_rows)
        gains = ordered_pair(gains, swap(gains, "y"), y, 1)
        gains = jnp.transpose(gains, (2, 0, 1, 3)).reshape(4, D).astype(F32)
        gain_q = lax.dynamic_slice(gains[0], (pair * width,), (width,))
        gain_k = lax.dynamic_slice(gains[1], (pair * width,), (width,))
        gain_a, gain_m = gains[2], gains[3]
        if planes == 4:
            out_pieces = qkv_array[:, : 2 * shard_rows, 3 * width :].reshape(planes, shard_rows // 4, D)
            out_rows = exchange_members(out_pieces, a, c).reshape(width, D)
        else:
            out_rows = lax.dynamic_slice(
                lax.all_gather(w_out, ("z", "y"), axis=0, tiled=True), (pair * width, 0), (width, D)
            )
        gu_w = (gu_array, 2 * shard_rows, 2 * ff_here)

        shaped = jax.ShapeDtypeStruct
        cosine, sine = rotation_tables(segments)
        qkv, squares = call(
            qkv_kernel, (blocks,), [row_block(D), resident_view(qkv_w)], [row_block(3 * width), stat_block()],
            [shaped((all_rows, 3 * width), F32), shaped((2, all_rows), F32)], 2 * all_rows * D * 3 * width,
            (x_all, qkv_array), (cosine, sine),
        )
        squares = plane_sum_tokens(squares.reshape(2, 8, own_rows)).reshape(2, all_rows)
        seg_row = segments.astype(F32).reshape(1, all_rows)
        gain_qk = jnp.stack([gain_q, gain_k])

        def attention(first, count, after):
            return call(
                attention_kernel, (count,),
                [
                    row_block(3 * width, first), stat_block(first), pl.BlockSpec((1, BLOCK), lambda i: (0, first + i)),
                    row_block(HEAD_DIM, first), row_block(HEAD_DIM, first), resident((2, width)), resident((width, D)),
                ],
                [row_block(3 * width), row_block(width), row_block(D)],
                [shaped((count * BLOCK, cols), BF) for cols in (3 * width, width, D)],
                2 * count * BLOCK * width * (D + 2 * MB),
                (qkv, squares, seg_row, cosine, sine, gain_qk, out_rows), after,
            )

        lows, atts = [], []

        def branch_part(first, count, after):
            low_part, att_part, part = attention(first, count, after)
            lows.append(low_part)
            atts.append(att_part)
            return part

        branch, _ = plane_scatter(branch_part)
        attended = jnp.concatenate(atts, axis=0)
        low = jnp.concatenate(lows, axis=0)

        def row_scale(values):
            return lax.rsqrt(jnp.mean(values * values, axis=-1, keepdims=True) + EPS)

        def norm_back(values, scale_here, gain, upstream):
            n = upstream * gain
            grad = scale_here * n - scale_here**3 * values * jnp.mean(n * values, axis=-1, keepdims=True)
            return grad, jnp.sum(upstream * values * scale_here, axis=0)

        branch_scale = row_scale(branch)
        middle = block_input.astype(F32) + branch * branch_scale * gain_a
        mid_all = plane_gather(middle.astype(BF))

        gate_up, hidden = call(
            gate_up_kernel, (blocks,), [row_block(D), resident_view(gu_w)],
            [row_block(2 * ff_here), row_block(ff_here)],
            [shaped((all_rows, 2 * ff_here), BF), shaped((all_rows, ff_here), BF)], 4 * all_rows * D * ff_here,
            (mid_all, gu_array),
        )
        size, first = quarter // 2, 2 * shard_rows // (quarter // 2)

        def take_kernel(in_ref, out_ref):
            out_ref[...] = in_ref[...]

        first_down = call(
            take_kernel, (2 * planes,), [pl.BlockSpec((1, size, D // 2), lambda i: (i // 2, first, i % 2))],
            pl.BlockSpec((1, size, D // 2), lambda i: (i // 2, i % 2, 0)),
            shaped((planes, quarter, D // 2), BF), 0, (gu_array,), (hidden,),
        )
        down_w = [first_down.reshape(ff_here, D // 2), last_down]
        mixed0, marks = plane_scatter(lambda first, count, after: block_product(hidden, down_w[0], first, count, False, after))
        mixed1, _ = plane_scatter(
            lambda first, count, after: block_product(hidden, down_w[1], first, count, False, after + marks)
        )
        mixed = jnp.concatenate([mixed0, mixed1], axis=1)
        mixed_scale = row_scale(mixed)
        block_output = ((middle + mixed * mixed_scale * gain_m) * live).astype(BF)

        grad_rows = out_cotangent.astype(F32) * live
        d_mixed, d_gain_mlp = norm_back(mixed, mixed_scale, gain_m, grad_rows)
        early = []
        dm_halves = [d_mixed[:, cut].astype(BF) for cut in HALVES]
        dm_all = [plane_gather(dm_halves[0], early)]
        grad_down_parts = [product_tn(hidden, dm_all[0]).astype(BF)]
        dm_all.append(plane_gather(ordered(dm_halves[1], early), hold=grad_down_parts))
        grad_down_parts = grad_down_parts + [product_tn(hidden, dm_all[1]).astype(BF)]

        def plane_sum(values):
            return lax.psum_scatter(values.astype(BF), "z", scatter_dimension=0, tiled=True)

        grad_down = [plane_sum(part) for part in grad_down_parts]
        d_gu = call(
            hidden_back_kernel, (blocks,),
            [row_block(D // 2), row_block(D // 2), resident((ff_here, D // 2)), resident((ff_here, D // 2)),
             row_block(2 * ff_here)],
            row_block(2 * ff_here), shaped((all_rows, 2 * ff_here), BF), 2 * all_rows * D * ff_here,
            (*dm_all, *down_w, gate_up), grad_down_parts,
        )
        down_first = ordered(grad_down[0], (d_gu,))
        grad_gu_part = weight_grad(mid_all, d_gu, (down_first,))[0]
        grad_gu = plane_sum(grad_gu_part)
        d_middle, _ = plane_scatter(
            lambda first, count, after: block_product(d_gu, gu_w, first, count, True, after + (grad_gu_part,))
        )
        scalars = jnp.stack([a, c, y]).astype(jnp.int32)

        def member_of(j_a, j_c, scalars):
            return (scalars[0] ^ j_a) * 2 + (scalars[1] ^ j_c)

        d_middle = grad_rows + d_middle
        down_last = ordered(grad_down[1], (d_middle,))

        d_branch, d_gain_attn = norm_back(branch, branch_scale, gain_a, d_middle)
        def attention_back(first, pieces, filled, after):
            places = []
            for piece in pieces:
                places.append((sum(p.shape[0] for p in pieces[: len(places)]), piece.shape[0]))
            count = sum(rows for _, rows in places) // BLOCK

            def kernel(*refs):
                ins, rest = refs[: len(pieces)], refs[len(pieces) :]
                db_ref = rest[8 + len(filled)]
                for (start, rows), ref in zip(places, ins):

                    @pl.when(pl.program_id(0) == start // BLOCK)
                    def _():
                        db_ref[start % BLOCK : start % BLOCK + rows, :] = ref[...]

                attention_back_kernel(*rest[:8], *rest[8 + len(filled) :])

            return call_back(kernel, first, count, pieces, filled, after)

        def call_back(kernel, first, count, pieces, filled, after):
            known = len(pieces) + 8
            shapes = [
                shaped((all_rows, D), BF), shaped((all_rows, 2 * width), F32), shaped((all_rows, width), BF),
                shaped((2, all_rows), F32), shaped((count, 2, width), F32),
            ]
            anywhere = pl.BlockSpec(memory_space=pl.ANY)
            args = (low, qkv, squares, seg_row, cosine, sine, gain_qk, out_rows)
            extra = len(after)

            def body(*refs):
                kernel(*refs[: known + len(filled)], *refs[known + len(filled) + extra :])

            return pl.pallas_call(
                body,
                grid=(count,),
                in_specs=[resident(piece.shape) for piece in pieces]
                + [
                    row_block(3 * width, first), row_block(2 * width, first), stat_block(first),
                    pl.BlockSpec((1, BLOCK), lambda i: (0, first + i)), row_block(HEAD_DIM, first),
                    row_block(HEAD_DIM, first), resident((2, width)), resident((width, D)),
                ]
                + [anywhere] * (len(filled) + extra),
                out_specs=[
                    row_block(D, first), row_block(2 * width, first), row_block(width, first), stat_block(first),
                    pl.BlockSpec((1, 2, width), lambda i: (i, 0, 0)),
                ],
                out_shape=shapes,
                input_output_aliases={known + k: k for k in range(len(filled))},
                compiler_params=pltpu.CompilerParams(vmem_limit_bytes=58 * 1024 * 1024),
                cost_estimate=cost(2 * count * BLOCK * width * (D + 12 * MB), *pieces),
            )(*pieces, *args, *filled, *after)

        half = own_rows // 2
        db_own = d_branch.astype(BF)
        db_a, db_y = swap(db_own, "a"), swap(db_own, "y")
        *filled, gain_part0 = attention_back(6, [db_own, swap(db_own, "c")], (), (down_last,))
        top = swap(ordered(db_y[:half], (gain_part0,)), "a")
        bottom = swap(ordered(db_a[half:], (gain_part0,)), "y")
        far_a, far_y = swap(db_a, "c"), swap(db_y, "c")
        *filled, gain_part1 = attention_back(2, [db_a, far_a, db_y, far_y], filled, ())
        corner = [top, bottom] + [swap(ordered(piece, (gain_part1,)), "c") for piece in (top, bottom)]
        db_all, n_qk, d_value, dots, gain_part2 = attention_back(0, corner, filled, ())
        gu_mine, gu_given = split_rows(grad_gu, y, shard_rows, (gain_part1, top, bottom))
        grad_down_all = lax.all_gather(beside(down_first, down_last, (gu_mine,)), ("a", "c"), axis=0, tiled=True)
        gain_part = jnp.concatenate([gain_part0, gain_part1, gain_part2], axis=0)
        d_gain_query, d_gain_key = jnp.sum(gain_part, axis=0)
        zero = jnp.zeros((D,), F32)
        totals = jnp.concatenate(
            [
                dots.reshape(2, all_rows // D, D).reshape(-1, D),
                lax.dynamic_update_slice(zero, d_gain_query, (pair * width,))[None],
                lax.dynamic_update_slice(zero, d_gain_key, (pair * width,))[None],
                d_gain_attn[None],
                d_gain_mlp[None],
            ]
        )
        for axis, dim in (("a", 1), ("y", 2), ("c", 3)):
            other = swap(totals, axis)
            turned = jnp.flip(other[:-4].reshape(2, 2, 2, 2, own_rows), dim).reshape(-1, D)
            totals = totals + jnp.concatenate([turned, other[-4:]])
            if axis == "a":
                grad_out = weight_grad(attended, db_all, (totals,))[0]
                if planes == 4:
                    out_mine, out_other = exchange_first(grad_out.reshape(planes, -1, D), a)
        dots, gain_terms = totals[:-4].reshape(2, all_rows), totals[-4:]
        d_qkv = call(
            qkv_back_kernel, (blocks,),
            [row_block(2 * width), row_block(2 * width), stat_block(), stat_block(), row_block(width)],
            row_block(3 * width), shaped((all_rows, 3 * width), BF), 0, (n_qk, qkv, squares, dots, d_value),
            (grad_down_all,),
        )
        gain_rows = jnp.transpose(gain_terms.reshape(4, planes, 2, shard_rows), (1, 2, 0, 3)).reshape(planes, -1)
        more = -(8 * shard_rows) % (3 * width)
        gain_rows = jnp.pad(gain_rows.astype(BF), ((0, 0), (0, more))).reshape(planes, -1, 3 * width)
        gain_rows = jnp.pad(gain_rows, ((0, 0), (0, 16 - gain_rows.shape[1]), (0, 0)))
        grad_qkv_part = weight_grad(x_all, d_qkv, (), planes, 16)
        grad_qkv = plane_sum(
            lax.dynamic_update_slice(grad_qkv_part, gain_rows, (0, 2 * shard_rows, 0)).reshape(-1, 3 * width)
        )
        own_gains = grad_qkv[2 * shard_rows :].reshape(-1)[: 8 * shard_rows].reshape(2, 4, shard_rows)
        own_gains = lax.dynamic_index_in_dim(own_gains, y, 0, keepdims=False).astype(F32)
        if planes == 4:
            grad_out = exchange_last(out_mine, ordered(out_other, (grad_qkv_part,)), a, c).reshape(width, D)
            grad_out = plane_sum(ordered(grad_out, (grad_qkv,)))
        gu_near, gu_other = (swap(ordered(piece, (grad_qkv_part,)), axis) for piece, axis in ((gu_mine, "a"), (gu_given, "y")))
        gu_far = swap(gu_other, "a")
        gu_pieces = [gu_mine, gu_other, gu_near, gu_far]
        gu_pieces += [swap(piece, "c") for piece in gu_pieces]
        def column_pair(j, scalars):
            return member_of((j // 2) % 2, j // 4, scalars), scalars[2] ^ (j % 2)

        if quarter % 128 == 0:
            owners = [column_pair(j, scalars) for j in range(8)]
            places = jnp.stack([jnp.stack([(p * 2 + of_y) * 4 + of for p in range(planes)]) for of, of_y in owners])
            grad_gate, grad_up = assemble_hidden(gu_pieces, 8 * ff_here, places.astype(jnp.int32), quarter, planes)
        else:
            filled = jnp.zeros((shard_rows, 2, planes, 2, 4, quarter), F32)
            for j, piece in enumerate(gu_pieces):
                owner, which_y = column_pair(j, scalars)
                piece = piece.astype(F32).reshape(shard_rows, 2, planes, 1, 1, quarter)
                filled = lax.dynamic_update_slice(filled, piece, (0, 0, 0, which_y, owner, 0))
            grad_gate, grad_up = (filled[:, o].reshape(shard_rows, 8 * ff_here) for o in range(2))

        qkv_mine, qkv_given = split_rows(grad_qkv, y, shard_rows)
        qkv_near, qkv_other = swap(qkv_mine, "a"), swap(qkv_given, "y")
        in_parts = []

        def in_part(first, count, after):
            in_parts.append(block_product(d_qkv, qkv_w, first, count, True, after + (grad_qkv_part,)))
            return in_parts[-1]


        d_input, _ = plane_scatter(in_part, lean=True)
        d_input = d_middle + d_input

        def qkv_place(o, j, s, scalars):
            owner, which_y = column_pair(j, scalars)
            return 0, owner * 2 + which_y

        qkv_far = swap(qkv_other, "a")
        qkv_pieces = [qkv_mine, qkv_other, qkv_near, qkv_far]
        qkv_pieces += [swap(piece, "c") for piece in qkv_pieces]
        grad_query, grad_key, grad_value = assemble(
            qkv_pieces, [shaped((shard_rows, D), F32)] * 3, shard_rows, width, 1,
            lambda o, s: (0, o), qkv_place, scalars,
        )
        if planes == 4:
            (grad_out,) = assemble(
                spread([grad_out]), [shaped((shard_rows, D), F32)], shard_rows // 4, D, 1,
                lambda o, s: (0, 0), lambda o, j, s, scalars: (member_of(j % 2, j // 2, scalars), 0), scalars,
            )
        else:
            whole = lax.dynamic_update_slice(jnp.zeros((D, D), BF), grad_out, (pair * width, 0))
            whole = lax.psum_scatter(whole, ("z", "y"), scatter_dimension=0, tiled=True)
            grad_out = lax.psum(whole, ("a", "c")).astype(F32)

        return (
            block_output,
            d_input,
            grad_query,
            grad_key,
            grad_value,
            grad_out,
            own_gains[0],
            own_gains[1],
            own_gains[2],
            grad_gate,
            grad_up,
            grad_down_all.astype(F32),
            own_gains[3],
        )

    return body


def solution(mesh):
    replicas, shards = mesh.shape["dp"], mesh.shape["fsdp"]
    planes = shards // 2
    fine = Mesh(mesh.devices.reshape(replicas // 2, 2, planes, 2), ("a", "c", "z", "y"))
    tokens = ("a", "c", "z", "y")
    owner = ("z", "y")
    rows, row, wide, vec = P(tokens, None), P(tokens), P(owner, None), P(owner)
    in_specs = (rows, row, wide, wide, wide, wide, vec, vec, vec, wide, wide, wide, vec, rows)
    out_specs = (rows, rows, wide, wide, wide, wide, vec, vec, vec, wide, wide, wide, vec)
    return jax.shard_map(make_body(planes), mesh=fine, in_specs=in_specs, out_specs=out_specs, check_vma=False)
```

time: 941 us -> 886 us (0.942)
  matrix products: 56.3 us -> 11.9 us
  Pallas kernels: 191 us -> 224 us
  starting transfers between devices: 101 us -> 74.4 us
  waiting for transfers between devices: 397 us -> 377 us
    pallas_call x20 -> x44, Pallas kernels: 153 us -> 215 us  [the longest x38 168 us: call(): pl.pallas_call(body, grid=grid, in_specs=list(in_specs) + [anywhere] * ex...]
    dot_general x5 -> x2, matrix products: 56.3 us -> 11.9 us  [product_tn(): lax.dot_general(left_rows, right_rows, (((0,), (0,)), ((), ())), preferre...]
    pallas_call x4 -> x2, Pallas kernels: 38.5 us -> 8.97 us  [assemble(): pl.pallas_call(kernel, grid_spec=pltpu.PrefetchScalarGridSpec(num_scalar_...]
    ppermute x123 -> x117, waiting for transfers between devices: 345 us -> 317 us  [swap(): return lax.ppermute(values, axis, SWAP)]
    all_to_all x2 -> x0, waiting for transfers between devices: 19.3 us -> none  [the longest x1 10.4 us: body(): lax.all_to_all(grad_out, ('a', 'c'), split_axis=0, concat_axis=0, tiled=T...]
    reduce_scatter x5, waiting for transfers between devices: 0.03 us -> 19 us  [plane_sum(): lax.psum_scatter(values.astype(BF), 'z', scatter_dimension=0, tiled=True)]
    ppermute x123 -> x117, starting transfers between devices: 89.2 us -> 74 us  [swap(): return lax.ppermute(values, axis, SWAP)]
    all_gather x5 -> x4, waiting for transfers between devices: 29.5 us -> 40.9 us  [the longest x3 30.3 us: gather_planes(): return lax.all_gather(piece, 'z', axis=0, tiled=False)]
  transfers between devices with their start and end apart: 139 -> 126, of which waited for: 53 -> 56; matrix products, arithmetic and copies ran while one was open for 18% -> 13% of each run, Pallas kernels for 18% -> 23%
where the time goes in v2:
time: 886 us; the launch traced here: 877 us
  waiting for transfers between devices  377 us (43%)
  Pallas kernels  224 us (25%)
  local copies, waits for them, and re-layouts  124 us (14%)
  starting transfers between devices  74.4 us (8%)
  other arithmetic  49.5 us (6%)
  between operations  16.8 us (2%)
  matrix products  11.9 us (1%)
    ppermute x117, waiting for transfers between devices, swap(): return lax.ppermute(values, axis, SWAP)  317 us
    pallas_call x38, Pallas kernels, call(): pl.pallas_call(body, grid=grid, in_specs=list(in_specs) + [anywhere] * ex...  168 us
    unnamed x238, local copies, waits for them, and re-layouts  93.5 us
    ppermute x117, starting transfers between devices, swap(): return lax.ppermute(values, axis, SWAP)  74 us
    pallas_call x3, Pallas kernels, call_back(): pl.pallas_call(body, grid=(count,), in_specs=[resident(piece.shape) for p...  31.4 us
    all_gather x3, waiting for transfers between devices, gather_planes(): return lax.all_gather(piece, 'z', axis=0, tiled=False)  30.3 us
    reduce_scatter x5, waiting for transfers between devices, plane_sum(): lax.psum_scatter(values.astype(BF), 'z', scatter_dimension=0, tiled=True)  19 us
  transfers between devices with their start and end apart: 126, of which 56 were waited for; matrix products, arithmetic and copies ran while one was open for 13% of the time, Pallas kernels for 23%

profile of v2, /device:TPU:0, one launch (start us, length us, event | category | flops | bytes accessed | tf_op | source)
XLA Modules:
  0.0 876.7 jit_solution(16110039658540647769)
XLA Ops:
  13.7 8.8 %collective-permute-done.9 = bf16[256,768]{1,0:T(8,128)(2,1)S(1)} collective-permute-done((bf16[256,768]{1,0:T(8,128)(2,1)S(1)}, bf16[256,768]{1,0:T(8,128)(2,1)S(1)}, u32[]{:S(2)}, u32[]{:S(2)}) %collective-permute-start.9) | collective-permute-done | bytes 393248 | tf_op jit(solution)/shard_map/ppermute | solution.py:42
  38.0 10.5 %collective-permute-done.refs_2_ = bf16[256,2048]{1,0:T(8,128)(2,1)S(1)} collective-permute-done((bf16[256,2048]{1,0:T(8,128)(2,1)}, bf16[256,2048]{1,0:T(8,128)(2,1)S(1)}, u32[]{:S(2)}, u32[]{:S(2)}) %collective-permute-start) | collective-permute-done | bytes 1048608 | tf_op jit(solution)/shard_map/ppermute | solution.py:42
  52.4 21.5 %collective-permute-done.36 = bf16[256,2048]{1,0:T(8,128)(2,1)S(1)} collective-permute-done((bf16[256,2048]{1,0:T(8,128)(2,1)}, bf16[256,2048]{1,0:T(8,128)(2,1)S(1)}, u32[]{:S(2)}, u32[]{:S(2)}) %collective-permute-start.36) | collective-permute-done | bytes 1048608 | tf_op jit(solution)/shard_map/ppermute | solution.py:42
  126.2 10.4 %shard_map.237 = (f32[2048,768]{1,0:T(8,128)S(1)}, f32[2,2048]{1,0:T(2,128)S(1)}) custom-call(bf16[2048,2048]{1,0:T(8,128)(2,1)} %constant_dynamic-update-slice_fusion.refs_0_, bf16[4,528,1024]{2,1,0:T(8,128)(2,1)S(1)} %bitcast.123, f32[2048,128]{1,0:T(8,128)S(1)} %get-tuple-element.176.refs_2_.refs_3_.refs_6_.refs_8_, ...), custom_call_target="tpu_custom_call" | custom-call | flops 6442450944 | bytes 19021824 | tf_op jit(solution)/shard_map/pallas_call | solution.py:145
  173.1 10.6 %collective-permute-done.22 = bf16[128,2048]{1,0:T(8,128)(2,1)S(1)} collective-permute-done((bf16[128,2048]{1,0:T(8,128)(2,1)S(1)}, bf16[128,2048]{1,0:T(8,128)(2,1)S(1)}, u32[]{:S(2)}, u32[]{:S(2)}) %collective-permute-start.22) | collective-permute-done | bytes 524320 | tf_op jit(solution)/shard_map/ppermute | solution.py:42
  186.7 21.7 %collective-permute-done.23 = bf16[256,2048]{1,0:T(8,128)(2,1)S(1)} collective-permute-done((bf16[256,2048]{1,0:T(8,128)(2,1)S(1)}, bf16[256,2048]{1,0:T(8,128)(2,1)S(1)}, u32[]{:S(2)}, u32[]{:S(2)}) %collective-permute-start.23) | collective-permute-done | bytes 1048608 | tf_op jit(solution)/shard_map/ppermute | solution.py:42
  214.9 21.6 %collective-permute-done.27 = bf16[256,2048]{1,0:T(8,128)(2,1)S(1)} collective-permute-done((bf16[256,2048]{1,0:T(8,128)(2,1)S(1)}, bf16[256,2048]{1,0:T(8,128)(2,1)S(1)}, u32[]{:S(2)}, u32[]{:S(2)}) %collective-permute-start.27) | collective-permute-done | bytes 1048608 | tf_op jit(solution)/shard_map/ppermute | solution.py:42
  239.4 9.3 %collective-permute-done.28 = bf16[128,2048]{1,0:T(8,128)(2,1)} collective-permute-done((bf16[128,2048]{1,0:T(8,128)(2,1)S(1)}, bf16[128,2048]{1,0:T(8,128)(2,1)}, u32[]{:S(2)}, u32[]{:S(2)}) %collective-permute-start.28) | collective-permute-done | bytes 524320 | tf_op jit(solution)/shard_map/ppermute | solution.py:42
  264.5 28.5 %all-gather.12.cloned.1.call-done = bf16[2560,2048]{1,0:T(8,128)(2,1)} async-done(((bf16[640,2048]{1,0:T(8,128)(2,1)}), bf16[2560,2048]{1,0:T(8,128)(2,1)}) %all-gather.12.cloned.1.call-update) | async-done | bytes 10485776 | tf_op jit(solution)/shard_map/all_gather | solution.py:536
  293.0 22.8 %shard_map.242 = (bf16[2048,2048]{1,0:T(8,128)(2,1)S(1)}, bf16[2048,1024]{1,0:T(8,128)(2,1)S(1)}) custom-call(bf16[2048,2048]{1,0:T(8,128)(2,1)} %constant_dynamic-update-slice_fusion.10.refs_0_, bf16[4,640,2048]{2,1,0:T(8,128)(2,1)} %bitcast.136), custom_call_target="tpu_custom_call" | custom-call | flops 17179869184 | bytes 31457280 | tf_op jit(solution)/shard_map/pallas_call | solution.py:145
  356.3 9.9 %collective-permute-done.48 = bf16[128,1024]{1,0:T(8,128)(2,1)S(1)} collective-permute-done((bf16[128,1024]{1,0:T(8,128)(2,1)S(1)}, bf16[128,1024]{1,0:T(8,128)(2,1)S(1)}, u32[]{:S(2)}, u32[]{:S(2)}) %collective-permute-start.48) | collective-permute-done | bytes 262176 | tf_op jit(solution)/shard_map/ppermute | solution.py:42
  377.3 8.7 collective-permute-done.49
  391.4 9.1 %collective-permute-done.53.refs_2_ = bf16[256,1024]{1,0:T(8,128)(2,1)S(1)} collective-permute-done((bf16[256,1024]{1,0:T(8,128)(2,1)S(1)}, bf16[256,1024]{1,0:T(8,128)(2,1)S(1)}, u32[]{:S(2)}, u32[]{:S(2)}) %collective-permute-start.53) | collective-permute-done | bytes 524320 | tf_op jit(solution)/shard_map/ppermute | solution.py:42
  423.8 12.6 %collective-permute-done.62 = bf16[256,1024]{1,0:T(8,128)(2,1)S(1)} collective-permute-done((bf16[256,1024]{1,0:T(8,128)(2,1)S(1)}, bf16[256,1024]{1,0:T(8,128)(2,1)S(1)}, u32[]{:S(2)}, u32[]{:S(2)}) %collective-permute-start.62) | collective-permute-done | bytes 524320 | tf_op jit(solution)/shard_map/ppermute | solution.py:42
  464.9 16.1 %shard_map.253.refs_1_.refs_0_ = bf16[2048,2048]{1,0:T(8,128)(2,1)} custom-call(bf16[2048,1024]{1,0:T(8,128)(2,1)S(1)} %copy-done.38, bf16[2048,1024]{1,0:T(8,128)(2,1)} %copy-done.80, bf16[1024,1024]{1,0:T(8,128)(2,1)S(1)} %bitcast.112, bf16[1024,1024]{1,0:T(8,128)(2,1)S(1)} %copy-done.24, bf16[2048,2048]{1,0:T(8,128)(2,1)} %copy-done.33, ...), custom_call_target="tpu_custom_call" | custom-call | flops 8589934592 | bytes 29360128 | tf_op jit(solution)/shard_map/pallas_call | solution.py:145
  485.5 22.8 %shard_map.255 = bf16[1,2048,2048]{2,1,0:T(8,128)(2,1)S(1)} custom-call(bf16[2048,2048]{1,0:T(8,128)(2,1)} %constant_dynamic-update-slice_fusion.10.refs_0_, bf16[2048,2048]{1,0:T(8,128)(2,1)} %shard_map.253.refs_1_.refs_0_, bf16[256,1024]{1,0:T(8,128)(2,1)S(1)} %shard_map.254.refs_2_.refs_0_), custom_call_target="tpu_custom_call" | custom-call | flops 17179869184 | bytes 25165824 | tf_op jit(solution)/shard_map/pallas_call | solution.py:145
  515.1 9.1 %shard_map.256.refs_2_ = bf16[512,2048]{1,0:T(8,128)(2,1)S(1)} custom-call(bf16[2048,2048]{1,0:T(8,128)(2,1)S(1)} %copy-done.5, bf16[4,640,2048]{2,1,0:T(8,128)(2,1)} %bitcast.138, bf16[2048,2048]{1,0:T(8,128)(2,1)} %bitcast.106), custom_call_target="tpu_custom_call" | custom-call | flops 4294967296 | bytes 20971520 | tf_op jit(solution)/shard_map/pallas_call | solution.py:145
  524.4 13.4 %shard_map.257.refs_3_ = bf16[1024,2048]{1,0:T(8,128)(2,1)S(1)} custom-call(bf16[2048,2048]{1,0:T(8,128)(2,1)} %shard_map.253.refs_1_.refs_0_, bf16[4,640,2048]{2,1,0:T(8,128)(2,1)} %bitcast.139, bf16[512,2048]{1,0:T(8,128)(2,1)S(1)} %shard_map.256.refs_2_, bf16[2048,2048]{1,0:T(8,128)(2,1)} %bitcast.107), custom_call_target="tpu_custom_call" | custom-call | flops 8589934592 | bytes 23068672 | tf_op jit(solution)/shard_map/pallas_call | solution.py:145
  539.0 8.5 shard_map.258
  550.5 11.7 %collective-permute-done.74 = bf16[128,2048]{1,0:T(8,128)(2,1)S(1)} collective-permute-done((bf16[128,2048]{1,0:T(8,128)(2,1)S(1)}, bf16[128,2048]{1,0:T(8,128)(2,1)S(1)}, u32[]{:S(2)}, u32[]{:S(2)}) %collective-permute-start.74) | collective-permute-done | bytes 524320 | tf_op jit(solution)/shard_map/ppermute | solution.py:42
  565.2 21.7 %collective-permute-done.75 = bf16[256,2048]{1,0:T(8,128)(2,1)S(1)} collective-permute-done((bf16[256,2048]{1,0:T(8,128)(2,1)S(1)}, bf16[256,2048]{1,0:T(8,128)(2,1)S(1)}, u32[]{:S(2)}, u32[]{:S(2)}) %collective-permute-start.75) | collective-permute-done | bytes 1048608 | tf_op jit(solution)/shard_map/ppermute | solution.py:42
  596.0 22.0 %collective-permute-done.82.refs_0_ = bf16[256,2048]{1,0:T(8,128)(2,1)} collective-permute-done((bf16[256,2048]{1,0:T(8,128)(2,1)}, bf16[256,2048]{1,0:T(8,128)(2,1)}, u32[]{:S(2)}, u32[]{:S(2)}) %collective-permute-start.82) | collective-permute-done | bytes 1048608 | tf_op jit(solution)/shard_map/ppermute | solution.py:42
  624.6 8.7 shard_map.260
  637.9 14.2 %shard_map.263 = (bf16[2048,2048]{1,0:T(8,128)(2,1)}, f32[2048,512]{1,0:T(8,128)}, bf16[2048,256]{1,0:T(8,128)(2,1)}, f32[2,2048]{1,0:T(2,128)}, f32[4,2,256]{2,1,0:T(2,128)}) custom-call(bf16[256,2048]{1,0:T(8,128)(2,1)} %collective-permute-done.82.refs_0_, ...), custom_call_target="tpu_custom_call", output_to_operand_aliasing={{0}: (12, {}), {1}: (13, {}), {2}: (14, {}), {3}: (15, {})} | custom-call | flops 1879048192 | bytes 4194304 | tf_op jit(solution)/shard_map/pallas_call | solution.py:712
  662.8 8.5 shard_map.266
  685.3 10.7 %all-gather.8.cloned.1.call-done.refs_5_ = bf16[1024,2048]{1,0:T(8,128)(2,1)} async-done(((bf16[256,2048]{1,0:T(8,128)(2,1)}), bf16[1024,2048]{1,0:T(8,128)(2,1)}) %all-gather.8.cloned.1.call-update) | async-done | bytes 4194320 | tf_op jit(solution)/shard_map/all_gather | solution.py:743
  705.8 11.5 %shard_map.270.refs_2_.refs_3_.refs_4_.refs_1_ = bf16[4,528,768]{2,1,0:T(8,128)(2,1)S(1)} custom-call(bf16[2048,2048]{1,0:T(8,128)(2,1)} %constant_dynamic-update-slice_fusion.refs_0_, bf16[2048,768]{1,0:T(8,128)(2,1)S(1)} %shard_map.269.refs_1_.refs_0_), custom_call_target="tpu_custom_call" | custom-call | flops 6442450944 | bytes 14778368 | tf_op jit(solution)/shard_map/pallas_call | solution.py:145
  734.9 6.8 collective-permute-done.105.refs_0_
  765.9 15.7 %reduce-scatter.12.cloned.1.call-done.mine_ref.given_ref.refs_1_ = bf16[528,768]{1,0:T(8,128)(2,1)} async-done(((bf16[2112,768]{1,0:T(8,128)(2,1)}), bf16[528,768]{1,0:T(8,128)(2,1)}) %reduce-scatter.12.cloned.1.call-update) | async-done | bytes 811024 | tf_op jit(solution)/shard_map/reduce_scatter | solution.py:655
  804.6 29.1 %collective-permute-done.98.refs_3_.refs_4_.refs_5_ = bf16[256,768]{1,0:T(8,128)(2,1)S(1)} collective-permute-done((bf16[256,768]{1,0:T(8,128)(2,1)}, bf16[256,768]{1,0:T(8,128)(2,1)S(1)}, u32[]{:S(2)}, u32[]{:S(2)}) %collective-permute-start.98) | collective-permute-done | bytes 393248 | tf_op jit(solution)/shard_map/ppermute | solution.py:42
  834.6 6.8 convert_element_type.373
  849.1 10.4 %shard_map.282 = (f32[256,8192]{1,0:T(8,128)}, f32[256,8192]{1,0:T(8,128)}) custom-call(s32[8,4]{1,0:T(8,128)S(1)} %stack.343.places_ref, bf16[256,2048]{1,0:T(8,128)(2,1)} %get-tuple-element.74.refs_2_.refs_0_, bf16[256,2048]{1,0:T(8,128)(2,1)} %collective-permute-done.110.refs_1_, bf16[256,2048]{1,0:T(8,128)(2,1)} %collective-permute-done.111.refs_2_, ...), custom_call_target="tpu_custom_call" | custom-call | bytes 25165824 | tf_op jit(solution)/shard_map/pallas_call | solution.py:96
  (705 shorter events, 406.6 us)
Async XLA Ops:
  7.2 108.6 %all-gather.10.cloned.1.call-start = ((), (), s32[]{:S(2)}) async-start(), calls=%async_computation.11 | async-start | bytes 5406720 | tf_op jit(solution)/shard_map/all_gather | solution.py:536
  23.8 269.2 %all-gather.12.cloned.1.call-start = ((), (), s32[]{:S(2)}) async-start(), calls=%async_computation.12 | async-start | bytes 13107200 | tf_op jit(solution)/shard_map/all_gather | solution.py:536
  23.9 24.6 %collective-permute-start = (bf16[256,2048]{1,0:T(8,128)(2,1)}, bf16[256,2048]{1,0:T(8,128)(2,1)S(1)}, u32[]{:S(2)}, u32[]{:S(2)}) collective-permute-start(bf16[256,2048]{1,0:T(8,128)(2,1)} %param.14), channel_id=1, source_target_pairs={{0,1},{1,0},{2,3},{3,2},{4,5},{5,4},{6,7},{7,6},{8,9},{9,8},{10,11... | collective-permute-start | bytes 3145736 | tf_op jit(solution)/shard_map/ppermute | solution.py:42
  25.7 24.0 %collective-permute-start.2 = (bf16[256,2048]{1,0:T(8,128)(2,1)}, bf16[256,2048]{1,0:T(8,128)(2,1)S(1)}, u32[]{:S(2)}, u32[]{:S(2)}) collective-permute-start(bf16[256,2048]{1,0:T(8,128)(2,1)} %param.14), channel_id=1, source_target_pairs={{0,16},{16,0},{1,17},{17,1},{2,18},{18,2},{3,19},{19,3},{4,20},{20... | collective-permute-start | bytes 3145736 | tf_op jit(solution)/shard_map/ppermute | solution.py:42
  77.5 261.8 %all-gather.14.cloned.1.call-start = ((), (), s32[]{:S(2)}) async-start(), calls=%async_computation.13 | async-start | bytes 2621440 | tf_op jit(solution)/shard_map/all_gather | solution.py:536
  78.2 35.3 %collective-permute-start.8 = (bf16[256,2048]{1,0:T(8,128)(2,1)}, bf16[256,2048]{1,0:T(8,128)(2,1)}, u32[]{:S(2)}, u32[]{:S(2)}) collective-permute-start(bf16[256,2048]{1,0:T(8,128)(2,1)} %param.14), channel_id=1, source_target_pairs={{0,8},{8,0},{1,9},{9,1},{2,10},{10,2},{3,11},{11,3},{4,12},{12,4},... | collective-permute-start | bytes 3145736 | tf_op jit(solution)/shard_map/ppermute | solution.py:42
  183.9 24.5 %collective-permute-start.23 = (bf16[256,2048]{1,0:T(8,128)(2,1)S(1)}, bf16[256,2048]{1,0:T(8,128)(2,1)S(1)}, u32[]{:S(2)}, u32[]{:S(2)}) collective-permute-start(bf16[256,2048]{1,0:T(8,128)(2,1)S(1)} %pad_maximum_fusion.3), channel_id=1, source_target_pairs={{0,16},{16,0},{1,17},{17,1},{2,18},{18,2},{3,19},{19,3},{4,20},{20... | collective-permute-start | bytes 3145736 | tf_op jit(solution)/shard_map/ppermute | solution.py:42
  185.7 24.2 %collective-permute-start.26 = (bf16[256,2048]{1,0:T(8,128)(2,1)S(1)}, bf16[256,2048]{1,0:T(8,128)(2,1)S(1)}, u32[]{:S(2)}, u32[]{:S(2)}) collective-permute-start(bf16[256,2048]{1,0:T(8,128)(2,1)S(1)} %pad_maximum_fusion.4), channel_id=1, source_target_pairs={{0,1},{1,0},{2,3},{3,2},{4,5},{5,4},{6,7},{7,6},{8,9},{9,8},{10,11... | collective-permute-start | bytes 3145736 | tf_op jit(solution)/shard_map/ppermute | solution.py:42
  250.6 230.4 %reduce-scatter.6.cloned.1.call-start = ((), (), s32[]{:S(2)}) async-start(), calls=%async_computation.5 | async-start | bytes 2621440 | tf_op jit(solution)/shard_map/reduce_scatter | solution.py:655
  346.2 29.1 %collective-permute-start.38 = (bf16[256,1024]{1,0:T(8,128)(2,1)S(1)}, bf16[256,1024]{1,0:T(8,128)(2,1)S(1)}, u32[]{:S(2)}, u32[]{:S(2)}) collective-permute-start(bf16[256,1024]{1,0:T(8,128)(2,1)S(1)} %slice.439), channel_id=1, source_target_pairs={{0,8},{8,0},{1,9},{9,1},{2,10},{10,2},{3,11},{11,3},{4,12},{12,4},... | collective-permute-start | bytes 1572872 | tf_op jit(solution)/shard_map/ppermute | solution.py:42
  346.7 30.2 %collective-permute-start.44 = (bf16[256,1024]{1,0:T(8,128)(2,1)S(1)}, bf16[256,1024]{1,0:T(8,128)(2,1)S(1)}, u32[]{:S(2)}, u32[]{:S(2)}) collective-permute-start(bf16[256,1024]{1,0:T(8,128)(2,1)S(1)} %pad_maximum_fusion.9.refs_3_.refs_4_.refs_5_), channel_id=1, source_target_pairs={{0,1},{1,0},{2,3},{3,2},{4,5},{5,4},{6,7},{7,6},{8,9},{9,8},{10,11... | collective-permute-start | bytes 1572872 | tf_op jit(solution)/shard_map/ppermute | solution.py:42
  348.2 28.7 %collective-permute-start.41 = (bf16[256,1024]{1,0:T(8,128)(2,1)S(1)}, bf16[256,1024]{1,0:T(8,128)(2,1)S(1)}, u32[]{:S(2)}, u32[]{:S(2)}) collective-permute-start(bf16[256,1024]{1,0:T(8,128)(2,1)S(1)} %pad_maximum_fusion.8.refs_2_.refs_3_.refs_4_), channel_id=1, source_target_pairs={{0,16},{16,0},{1,17},{17,1},{2,18},{18,2},{3,19},{19,3},{4,20},{20... | collective-permute-start | bytes 1572872 | tf_op jit(solution)/shard_map/ppermute | solution.py:42
  421.1 200.6 %reduce-scatter.8.cloned.1.call-start = ((), (), s32[]{:S(2)}) async-start(), calls=%async_computation.6 | async-start | bytes 2621440 | tf_op jit(solution)/shard_map/reduce_scatter | solution.py:655
  457.8 197.6 %reduce-scatter.10.cloned.1.call-start = ((), (), s32[]{:S(2)}) async-start(), calls=%async_computation.7 | async-start | bytes 10485760 | tf_op jit(solution)/shard_map/reduce_scatter | solution.py:655
  511.7 184.2 %all-gather.8.cloned.1.call-start = ((), (), s32[]{:S(2)}) async-start(), calls=%async_computation.8 | async-start | bytes 5242880 | tf_op jit(solution)/shard_map/all_gather | solution.py:743
  562.4 24.5 %collective-permute-start.75 = (bf16[256,2048]{1,0:T(8,128)(2,1)S(1)}, bf16[256,2048]{1,0:T(8,128)(2,1)S(1)}, u32[]{:S(2)}, u32[]{:S(2)}) collective-permute-start(bf16[256,2048]{1,0:T(8,128)(2,1)S(1)} %pad_maximum_fusion.5), channel_id=1, source_target_pairs={{0,16},{16,0},{1,17},{17,1},{2,18},{18,2},{3,19},{19,3},{4,20},{20... | collective-permute-start | bytes 3145736 | tf_op jit(solution)/shard_map/ppermute | solution.py:42
  564.3 24.2 %collective-permute-start.78 = (bf16[256,2048]{1,0:T(8,128)(2,1)S(1)}, bf16[256,2048]{1,0:T(8,128)(2,1)S(1)}, u32[]{:S(2)}, u32[]{:S(2)}) collective-permute-start(bf16[256,2048]{1,0:T(8,128)(2,1)S(1)} %pad_maximum_fusion.6), channel_id=1, source_target_pairs={{0,1},{1,0},{2,3},{3,2},{4,5},{5,4},{6,7},{7,6},{8,9},{9,8},{10,11... | collective-permute-start | bytes 3145736 | tf_op jit(solution)/shard_map/ppermute | solution.py:42
  596.0 28.6 %collective-permute-start.80 = (bf16[256,2048]{1,0:T(8,128)(2,1)}, bf16[256,2048]{1,0:T(8,128)(2,1)}, u32[]{:S(2)}, u32[]{:S(2)}) collective-permute-start(bf16[256,2048]{1,0:T(8,128)(2,1)} %subtract_convert_fusion.refs_0_), channel_id=1, source_target_pairs={{0,8},{8,0},{1,9},{9,1},{2,10},{10,2},{3,11},{11,3},{4,12},{12,4},... | collective-permute-start | bytes 3145736 | tf_op jit(solution)/shard_map/ppermute | solution.py:42
  659.2 122.5 %reduce-scatter.12.cloned.1.call-start = ((), (), s32[]{:S(2)}) async-start(), calls=%async_computation.9 | async-start | bytes 4055040 | tf_op jit(solution)/shard_map/reduce_scatter | solution.py:655
  719.7 124.5 %reduce-scatter.14.cloned.1.call-start = ((), (), s32[]{:S(2)}) async-start(), calls=%async_computation.10 | async-start | bytes 1310720 | tf_op jit(solution)/shard_map/reduce_scatter | solution.py:655
  728.6 35.7 %collective-permute-start.111 = (bf16[256,2048]{1,0:T(8,128)(2,1)S(1)}, bf16[256,2048]{1,0:T(8,128)(2,1)}, u32[]{:S(2)}, u32[]{:S(2)}) collective-permute-start(bf16[256,2048]{1,0:T(8,128)(2,1)S(1)} %shard_map.281), channel_id=1, source_target_pairs={{0,16},{16,0},{1,17},{17,1},{2,18},{18,2},{3,19},{19,3},{4,20},{20... | collective-permute-start | bytes 3145736 | tf_op jit(solution)/shard_map/ppermute | solution.py:42
  730.4 24.9 %collective-permute-start.110 = (bf16[256,2048]{1,0:T(8,128)(2,1)S(1)}, bf16[256,2048]{1,0:T(8,128)(2,1)}, u32[]{:S(2)}, u32[]{:S(2)}) collective-permute-start(bf16[256,2048]{1,0:T(8,128)(2,1)S(1)} %shard_map.280), channel_id=1, source_target_pairs={{0,1},{1,0},{2,3},{3,2},{4,5},{5,4},{6,7},{7,6},{8,9},{9,8},{10,11... | collective-permute-start | bytes 3145736 | tf_op jit(solution)/shard_map/ppermute | solution.py:42
  755.3 29.7 %collective-permute-start.96 = (bf16[256,2048]{1,0:T(8,128)(2,1)}, bf16[256,2048]{1,0:T(8,128)(2,1)}, u32[]{:S(2)}, u32[]{:S(2)}) collective-permute-start(bf16[256,2048]{1,0:T(8,128)(2,1)} %get-tuple-element.97), channel_id=1, source_target_pairs={{0,8},{8,0},{1,9},{9,1},{2,10},{10,2},{3,11},{11,3},{4,12},{12,4},... | collective-permute-start | bytes 3145736 | tf_op jit(solution)/shard_map/ppermute | solution.py:42
  755.4 38.0 %collective-permute-start.112 = (bf16[256,2048]{1,0:T(8,128)(2,1)}, bf16[256,2048]{1,0:T(8,128)(2,1)}, u32[]{:S(2)}, u32[]{:S(2)}) collective-permute-start(bf16[256,2048]{1,0:T(8,128)(2,1)} %collective-permute-done.110.refs_1_), channel_id=1, source_target_pairs={{0,16},{16,0},{1,17},{17,1},{2,18},{18,2},{3,19},{19,3},{4,20},{20... | collective-permute-start | bytes 3145736 | tf_op jit(solution)/shard_map/ppermute | solution.py:42
  757.1 36.8 %collective-permute-start.94 = (bf16[256,2048]{1,0:T(8,128)(2,1)}, bf16[256,2048]{1,0:T(8,128)(2,1)}, u32[]{:S(2)}, u32[]{:S(2)}) collective-permute-start(bf16[256,2048]{1,0:T(8,128)(2,1)} %add_convert_fusion.2.refs_2_), channel_id=1, source_target_pairs={{0,1},{1,0},{2,3},{3,2},{4,5},{5,4},{6,7},{7,6},{8,9},{9,8},{10,11... | collective-permute-start | bytes 3145736 | tf_op jit(solution)/shard_map/ppermute | solution.py:42
  764.3 34.0 %collective-permute-start.113 = (bf16[256,2048]{1,0:T(8,128)(2,1)}, bf16[256,2048]{1,0:T(8,128)(2,1)}, u32[]{:S(2)}, u32[]{:S(2)}) collective-permute-start(bf16[256,2048]{1,0:T(8,128)(2,1)} %get-tuple-element.74.refs_2_.refs_0_), channel_id=1, source_target_pairs={{0,8},{8,0},{1,9},{9,1},{2,10},{10,2},{3,11},{11,3},{4,12},{12,4},... | collective-permute-start | bytes 3145736 | tf_op jit(solution)/shard_map/ppermute | solution.py:42
  765.4 34.4 %collective-permute-start.115 = (bf16[256,2048]{1,0:T(8,128)(2,1)}, bf16[256,2048]{1,0:T(8,128)(2,1)}, u32[]{:S(2)}, u32[]{:S(2)}) collective-permute-start(bf16[256,2048]{1,0:T(8,128)(2,1)} %collective-permute-done.111.refs_2_), channel_id=1, source_target_pairs={{0,8},{8,0},{1,9},{9,1},{2,10},{10,2},{3,11},{11,3},{4,12},{12,4},... | collective-permute-start | bytes 3145736 | tf_op jit(solution)/shard_map/ppermute | solution.py:42
  793.9 47.5 %collective-permute-start.116 = (bf16[256,2048]{1,0:T(8,128)(2,1)}, bf16[256,2048]{1,0:T(8,128)(2,1)}, u32[]{:S(2)}, u32[]{:S(2)}) collective-permute-start(bf16[256,2048]{1,0:T(8,128)(2,1)} %collective-permute-done.112.refs_3_), channel_id=1, source_target_pairs={{0,8},{8,0},{1,9},{9,1},{2,10},{10,2},{3,11},{11,3},{4,12},{12,4},... | collective-permute-start | bytes 3145736 | tf_op jit(solution)/shard_map/ppermute | solution.py:42
  798.3 43.1 %collective-permute-start.95 = (bf16[256,2048]{1,0:T(8,128)(2,1)}, bf16[256,2048]{1,0:T(8,128)(2,1)}, u32[]{:S(2)}, u32[]{:S(2)}) collective-permute-start(bf16[256,2048]{1,0:T(8,128)(2,1)} %get-tuple-element.94), channel_id=1, source_target_pairs={{0,16},{16,0},{1,17},{17,1},{2,18},{18,2},{3,19},{19,3},{4,20},{20... | collective-permute-start | bytes 3145736 | tf_op jit(solution)/shard_map/ppermute | solution.py:42
  799.8 44.4 %collective-permute-start.97 = (bf16[256,2048]{1,0:T(8,128)(2,1)}, bf16[256,2048]{1,0:T(8,128)(2,1)}, u32[]{:S(2)}, u32[]{:S(2)}) collective-permute-start(bf16[256,2048]{1,0:T(8,128)(2,1)} %get-tuple-element.95), channel_id=1, source_target_pairs={{0,1},{1,0},{2,3},{3,2},{4,5},{5,4},{6,7},{7,6},{8,9},{9,8},{10,11... | collective-permute-start | bytes 3145736 | tf_op jit(solution)/shard_map/ppermute | solution.py:42
  803.2 30.4 %collective-permute-start.98 = (bf16[256,768]{1,0:T(8,128)(2,1)}, bf16[256,768]{1,0:T(8,128)(2,1)S(1)}, u32[]{:S(2)}, u32[]{:S(2)}) collective-permute-start(bf16[256,768]{1,0:T(8,128)(2,1)} %get-tuple-element.76), channel_id=1, source_target_pairs={{0,1},{1,0},{2,3},{3,2},{4,5},{5,4},{6,7},{7,6},{8,9},{9,8},{10,11... | collective-permute-start | bytes 1179656 | tf_op jit(solution)/shard_map/ppermute | solution.py:42
  803.9 38.0 %collective-permute-start.99 = (bf16[256,768]{1,0:T(8,128)(2,1)}, bf16[256,768]{1,0:T(8,128)(2,1)S(1)}, u32[]{:S(2)}, u32[]{:S(2)}) collective-permute-start(bf16[256,768]{1,0:T(8,128)(2,1)} %get-tuple-element.75.refs_0_.refs_1_.refs_2_), channel_id=1, source_target_pairs={{0,16},{16,0},{1,17},{17,1},{2,18},{18,2},{3,19},{19,3},{4,20},{20... | collective-permute-start | bytes 1179656 | tf_op jit(solution)/shard_map/ppermute | solution.py:42
  (189 other events, 1890.9 us)
Sparse Core Ops, SparseCore 0:
  23.9 84.3 all-gather.9
  110.5 182.4 all-gather.11
  295.1 44.1 all-gather.13
  421.2 41.5 reduce-scatter.5
  465.6 43.1 reduce-scatter.7
  511.8 143.5 reduce-scatter.9
  659.3 36.5 all-gather.7
  719.8 61.7 reduce-scatter.11
  785.2 27.2 reduce-scatter.13

commit v3 on v2

--- a/solution.py
+++ b/solution.py
@@ -285,7 +285,10 @@
     out_ref[:, 2 * width :] = dv_ref[...]
 
 
-def gate_up_kernel(mid_ref, w_ref, gate_up_ref, hidden_ref):
+def gate_up_kernel(mid_ref, w_ref, *refs):
+    gate_up_ref, hidden_ref = refs[1:3] if len(refs) > 2 else refs
+    if len(refs) > 2:
+        refs[3][...] = refs[0][...]
     half = hidden_ref.shape[1]
     both = product(mid_ref[...], flat(w_ref))
     gate, up = both[:, :half], both[:, half:]
@@ -617,23 +620,24 @@
         middle = block_input.astype(F32) + branch * branch_scale * gain_a
         mid_all = plane_gather(middle.astype(BF))
 
-        gate_up, hidden = call(
-            gate_up_kernel, (blocks,), [row_block(D), resident_view(gu_w)],
-            [row_block(2 * ff_here), row_block(ff_here)],
-            [shaped((all_rows, 2 * ff_here), BF), shaped((all_rows, ff_here), BF)], 4 * all_rows * D * ff_here,
-            (mid_all, gu_array),
-        )
         size, first = quarter // 2, 2 * shard_rows // (quarter // 2)
-
-        def take_kernel(in_ref, out_ref):
-            out_ref[...] = in_ref[...]
-
-        first_down = call(
-            take_kernel, (2 * planes,), [pl.BlockSpec((1, size, D // 2), lambda i: (i // 2, first, i % 2))],
-            pl.BlockSpec((1, size, D // 2), lambda i: (i // 2, i % 2, 0)),
-            shaped((planes, quarter, D // 2), BF), 0, (gu_array,), (hidden,),
-        )
-        down_w = [first_down.reshape(ff_here, D // 2), last_down]
+        half_in = pl.BlockSpec((1, size, D // 2), lambda i: (i // 2, first, i % 2))
+        half_out = pl.BlockSpec((1, size, D // 2), lambda i: (i // 2, i % 2, 0))
+        half_shape = shaped((planes, quarter, D // 2), BF)
+        together = blocks == 2 * planes
+        gate_up, hidden, *first_down = call(
+            gate_up_kernel, (blocks,), [row_block(D), resident_view(gu_w)] + [half_in] * together,
+            [row_block(2 * ff_here), row_block(ff_here)] + [half_out] * together,
+            [shaped((all_rows, 2 * ff_here), BF), shaped((all_rows, ff_here), BF)] + [half_shape] * together,
+            4 * all_rows * D * ff_here, (mid_all, gu_array) + (gu_array,) * together,
+        )
+        if not together:
+
+            def take_kernel(in_ref, out_ref):
+                out_ref[...] = in_ref[...]
+
+            first_down = call(take_kernel, (2 * planes,), [half_in], [half_out], [half_shape], 0, (gu_array,), (hidden,))
+        down_w = [first_down[0].reshape(ff_here, D // 2), last_down]
         mixed0, marks = plane_scatter(lambda first, count, after: block_product(hidden, down_w[0], first, count, False, after))
         mixed1, _ = plane_scatter(
             lambda first, count, after: block_product(hidden, down_w[1], first, count, False, after + marks)
@@ -660,7 +664,7 @@
             [row_block(D // 2), row_block(D // 2), resident((ff_here, D // 2)), resident((ff_here, D // 2)),
              row_block(2 * ff_here)],
             row_block(2 * ff_here), shaped((all_rows, 2 * ff_here), BF), 2 * all_rows * D * ff_here,
-            (*dm_all, *down_w, gate_up), grad_down_parts,
+            (*dm_all, *down_w, gate_up), grad_down_parts[:1],
         )
         down_first = ordered(grad_down[0], (d_gu,))
         grad_gu_part = weight_grad(mid_all, d_gu, (down_first,))[0]
@@ -766,13 +770,12 @@
             qkv_back_kernel, (blocks,),
             [row_block(2 * width), row_block(2 * width), stat_block(), stat_block(), row_block(width)],
             row_block(3 * width), shaped((all_rows, 3 * width), BF), 0, (n_qk, qkv, squares, dots, d_value),
-            (grad_down_all,),
         )
         gain_rows = jnp.transpose(gain_terms.reshape(4, planes, 2, shard_rows), (1, 2, 0, 3)).reshape(planes, -1)
         more = -(8 * shard_rows) % (3 * width)
         gain_rows = jnp.pad(gain_rows.astype(BF), ((0, 0), (0, more))).reshape(planes, -1, 3 * width)
         gain_rows = jnp.pad(gain_rows, ((0, 0), (0, 16 - gain_rows.shape[1]), (0, 0)))
-        grad_qkv_part = weight_grad(x_all, d_qkv, (), planes, 16)
+        grad_qkv_part = weight_grad(x_all, d_qkv, (grad_down_all,), planes, 16)
         grad_qkv = plane_sum(
             lax.dynamic_update_slice(grad_qkv_part, gain_rows, (0, 2 * shard_rows, 0)).reshape(-1, 3 * width)
         )
@@ -780,7 +783,6 @@
         own_gains = lax.dynamic_index_in_dim(own_gains, y, 0, keepdims=False).astype(F32)
         if planes == 4:
             grad_out = exchange_last(out_mine, ordered(out_other, (grad_qkv_part,)), a, c).reshape(width, D)
-            grad_out = plane_sum(ordered(grad_out, (grad_qkv,)))
         gu_near, gu_other = (swap(ordered(piece, (grad_qkv_part,)), axis) for piece, axis in ((gu_mine, "a"), (gu_given, "y")))
         gu_far = swap(gu_other, "a")
         gu_pieces = [gu_mine, gu_other, gu_near, gu_far]
@@ -800,7 +802,8 @@
                 filled = lax.dynamic_update_slice(filled, piece, (0, 0, 0, which_y, owner, 0))
             grad_gate, grad_up = (filled[:, o].reshape(shard_rows, 8 * ff_here) for o in range(2))
 
-        qkv_mine, qkv_given = split_rows(grad_qkv, y, shard_rows)
+        grad_down_full = grad_down_all.astype(F32)
+        qkv_mine, qkv_given = split_rows(grad_qkv, y, shard_rows, (grad_gate, grad_down_full))
         qkv_near, qkv_other = swap(qkv_mine, "a"), swap(qkv_given, "y")
         in_parts = []
 
@@ -811,6 +814,8 @@
 
         d_input, _ = plane_scatter(in_part, lean=True)
         d_input = d_middle + d_input
+        if planes == 4:
+            grad_out = plane_sum(ordered(grad_out, (grad_qkv, in_parts[2])))
 
         def qkv_place(o, j, s, scalars):
             owner, which_y = column_pair(j, scalars)
@@ -845,7 +850,7 @@
             own_gains[2],
             grad_gate,
             grad_up,
-            grad_down_all.astype(F32),
+            grad_down_full,
             own_gains[3],
         )
 

time: 886 us -> 870 us (0.982)
  waiting for transfers between devices: 377 us -> 356 us
    all_gather x1, waiting for transfers between devices: 10.7 us -> 1.24 us  [body(): lax.all_gather(beside(down_first, down_last, (gu_mine,)), ('a', 'c'), axi...]
    ppermute x117, waiting for transfers between devices: 317 us -> 308 us  [swap(): return lax.ppermute(values, axis, SWAP)]
    unnamed x238 -> x230, local copies, waits for them, and re-layouts: 93.5 us -> 97.8 us
    pallas_call x38 -> x37, Pallas kernels: 168 us -> 164 us  [call(): pl.pallas_call(body, grid=grid, in_specs=list(in_specs) + [anywhere] * ex...]
  transfers between devices with their start and end apart: 126 -> 126, of which waited for: 56 -> 58; matrix products, arithmetic and copies ran while one was open for 13% -> 13% of each run, Pallas kernels for 23% -> 23%
where the time goes in v3:
time: 870 us; the launch traced here: 860 us
  waiting for transfers between devices  356 us (41%)
  Pallas kernels  221 us (25%)
  local copies, waits for them, and re-layouts  129 us (15%)
  starting transfers between devices  76.2 us (9%)
  other arithmetic  50.3 us (6%)
  between operations  16.7 us (2%)
  matrix products  11.9 us (1%)
    ppermute x117, waiting for transfers between devices, swap(): return lax.ppermute(values, axis, SWAP)  308 us
    pallas_call x37, Pallas kernels, call(): pl.pallas_call(body, grid=grid, in_specs=list(in_specs) + [anywhere] * ex...  164 us
    unnamed x230, local copies, waits for them, and re-layouts  97.8 us
    ppermute x117, starting transfers between devices, swap(): return lax.ppermute(values, axis, SWAP)  75.8 us
    all_gather x3, waiting for transfers between devices, gather_planes(): return lax.all_gather(piece, 'z', axis=0, tiled=False)  33.9 us
    pallas_call x3, Pallas kernels, call_back(): pl.pallas_call(body, grid=(count,), in_specs=[resident(piece.shape) for p...  31.4 us
  transfers between devices with their start and end apart: 126, of which 58 were waited for; matrix products, arithmetic and copies ran while one was open for 13% of the time, Pallas kernels for 23%

profile of v3, /device:TPU:0, one launch (start us, length us, event | category | flops | bytes accessed | tf_op | source)
XLA Modules:
  0.0 860.3 jit_solution(91728873985829301)
XLA Ops:
  13.7 8.8 %collective-permute-done.9 = bf16[256,768]{1,0:T(8,128)(2,1)S(1)} collective-permute-done((bf16[256,768]{1,0:T(8,128)(2,1)S(1)}, bf16[256,768]{1,0:T(8,128)(2,1)S(1)}, u32[]{:S(2)}, u32[]{:S(2)}) %collective-permute-start.9) | collective-permute-done | bytes 393248 | tf_op jit(solution)/shard_map/ppermute | solution.py:42
  38.0 10.5 %collective-permute-done.refs_2_ = bf16[256,2048]{1,0:T(8,128)(2,1)S(1)} collective-permute-done((bf16[256,2048]{1,0:T(8,128)(2,1)}, bf16[256,2048]{1,0:T(8,128)(2,1)S(1)}, u32[]{:S(2)}, u32[]{:S(2)}) %collective-permute-start) | collective-permute-done | bytes 1048608 | tf_op jit(solution)/shard_map/ppermute | solution.py:42
  52.4 21.5 %collective-permute-done.36 = bf16[256,2048]{1,0:T(8,128)(2,1)S(1)} collective-permute-done((bf16[256,2048]{1,0:T(8,128)(2,1)}, bf16[256,2048]{1,0:T(8,128)(2,1)S(1)}, u32[]{:S(2)}, u32[]{:S(2)}) %collective-permute-start.36) | collective-permute-done | bytes 1048608 | tf_op jit(solution)/shard_map/ppermute | solution.py:42
  126.2 10.4 %shard_map.237 = (f32[2048,768]{1,0:T(8,128)S(1)}, f32[2,2048]{1,0:T(2,128)S(1)}) custom-call(bf16[2048,2048]{1,0:T(8,128)(2,1)} %constant_dynamic-update-slice_fusion.refs_0_, bf16[4,528,1024]{2,1,0:T(8,128)(2,1)S(1)} %bitcast.119, f32[2048,128]{1,0:T(8,128)S(1)} %get-tuple-element.178.refs_2_.refs_3_.refs_6_.refs_8_, ...), custom_call_target="tpu_custom_call" | custom-call | flops 6442450944 | bytes 19021824 | tf_op jit(solution)/shard_map/pallas_call | solution.py:145
  173.1 10.6 %collective-permute-done.22 = bf16[128,2048]{1,0:T(8,128)(2,1)S(1)} collective-permute-done((bf16[128,2048]{1,0:T(8,128)(2,1)S(1)}, bf16[128,2048]{1,0:T(8,128)(2,1)S(1)}, u32[]{:S(2)}, u32[]{:S(2)}) %collective-permute-start.22) | collective-permute-done | bytes 524320 | tf_op jit(solution)/shard_map/ppermute | solution.py:42
  186.7 21.7 %collective-permute-done.23 = bf16[256,2048]{1,0:T(8,128)(2,1)S(1)} collective-permute-done((bf16[256,2048]{1,0:T(8,128)(2,1)S(1)}, bf16[256,2048]{1,0:T(8,128)(2,1)S(1)}, u32[]{:S(2)}, u32[]{:S(2)}) %collective-permute-start.23) | collective-permute-done | bytes 1048608 | tf_op jit(solution)/shard_map/ppermute | solution.py:42
  215.0 21.5 %collective-permute-done.27 = bf16[256,2048]{1,0:T(8,128)(2,1)S(1)} collective-permute-done((bf16[256,2048]{1,0:T(8,128)(2,1)S(1)}, bf16[256,2048]{1,0:T(8,128)(2,1)S(1)}, u32[]{:S(2)}, u32[]{:S(2)}) %collective-permute-start.27) | collective-permute-done | bytes 1048608 | tf_op jit(solution)/shard_map/ppermute | solution.py:42
  239.5 9.2 %collective-permute-done.28 = bf16[128,2048]{1,0:T(8,128)(2,1)} collective-permute-done((bf16[128,2048]{1,0:T(8,128)(2,1)S(1)}, bf16[128,2048]{1,0:T(8,128)(2,1)}, u32[]{:S(2)}, u32[]{:S(2)}) %collective-permute-start.28) | collective-permute-done | bytes 524320 | tf_op jit(solution)/shard_map/ppermute | solution.py:42
  264.5 28.5 %all-gather.12.cloned.1.call-done = bf16[2560,2048]{1,0:T(8,128)(2,1)} async-done(((bf16[640,2048]{1,0:T(8,128)(2,1)}), bf16[2560,2048]{1,0:T(8,128)(2,1)}) %all-gather.12.cloned.1.call-update) | async-done | bytes 10485776 | tf_op jit(solution)/shard_map/all_gather | solution.py:539
  293.0 24.2 %shard_map.242 = (bf16[2048,2048]{1,0:T(8,128)(2,1)}, bf16[2048,1024]{1,0:T(8,128)(2,1)S(1)}, bf16[4,256,1024]{2,1,0:T(8,128)(2,1)S(1)}) custom-call(bf16[2048,2048]{1,0:T(8,128)(2,1)} %constant_dynamic-update-slice_fusion.10.refs_0_, bf16[4,640,2048]{2,1,0:T(8,128)(2,1)} %bitcast.134, bf16[4,640,2048]{2,1,0:T(8,128)(2,1)} %bitcast.135), custom_call_target="tpu_custom_call" | custom-call | flops 17179869184 | bytes 44040192 | tf_op jit(solution)/shard_map/pallas_call | solution.py:145
  356.3 9.9 %collective-permute-done.48 = bf16[128,1024]{1,0:T(8,128)(2,1)S(1)} collective-permute-done((bf16[128,1024]{1,0:T(8,128)(2,1)S(1)}, bf16[128,1024]{1,0:T(8,128)(2,1)S(1)}, u32[]{:S(2)}, u32[]{:S(2)}) %collective-permute-start.48) | collective-permute-done | bytes 262176 | tf_op jit(solution)/shard_map/ppermute | solution.py:42
  377.3 8.7 %collective-permute-done.49 = bf16[256,1024]{1,0:T(8,128)(2,1)S(1)} collective-permute-done((bf16[256,1024]{1,0:T(8,128)(2,1)S(1)}, bf16[256,1024]{1,0:T(8,128)(2,1)S(1)}, u32[]{:S(2)}, u32[]{:S(2)}) %collective-permute-start.49) | collective-permute-done | bytes 524320 | tf_op jit(solution)/shard_map/ppermute | solution.py:42
  391.4 9.1 %collective-permute-done.53.refs_2_ = bf16[256,1024]{1,0:T(8,128)(2,1)S(1)} collective-permute-done((bf16[256,1024]{1,0:T(8,128)(2,1)S(1)}, bf16[256,1024]{1,0:T(8,128)(2,1)S(1)}, u32[]{:S(2)}, u32[]{:S(2)}) %collective-permute-start.53) | collective-permute-done | bytes 524320 | tf_op jit(solution)/shard_map/ppermute | solution.py:42
  423.8 12.6 %collective-permute-done.62 = bf16[256,1024]{1,0:T(8,128)(2,1)S(1)} collective-permute-done((bf16[256,1024]{1,0:T(8,128)(2,1)S(1)}, bf16[256,1024]{1,0:T(8,128)(2,1)S(1)}, u32[]{:S(2)}, u32[]{:S(2)}) %collective-permute-start.62) | collective-permute-done | bytes 524320 | tf_op jit(solution)/shard_map/ppermute | solution.py:42
  463.3 16.0 %shard_map.252.refs_1_.refs_0_ = bf16[2048,2048]{1,0:T(8,128)(2,1)} custom-call(bf16[2048,1024]{1,0:T(8,128)(2,1)S(1)} %copy-done.70, bf16[2048,1024]{1,0:T(8,128)(2,1)} %copy-done.84, bf16[1024,1024]{1,0:T(8,128)(2,1)S(1)} %bitcast.124, bf16[1024,1024]{1,0:T(8,128)(2,1)S(1)} %copy-done.31, bf16[2048,2048]{1,0:T(8,128)(2,1)} %get-tuple-element.58.refs_4_, ...), custom_call_target="tpu_custom_call" | custom-call | flops 8589934592 | bytes 29360128 | tf_op jit(solution)/shard_map/pallas_call | solution.py:145
  483.8 22.8 %shard_map.254 = bf16[1,2048,2048]{2,1,0:T(8,128)(2,1)S(1)} custom-call(bf16[2048,2048]{1,0:T(8,128)(2,1)} %constant_dynamic-update-slice_fusion.10.refs_0_, bf16[2048,2048]{1,0:T(8,128)(2,1)} %shard_map.252.refs_1_.refs_0_, bf16[256,1024]{1,0:T(8,128)(2,1)S(1)} %shard_map.253.refs_2_.refs_0_), custom_call_target="tpu_custom_call" | custom-call | flops 17179869184 | bytes 25165824 | tf_op jit(solution)/shard_map/pallas_call | solution.py:145
  513.5 8.5 shard_map.255.refs_2_
  522.2 13.3 %shard_map.256.refs_3_ = bf16[1024,2048]{1,0:T(8,128)(2,1)S(1)} custom-call(bf16[2048,2048]{1,0:T(8,128)(2,1)} %shard_map.252.refs_1_.refs_0_, bf16[4,640,2048]{2,1,0:T(8,128)(2,1)} %bitcast.137, bf16[512,2048]{1,0:T(8,128)(2,1)S(1)} %shard_map.255.refs_2_, bf16[2048,2048]{1,0:T(8,128)(2,1)} %bitcast.107), custom_call_target="tpu_custom_call" | custom-call | flops 8589934592 | bytes 23068672 | tf_op jit(solution)/shard_map/pallas_call | solution.py:145
  536.8 8.6 shard_map.257
  548.5 11.5 %collective-permute-done.74 = bf16[128,2048]{1,0:T(8,128)(2,1)S(1)} collective-permute-done((bf16[128,2048]{1,0:T(8,128)(2,1)S(1)}, bf16[128,2048]{1,0:T(8,128)(2,1)S(1)}, u32[]{:S(2)}, u32[]{:S(2)}) %collective-permute-start.74) | collective-permute-done | bytes 524320 | tf_op jit(solution)/shard_map/ppermute | solution.py:42
  563.0 21.8 %collective-permute-done.75 = bf16[256,2048]{1,0:T(8,128)(2,1)S(1)} collective-permute-done((bf16[256,2048]{1,0:T(8,128)(2,1)S(1)}, bf16[256,2048]{1,0:T(8,128)(2,1)S(1)}, u32[]{:S(2)}, u32[]{:S(2)}) %collective-permute-start.75) | collective-permute-done | bytes 1048608 | tf_op jit(solution)/shard_map/ppermute | solution.py:42
  593.6 22.0 %collective-permute-done.82.refs_0_ = bf16[256,2048]{1,0:T(8,128)(2,1)} collective-permute-done((bf16[256,2048]{1,0:T(8,128)(2,1)}, bf16[256,2048]{1,0:T(8,128)(2,1)}, u32[]{:S(2)}, u32[]{:S(2)}) %collective-permute-start.82) | collective-permute-done | bytes 1048608 | tf_op jit(solution)/shard_map/ppermute | solution.py:42
  622.2 8.7 %shard_map.259 = (bf16[2048,2048]{1,0:T(8,128)(2,1)}, f32[2048,512]{1,0:T(8,128)}, bf16[2048,256]{1,0:T(8,128)(2,1)}, f32[2,2048]{1,0:T(2,128)}, f32[2,2,256]{2,1,0:T(2,128)}) custom-call(bf16[256,2048]{1,0:T(8,128)(2,1)} %subtract_convert_fusion.refs_0_, bf16[256,2048]{1,0:T(8,128)(2,1)} %collective-permute-done.80.refs_1_, ...), custom_call_target="tpu_custom_call" | custom-call | flops 939524096 | bytes 2097152 | tf_op jit(solution)/shard_map/pallas_call | solution.py:716
  635.7 14.2 %shard_map.262 = (bf16[2048,2048]{1,0:T(8,128)(2,1)}, f32[2048,512]{1,0:T(8,128)}, bf16[2048,256]{1,0:T(8,128)(2,1)}, f32[2,2048]{1,0:T(2,128)}, f32[4,2,256]{2,1,0:T(2,128)}) custom-call(bf16[256,2048]{1,0:T(8,128)(2,1)} %collective-permute-done.82.refs_0_, ...), custom_call_target="tpu_custom_call", output_to_operand_aliasing={{0}: (12, {}), {1}: (13, {}), {2}: (14, {}), {3}: (15, {})} | custom-call | flops 1879048192 | bytes 4194304 | tf_op jit(solution)/shard_map/pallas_call | solution.py:716
  662.8 8.5 shard_map.265
  700.0 10.7 %shard_map.269.refs_2_.refs_3_.refs_4_.refs_1_ = bf16[4,528,768]{2,1,0:T(8,128)(2,1)S(1)} custom-call(bf16[2048,2048]{1,0:T(8,128)(2,1)} %constant_dynamic-update-slice_fusion.refs_0_, bf16[2048,768]{1,0:T(8,128)(2,1)S(1)} %copy-done.15, bf16[1024,2048]{1,0:T(8,128)(2,1)S(1)} %copy-done.44), custom_call_target="tpu_custom_call" | custom-call | flops 6442450944 | bytes 14778368 | tf_op jit(solution)/shard_map/pallas_call | solution.py:145
  743.2 10.7 %collective-permute-done.98.refs_1_ = bf16[256,2048]{1,0:T(8,128)(2,1)} collective-permute-done((bf16[256,2048]{1,0:T(8,128)(2,1)S(1)}, bf16[256,2048]{1,0:T(8,128)(2,1)}, u32[]{:S(2)}, u32[]{:S(2)}) %collective-permute-start.98) | collective-permute-done | bytes 1048608 | tf_op jit(solution)/shard_map/ppermute | solution.py:42
  767.7 7.3 reduce-scatter.12.cloned.1.call-done.mine_ref.given_ref.refs_1_
  791.8 6.7 convert_element_type.372.refs_1_
  798.5 10.2 %shard_map.275 = (f32[256,8192]{1,0:T(8,128)}, f32[256,8192]{1,0:T(8,128)}) custom-call(s32[8,4]{1,0:T(8,128)S(1)} %stack.337.places_ref, bf16[256,2048]{1,0:T(8,128)(2,1)} %get-tuple-element.76.refs_2_.refs_0_, bf16[256,2048]{1,0:T(8,128)(2,1)} %collective-permute-done.98.refs_1_, bf16[256,2048]{1,0:T(8,128)(2,1)} %collective-permute-done.99.refs_2_, ...), custom_call_target="tpu_custom_call" | custom-call | bytes 25165824 | tf_op jit(solution)/shard_map/pallas_call | solution.py:96
  813.1 10.4 %collective-permute-done.105.refs_3_.refs_4_.refs_5_ = bf16[256,768]{1,0:T(8,128)(2,1)S(1)} collective-permute-done((bf16[256,768]{1,0:T(8,128)(2,1)}, bf16[256,768]{1,0:T(8,128)(2,1)S(1)}, u32[]{:S(2)}, u32[]{:S(2)}) %collective-permute-start.105) | collective-permute-done | bytes 393248 | tf_op jit(solution)/shard_map/ppermute | solution.py:42
  825.9 7.8 collective-permute-done.107.refs_9_.refs_10_.refs_11_
  (695 shorter events, 417.0 us)
Async XLA Ops:
  7.2 108.6 %all-gather.10.cloned.1.call-start = ((), (), s32[]{:S(2)}) async-start(), calls=%async_computation.11 | async-start | bytes 5406720 | tf_op jit(solution)/shard_map/all_gather | solution.py:539
  23.8 269.2 %all-gather.12.cloned.1.call-start = ((), (), s32[]{:S(2)}) async-start(), calls=%async_computation.12 | async-start | bytes 13107200 | tf_op jit(solution)/shard_map/all_gather | solution.py:539
  23.9 24.6 %collective-permute-start = (bf16[256,2048]{1,0:T(8,128)(2,1)}, bf16[256,2048]{1,0:T(8,128)(2,1)S(1)}, u32[]{:S(2)}, u32[]{:S(2)}) collective-permute-start(bf16[256,2048]{1,0:T(8,128)(2,1)} %param.14), channel_id=1, source_target_pairs={{0,1},{1,0},{2,3},{3,2},{4,5},{5,4},{6,7},{7,6},{8,9},{9,8},{10,11... | collective-permute-start | bytes 3145736 | tf_op jit(solution)/shard_map/ppermute | solution.py:42
  25.7 24.0 %collective-permute-start.2 = (bf16[256,2048]{1,0:T(8,128)(2,1)}, bf16[256,2048]{1,0:T(8,128)(2,1)S(1)}, u32[]{:S(2)}, u32[]{:S(2)}) collective-permute-start(bf16[256,2048]{1,0:T(8,128)(2,1)} %param.14), channel_id=1, source_target_pairs={{0,16},{16,0},{1,17},{17,1},{2,18},{18,2},{3,19},{19,3},{4,20},{20... | collective-permute-start | bytes 3145736 | tf_op jit(solution)/shard_map/ppermute | solution.py:42
  77.5 261.8 %all-gather.14.cloned.1.call-start = ((), (), s32[]{:S(2)}) async-start(), calls=%async_computation.13 | async-start | bytes 2621440 | tf_op jit(solution)/shard_map/all_gather | solution.py:539
  78.2 35.3 %collective-permute-start.8 = (bf16[256,2048]{1,0:T(8,128)(2,1)}, bf16[256,2048]{1,0:T(8,128)(2,1)}, u32[]{:S(2)}, u32[]{:S(2)}) collective-permute-start(bf16[256,2048]{1,0:T(8,128)(2,1)} %param.14), channel_id=1, source_target_pairs={{0,8},{8,0},{1,9},{9,1},{2,10},{10,2},{3,11},{11,3},{4,12},{12,4},... | collective-permute-start | bytes 3145736 | tf_op jit(solution)/shard_map/ppermute | solution.py:42
  183.9 24.6 %collective-permute-start.23 = (bf16[256,2048]{1,0:T(8,128)(2,1)S(1)}, bf16[256,2048]{1,0:T(8,128)(2,1)S(1)}, u32[]{:S(2)}, u32[]{:S(2)}) collective-permute-start(bf16[256,2048]{1,0:T(8,128)(2,1)S(1)} %pad_maximum_fusion.3), channel_id=1, source_target_pairs={{0,16},{16,0},{1,17},{17,1},{2,18},{18,2},{3,19},{19,3},{4,20},{20... | collective-permute-start | bytes 3145736 | tf_op jit(solution)/shard_map/ppermute | solution.py:42
  185.7 24.2 %collective-permute-start.26 = (bf16[256,2048]{1,0:T(8,128)(2,1)S(1)}, bf16[256,2048]{1,0:T(8,128)(2,1)S(1)}, u32[]{:S(2)}, u32[]{:S(2)}) collective-permute-start(bf16[256,2048]{1,0:T(8,128)(2,1)S(1)} %pad_maximum_fusion.4), channel_id=1, source_target_pairs={{0,1},{1,0},{2,3},{3,2},{4,5},{5,4},{6,7},{7,6},{8,9},{9,8},{10,11... | collective-permute-start | bytes 3145736 | tf_op jit(solution)/shard_map/ppermute | solution.py:42
  214.2 23.8 %collective-permute-start.29 = (bf16[256,2048]{1,0:T(8,128)(2,1)S(1)}, bf16[256,2048]{1,0:T(8,128)(2,1)S(1)}, u32[]{:S(2)}, u32[]{:S(2)}) collective-permute-start(bf16[256,2048]{1,0:T(8,128)(2,1)S(1)} %fusion.2), channel_id=1, source_target_pairs={{0,16},{16,0},{1,17},{17,1},{2,18},{18,2},{3,19},{19,3},{4,20},{20... | collective-permute-start | bytes 3145736 | tf_op jit(solution)/shard_map/ppermute | solution.py:42
  250.5 228.8 %reduce-scatter.6.cloned.1.call-start = ((), (), s32[]{:S(2)}) async-start(), calls=%async_computation.5 | async-start | bytes 2621440 | tf_op jit(solution)/shard_map/reduce_scatter | solution.py:659
  346.2 29.1 %collective-permute-start.38 = (bf16[256,1024]{1,0:T(8,128)(2,1)S(1)}, bf16[256,1024]{1,0:T(8,128)(2,1)S(1)}, u32[]{:S(2)}, u32[]{:S(2)}) collective-permute-start(bf16[256,1024]{1,0:T(8,128)(2,1)S(1)} %slice.439), channel_id=1, source_target_pairs={{0,8},{8,0},{1,9},{9,1},{2,10},{10,2},{3,11},{11,3},{4,12},{12,4},... | collective-permute-start | bytes 1572872 | tf_op jit(solution)/shard_map/ppermute | solution.py:42
  346.7 30.2 %collective-permute-start.44 = (bf16[256,1024]{1,0:T(8,128)(2,1)S(1)}, bf16[256,1024]{1,0:T(8,128)(2,1)S(1)}, u32[]{:S(2)}, u32[]{:S(2)}) collective-permute-start(bf16[256,1024]{1,0:T(8,128)(2,1)S(1)} %pad_maximum_fusion.9.refs_3_.refs_4_.refs_5_), channel_id=1, source_target_pairs={{0,1},{1,0},{2,3},{3,2},{4,5},{5,4},{6,7},{7,6},{8,9},{9,8},{10,11... | collective-permute-start | bytes 1572872 | tf_op jit(solution)/shard_map/ppermute | solution.py:42
  348.2 28.7 %collective-permute-start.41 = (bf16[256,1024]{1,0:T(8,128)(2,1)S(1)}, bf16[256,1024]{1,0:T(8,128)(2,1)S(1)}, u32[]{:S(2)}, u32[]{:S(2)}) collective-permute-start(bf16[256,1024]{1,0:T(8,128)(2,1)S(1)} %pad_maximum_fusion.8.refs_2_.refs_3_.refs_4_), channel_id=1, source_target_pairs={{0,16},{16,0},{1,17},{17,1},{2,18},{18,2},{3,19},{19,3},{4,20},{20... | collective-permute-start | bytes 1572872 | tf_op jit(solution)/shard_map/ppermute | solution.py:42
  421.0 198.2 %reduce-scatter.8.cloned.1.call-start = ((), (), s32[]{:S(2)}) async-start(), calls=%async_computation.6 | async-start | bytes 2621440 | tf_op jit(solution)/shard_map/reduce_scatter | solution.py:659
  457.8 197.6 %reduce-scatter.10.cloned.1.call-start = ((), (), s32[]{:S(2)}) async-start(), calls=%async_computation.7 | async-start | bytes 10485760 | tf_op jit(solution)/shard_map/reduce_scatter | solution.py:659
  510.1 185.8 %all-gather.8.cloned.1.call-start = ((), (), s32[]{:S(2)}) async-start(), calls=%async_computation.8 | async-start | bytes 5242880 | tf_op jit(solution)/shard_map/all_gather | solution.py:747
  560.2 24.5 %collective-permute-start.75 = (bf16[256,2048]{1,0:T(8,128)(2,1)S(1)}, bf16[256,2048]{1,0:T(8,128)(2,1)S(1)}, u32[]{:S(2)}, u32[]{:S(2)}) collective-permute-start(bf16[256,2048]{1,0:T(8,128)(2,1)S(1)} %pad_maximum_fusion.5), channel_id=1, source_target_pairs={{0,16},{16,0},{1,17},{17,1},{2,18},{18,2},{3,19},{19,3},{4,20},{20... | collective-permute-start | bytes 3145736 | tf_op jit(solution)/shard_map/ppermute | solution.py:42
  561.9 24.3 %collective-permute-start.78 = (bf16[256,2048]{1,0:T(8,128)(2,1)S(1)}, bf16[256,2048]{1,0:T(8,128)(2,1)S(1)}, u32[]{:S(2)}, u32[]{:S(2)}) collective-permute-start(bf16[256,2048]{1,0:T(8,128)(2,1)S(1)} %pad_maximum_fusion.6), channel_id=1, source_target_pairs={{0,1},{1,0},{2,3},{3,2},{4,5},{5,4},{6,7},{7,6},{8,9},{9,8},{10,11... | collective-permute-start | bytes 3145736 | tf_op jit(solution)/shard_map/ppermute | solution.py:42
  591.9 23.7 %collective-permute-start.82 = (bf16[256,2048]{1,0:T(8,128)(2,1)}, bf16[256,2048]{1,0:T(8,128)(2,1)}, u32[]{:S(2)}, u32[]{:S(2)}) collective-permute-start(bf16[256,2048]{1,0:T(8,128)(2,1)} %subtract_convert_fusion.refs_0_), channel_id=1, source_target_pairs={{0,16},{16,0},{1,17},{17,1},{2,18},{18,2},{3,19},{19,3},{4,20},{20... | collective-permute-start | bytes 3145736 | tf_op jit(solution)/shard_map/ppermute | solution.py:42
  593.5 28.7 %collective-permute-start.80 = (bf16[256,2048]{1,0:T(8,128)(2,1)}, bf16[256,2048]{1,0:T(8,128)(2,1)}, u32[]{:S(2)}, u32[]{:S(2)}) collective-permute-start(bf16[256,2048]{1,0:T(8,128)(2,1)} %subtract_convert_fusion.refs_0_), channel_id=1, source_target_pairs={{0,8},{8,0},{1,9},{9,1},{2,10},{10,2},{3,11},{11,3},{4,12},{12,4},... | collective-permute-start | bytes 3145736 | tf_op jit(solution)/shard_map/ppermute | solution.py:42
  659.1 115.8 %reduce-scatter.12.cloned.1.call-start = ((), (), s32[]{:S(2)}) async-start(), calls=%async_computation.9 | async-start | bytes 4055040 | tf_op jit(solution)/shard_map/reduce_scatter | solution.py:659
  713.0 120.6 %reduce-scatter.14.cloned.1.call-start = ((), (), s32[]{:S(2)}) async-start(), calls=%async_computation.10 | async-start | bytes 1310720 | tf_op jit(solution)/shard_map/reduce_scatter | solution.py:659
  728.4 25.5 %collective-permute-start.98 = (bf16[256,2048]{1,0:T(8,128)(2,1)S(1)}, bf16[256,2048]{1,0:T(8,128)(2,1)}, u32[]{:S(2)}, u32[]{:S(2)}) collective-permute-start(bf16[256,2048]{1,0:T(8,128)(2,1)S(1)} %shard_map.273), channel_id=1, source_target_pairs={{0,1},{1,0},{2,3},{3,2},{4,5},{5,4},{6,7},{7,6},{8,9},{9,8},{10,11... | collective-permute-start | bytes 3145736 | tf_op jit(solution)/shard_map/ppermute | solution.py:42
  734.8 26.1 %collective-permute-start.99 = (bf16[256,2048]{1,0:T(8,128)(2,1)S(1)}, bf16[256,2048]{1,0:T(8,128)(2,1)}, u32[]{:S(2)}, u32[]{:S(2)}) collective-permute-start(bf16[256,2048]{1,0:T(8,128)(2,1)S(1)} %shard_map.274), channel_id=1, source_target_pairs={{0,16},{16,0},{1,17},{17,1},{2,18},{18,2},{3,19},{19,3},{4,20},{20... | collective-permute-start | bytes 3145736 | tf_op jit(solution)/shard_map/ppermute | solution.py:42
  742.8 37.3 %collective-permute-start.96 = (bf16[256,2048]{1,0:T(8,128)(2,1)}, bf16[256,2048]{1,0:T(8,128)(2,1)}, u32[]{:S(2)}, u32[]{:S(2)}) collective-permute-start(bf16[256,2048]{1,0:T(8,128)(2,1)} %get-tuple-element.99), channel_id=1, source_target_pairs={{0,8},{8,0},{1,9},{9,1},{2,10},{10,2},{3,11},{11,3},{4,12},{12,4},... | collective-permute-start | bytes 3145736 | tf_op jit(solution)/shard_map/ppermute | solution.py:42
  753.9 29.0 %collective-permute-start.100 = (bf16[256,2048]{1,0:T(8,128)(2,1)}, bf16[256,2048]{1,0:T(8,128)(2,1)}, u32[]{:S(2)}, u32[]{:S(2)}) collective-permute-start(bf16[256,2048]{1,0:T(8,128)(2,1)} %collective-permute-done.98.refs_1_), channel_id=1, source_target_pairs={{0,16},{16,0},{1,17},{17,1},{2,18},{18,2},{3,19},{19,3},{4,20},{20... | collective-permute-start | bytes 3145736 | tf_op jit(solution)/shard_map/ppermute | solution.py:42
  756.2 27.8 %collective-permute-start.94 = (bf16[256,2048]{1,0:T(8,128)(2,1)}, bf16[256,2048]{1,0:T(8,128)(2,1)}, u32[]{:S(2)}, u32[]{:S(2)}) collective-permute-start(bf16[256,2048]{1,0:T(8,128)(2,1)} %add_convert_fusion.2.refs_2_), channel_id=1, source_target_pairs={{0,1},{1,0},{2,3},{3,2},{4,5},{5,4},{6,7},{7,6},{8,9},{9,8},{10,11... | collective-permute-start | bytes 3145736 | tf_op jit(solution)/shard_map/ppermute | solution.py:42
  760.9 28.8 %collective-permute-start.101 = (bf16[256,2048]{1,0:T(8,128)(2,1)}, bf16[256,2048]{1,0:T(8,128)(2,1)}, u32[]{:S(2)}, u32[]{:S(2)}) collective-permute-start(bf16[256,2048]{1,0:T(8,128)(2,1)} %get-tuple-element.76.refs_2_.refs_0_), channel_id=1, source_target_pairs={{0,8},{8,0},{1,9},{9,1},{2,10},{10,2},{3,11},{11,3},{4,12},{12,4},... | collective-permute-start | bytes 3145736 | tf_op jit(solution)/shard_map/ppermute | solution.py:42
  761.9 27.9 %collective-permute-start.103 = (bf16[256,2048]{1,0:T(8,128)(2,1)}, bf16[256,2048]{1,0:T(8,128)(2,1)}, u32[]{:S(2)}, u32[]{:S(2)}) collective-permute-start(bf16[256,2048]{1,0:T(8,128)(2,1)} %collective-permute-done.99.refs_2_), channel_id=1, source_target_pairs={{0,8},{8,0},{1,9},{9,1},{2,10},{10,2},{3,11},{11,3},{4,12},{12,4},... | collective-permute-start | bytes 3145736 | tf_op jit(solution)/shard_map/ppermute | solution.py:42
  784.0 41.2 %collective-permute-start.92 = (bf16[256,2048]{1,0:T(8,128)(2,1)}, bf16[256,2048]{1,0:T(8,128)(2,1)}, u32[]{:S(2)}, u32[]{:S(2)}) collective-permute-start(bf16[256,2048]{1,0:T(8,128)(2,1)} %slice.497), channel_id=1, source_target_pairs={{0,8},{8,0},{1,9},{9,1},{2,10},{10,2},{3,11},{11,3},{4,12},{12,4},... | collective-permute-start | bytes 3145736 | tf_op jit(solution)/shard_map/ppermute | solution.py:42
  789.7 35.6 %collective-permute-start.95 = (bf16[256,2048]{1,0:T(8,128)(2,1)}, bf16[256,2048]{1,0:T(8,128)(2,1)}, u32[]{:S(2)}, u32[]{:S(2)}) collective-permute-start(bf16[256,2048]{1,0:T(8,128)(2,1)} %get-tuple-element.96), channel_id=1, source_target_pairs={{0,16},{16,0},{1,17},{17,1},{2,18},{18,2},{3,19},{19,3},{4,20},{20... | collective-permute-start | bytes 3145736 | tf_op jit(solution)/shard_map/ppermute | solution.py:42
  789.8 43.8 %collective-permute-start.97 = (bf16[256,2048]{1,0:T(8,128)(2,1)}, bf16[256,2048]{1,0:T(8,128)(2,1)}, u32[]{:S(2)}, u32[]{:S(2)}) collective-permute-start(bf16[256,2048]{1,0:T(8,128)(2,1)} %get-tuple-element.97), channel_id=1, source_target_pairs={{0,1},{1,0},{2,3},{3,2},{4,5},{5,4},{6,7},{7,6},{8,9},{9,8},{10,11... | collective-permute-start | bytes 3145736 | tf_op jit(solution)/shard_map/ppermute | solution.py:42
  (185 other events, 1791.6 us)
Sparse Core Ops, SparseCore 0:
  23.9 84.3 all-gather.9
  110.5 182.4 all-gather.11
  295.1 44.1 all-gather.13
  421.2 41.5 reduce-scatter.5
  465.5 43.1 reduce-scatter.7
  511.6 143.7 reduce-scatter.9
  659.3 36.6 all-gather.7
  713.2 61.7 reduce-scatter.11
  780.2 27.2 reduce-scatter.13

commit v4 on v3

--- a/solution.py
+++ b/solution.py
@@ -652,7 +652,7 @@
         dm_halves = [d_mixed[:, cut].astype(BF) for cut in HALVES]
         dm_all = [plane_gather(dm_halves[0], early)]
         grad_down_parts = [product_tn(hidden, dm_all[0]).astype(BF)]
-        dm_all.append(plane_gather(ordered(dm_halves[1], early), hold=grad_down_parts))
+        dm_all.append(plane_gather(ordered(dm_halves[1], early)))
         grad_down_parts = grad_down_parts + [product_tn(hidden, dm_all[1]).astype(BF)]
 
         def plane_sum(values):

time: 870 us -> 870 us (level)
    pallas_call x37 -> x35, Pallas kernels: 164 us -> 164 us  [call(): pl.pallas_call(body, grid=grid, in_specs=list(in_specs) + [anywhere] * ex...]
    unnamed x230 -> x228, local copies, waits for them, and re-layouts: 97.8 us -> 97.7 us
where the time goes in v4:
time: 870 us; the launch traced here: 860 us
  waiting for transfers between devices  356 us (41%)
  Pallas kernels  220 us (25%)
  local copies, waits for them, and re-layouts  129 us (15%)
  starting transfers between devices  76.2 us (9%)
  other arithmetic  50.3 us (6%)
  between operations  16.7 us (2%)
  matrix products  11.9 us (1%)
    ppermute x117, waiting for transfers between devices, swap(): return lax.ppermute(values, axis, SWAP)  308 us
    pallas_call x35, Pallas kernels, call(): pl.pallas_call(body, grid=grid, in_specs=list(in_specs) + [anywhere] * ex...  164 us
    unnamed x228, local copies, waits for them, and re-layouts  97.7 us
    ppermute x117, starting transfers between devices, swap(): return lax.ppermute(values, axis, SWAP)  75.8 us
    all_gather x3, waiting for transfers between devices, gather_planes(): return lax.all_gather(piece, 'z', axis=0, tiled=False)  33.9 us
    pallas_call x3, Pallas kernels, call_back(): pl.pallas_call(body, grid=(count,), in_specs=[resident(piece.shape) for p...  31.3 us
  transfers between devices with their start and end apart: 126, of which 58 were waited for; matrix products, arithmetic and copies ran while one was open for 13% of the time, Pallas kernels for 23%

profile of v4, /device:TPU:0, one launch (start us, length us, event | category | flops | bytes accessed | tf_op | source)
XLA Modules:
  0.0 860.2 jit_solution(5082865439718659009)
XLA Ops:
  13.7 8.8 %collective-permute-done.9 = bf16[256,768]{1,0:T(8,128)(2,1)S(1)} collective-permute-done((bf16[256,768]{1,0:T(8,128)(2,1)S(1)}, bf16[256,768]{1,0:T(8,128)(2,1)S(1)}, u32[]{:S(2)}, u32[]{:S(2)}) %collective-permute-start.9) | collective-permute-done | bytes 393248 | tf_op jit(solution)/shard_map/ppermute | solution.py:42
  38.0 10.5 %collective-permute-done.refs_2_ = bf16[256,2048]{1,0:T(8,128)(2,1)S(1)} collective-permute-done((bf16[256,2048]{1,0:T(8,128)(2,1)}, bf16[256,2048]{1,0:T(8,128)(2,1)S(1)}, u32[]{:S(2)}, u32[]{:S(2)}) %collective-permute-start) | collective-permute-done | bytes 1048608 | tf_op jit(solution)/shard_map/ppermute | solution.py:42
  52.4 21.5 %collective-permute-done.36 = bf16[256,2048]{1,0:T(8,128)(2,1)S(1)} collective-permute-done((bf16[256,2048]{1,0:T(8,128)(2,1)}, bf16[256,2048]{1,0:T(8,128)(2,1)S(1)}, u32[]{:S(2)}, u32[]{:S(2)}) %collective-permute-start.36) | collective-permute-done | bytes 1048608 | tf_op jit(solution)/shard_map/ppermute | solution.py:42
  126.2 10.4 %shard_map.237 = (f32[2048,768]{1,0:T(8,128)S(1)}, f32[2,2048]{1,0:T(2,128)S(1)}) custom-call(bf16[2048,2048]{1,0:T(8,128)(2,1)} %constant_dynamic-update-slice_fusion.refs_0_, bf16[4,528,1024]{2,1,0:T(8,128)(2,1)S(1)} %bitcast.119, f32[2048,128]{1,0:T(8,128)S(1)} %get-tuple-element.178.refs_2_.refs_3_.refs_6_.refs_8_, ...), custom_call_target="tpu_custom_call" | custom-call | flops 6442450944 | bytes 19021824 | tf_op jit(solution)/shard_map/pallas_call | solution.py:145
  173.1 10.6 %collective-permute-done.22 = bf16[128,2048]{1,0:T(8,128)(2,1)S(1)} collective-permute-done((bf16[128,2048]{1,0:T(8,128)(2,1)S(1)}, bf16[128,2048]{1,0:T(8,128)(2,1)S(1)}, u32[]{:S(2)}, u32[]{:S(2)}) %collective-permute-start.22) | collective-permute-done | bytes 524320 | tf_op jit(solution)/shard_map/ppermute | solution.py:42
  186.7 21.8 %collective-permute-done.23 = bf16[256,2048]{1,0:T(8,128)(2,1)S(1)} collective-permute-done((bf16[256,2048]{1,0:T(8,128)(2,1)S(1)}, bf16[256,2048]{1,0:T(8,128)(2,1)S(1)}, u32[]{:S(2)}, u32[]{:S(2)}) %collective-permute-start.23) | collective-permute-done | bytes 1048608 | tf_op jit(solution)/shard_map/ppermute | solution.py:42
  215.0 21.6 %collective-permute-done.27 = bf16[256,2048]{1,0:T(8,128)(2,1)S(1)} collective-permute-done((bf16[256,2048]{1,0:T(8,128)(2,1)S(1)}, bf16[256,2048]{1,0:T(8,128)(2,1)S(1)}, u32[]{:S(2)}, u32[]{:S(2)}) %collective-permute-start.27) | collective-permute-done | bytes 1048608 | tf_op jit(solution)/shard_map/ppermute | solution.py:42
  239.4 9.3 %collective-permute-done.28 = bf16[128,2048]{1,0:T(8,128)(2,1)} collective-permute-done((bf16[128,2048]{1,0:T(8,128)(2,1)S(1)}, bf16[128,2048]{1,0:T(8,128)(2,1)}, u32[]{:S(2)}, u32[]{:S(2)}) %collective-permute-start.28) | collective-permute-done | bytes 524320 | tf_op jit(solution)/shard_map/ppermute | solution.py:42
  264.5 28.5 %all-gather.12.cloned.1.call-done = bf16[2560,2048]{1,0:T(8,128)(2,1)} async-done(((bf16[640,2048]{1,0:T(8,128)(2,1)}), bf16[2560,2048]{1,0:T(8,128)(2,1)}) %all-gather.12.cloned.1.call-update) | async-done | bytes 10485776 | tf_op jit(solution)/shard_map/all_gather | solution.py:539
  293.0 24.2 %shard_map.242 = (bf16[2048,2048]{1,0:T(8,128)(2,1)}, bf16[2048,1024]{1,0:T(8,128)(2,1)S(1)}, bf16[4,256,1024]{2,1,0:T(8,128)(2,1)S(1)}) custom-call(bf16[2048,2048]{1,0:T(8,128)(2,1)} %constant_dynamic-update-slice_fusion.10.refs_0_, bf16[4,640,2048]{2,1,0:T(8,128)(2,1)} %bitcast.134, bf16[4,640,2048]{2,1,0:T(8,128)(2,1)} %bitcast.135), custom_call_target="tpu_custom_call" | custom-call | flops 17179869184 | bytes 44040192 | tf_op jit(solution)/shard_map/pallas_call | solution.py:145
  356.3 9.9 %collective-permute-done.48 = bf16[128,1024]{1,0:T(8,128)(2,1)S(1)} collective-permute-done((bf16[128,1024]{1,0:T(8,128)(2,1)S(1)}, bf16[128,1024]{1,0:T(8,128)(2,1)S(1)}, u32[]{:S(2)}, u32[]{:S(2)}) %collective-permute-start.48) | collective-permute-done | bytes 262176 | tf_op jit(solution)/shard_map/ppermute | solution.py:42
  377.3 8.7 %collective-permute-done.49 = bf16[256,1024]{1,0:T(8,128)(2,1)S(1)} collective-permute-done((bf16[256,1024]{1,0:T(8,128)(2,1)S(1)}, bf16[256,1024]{1,0:T(8,128)(2,1)S(1)}, u32[]{:S(2)}, u32[]{:S(2)}) %collective-permute-start.49) | collective-permute-done | bytes 524320 | tf_op jit(solution)/shard_map/ppermute | solution.py:42
  391.4 9.1 %collective-permute-done.53.refs_2_ = bf16[256,1024]{1,0:T(8,128)(2,1)S(1)} collective-permute-done((bf16[256,1024]{1,0:T(8,128)(2,1)S(1)}, bf16[256,1024]{1,0:T(8,128)(2,1)S(1)}, u32[]{:S(2)}, u32[]{:S(2)}) %collective-permute-start.53) | collective-permute-done | bytes 524320 | tf_op jit(solution)/shard_map/ppermute | solution.py:42
  423.6 12.6 %collective-permute-done.62 = bf16[256,1024]{1,0:T(8,128)(2,1)S(1)} collective-permute-done((bf16[256,1024]{1,0:T(8,128)(2,1)S(1)}, bf16[256,1024]{1,0:T(8,128)(2,1)S(1)}, u32[]{:S(2)}, u32[]{:S(2)}) %collective-permute-start.62) | collective-permute-done | bytes 524320 | tf_op jit(solution)/shard_map/ppermute | solution.py:42
  463.1 16.0 %shard_map.250.refs_1_.refs_0_ = bf16[2048,2048]{1,0:T(8,128)(2,1)} custom-call(bf16[2048,1024]{1,0:T(8,128)(2,1)S(1)} %copy-done.69, bf16[2048,1024]{1,0:T(8,128)(2,1)} %copy-done.83, bf16[1024,1024]{1,0:T(8,128)(2,1)S(1)} %bitcast.124, bf16[1024,1024]{1,0:T(8,128)(2,1)S(1)} %copy-done.29, bf16[2048,2048]{1,0:T(8,128)(2,1)} %get-tuple-element.58.refs_4_, ...), custom_call_target="tpu_custom_call" | custom-call | flops 8589934592 | bytes 29360128 | tf_op jit(solution)/shard_map/pallas_call | solution.py:145
  483.6 22.8 %shard_map.252 = bf16[1,2048,2048]{2,1,0:T(8,128)(2,1)S(1)} custom-call(bf16[2048,2048]{1,0:T(8,128)(2,1)} %constant_dynamic-update-slice_fusion.10.refs_0_, bf16[2048,2048]{1,0:T(8,128)(2,1)} %shard_map.250.refs_1_.refs_0_, bf16[256,1024]{1,0:T(8,128)(2,1)S(1)} %shard_map.251.refs_2_.refs_0_), custom_call_target="tpu_custom_call" | custom-call | flops 17179869184 | bytes 25165824 | tf_op jit(solution)/shard_map/pallas_call | solution.py:145
  513.3 8.3 shard_map.253.refs_2_
  521.9 13.3 %shard_map.254.refs_3_ = bf16[1024,2048]{1,0:T(8,128)(2,1)S(1)} custom-call(bf16[2048,2048]{1,0:T(8,128)(2,1)} %shard_map.250.refs_1_.refs_0_, bf16[4,640,2048]{2,1,0:T(8,128)(2,1)} %bitcast.137, bf16[512,2048]{1,0:T(8,128)(2,1)S(1)} %shard_map.253.refs_2_, bf16[2048,2048]{1,0:T(8,128)(2,1)} %bitcast.107), custom_call_target="tpu_custom_call" | custom-call | flops 8589934592 | bytes 23068672 | tf_op jit(solution)/shard_map/pallas_call | solution.py:145
  536.4 8.6 shard_map.255
  548.3 11.3 %collective-permute-done.74 = bf16[128,2048]{1,0:T(8,128)(2,1)S(1)} collective-permute-done((bf16[128,2048]{1,0:T(8,128)(2,1)S(1)}, bf16[128,2048]{1,0:T(8,128)(2,1)S(1)}, u32[]{:S(2)}, u32[]{:S(2)}) %collective-permute-start.74) | collective-permute-done | bytes 524320 | tf_op jit(solution)/shard_map/ppermute | solution.py:42
  562.6 21.8 %collective-permute-done.75 = bf16[256,2048]{1,0:T(8,128)(2,1)S(1)} collective-permute-done((bf16[256,2048]{1,0:T(8,128)(2,1)S(1)}, bf16[256,2048]{1,0:T(8,128)(2,1)S(1)}, u32[]{:S(2)}, u32[]{:S(2)}) %collective-permute-start.75) | collective-permute-done | bytes 1048608 | tf_op jit(solution)/shard_map/ppermute | solution.py:42
  593.4 22.0 %collective-permute-done.82.refs_0_ = bf16[256,2048]{1,0:T(8,128)(2,1)} collective-permute-done((bf16[256,2048]{1,0:T(8,128)(2,1)}, bf16[256,2048]{1,0:T(8,128)(2,1)}, u32[]{:S(2)}, u32[]{:S(2)}) %collective-permute-start.82) | collective-permute-done | bytes 1048608 | tf_op jit(solution)/shard_map/ppermute | solution.py:42
  622.1 8.7 %shard_map.257 = (bf16[2048,2048]{1,0:T(8,128)(2,1)}, f32[2048,512]{1,0:T(8,128)}, bf16[2048,256]{1,0:T(8,128)(2,1)}, f32[2,2048]{1,0:T(2,128)}, f32[2,2,256]{2,1,0:T(2,128)}) custom-call(bf16[256,2048]{1,0:T(8,128)(2,1)} %subtract_convert_fusion.refs_0_, bf16[256,2048]{1,0:T(8,128)(2,1)} %collective-permute-done.80.refs_1_, ...), custom_call_target="tpu_custom_call" | custom-call | flops 939524096 | bytes 2097152 | tf_op jit(solution)/shard_map/pallas_call | solution.py:716
  635.5 14.2 %shard_map.260 = (bf16[2048,2048]{1,0:T(8,128)(2,1)}, f32[2048,512]{1,0:T(8,128)}, bf16[2048,256]{1,0:T(8,128)(2,1)}, f32[2,2048]{1,0:T(2,128)}, f32[4,2,256]{2,1,0:T(2,128)}) custom-call(bf16[256,2048]{1,0:T(8,128)(2,1)} %collective-permute-done.82.refs_0_, ...), custom_call_target="tpu_custom_call", output_to_operand_aliasing={{0}: (12, {}), {1}: (13, {}), {2}: (14, {}), {3}: (15, {})} | custom-call | flops 1879048192 | bytes 4194304 | tf_op jit(solution)/shard_map/pallas_call | solution.py:716
  662.8 8.5 shard_map.263
  700.0 10.7 %shard_map.267.refs_2_.refs_3_.refs_4_.refs_1_ = bf16[4,528,768]{2,1,0:T(8,128)(2,1)S(1)} custom-call(bf16[2048,2048]{1,0:T(8,128)(2,1)} %constant_dynamic-update-slice_fusion.refs_0_, bf16[2048,768]{1,0:T(8,128)(2,1)S(1)} %copy-done.15, bf16[1024,2048]{1,0:T(8,128)(2,1)S(1)} %copy-done.42), custom_call_target="tpu_custom_call" | custom-call | flops 6442450944 | bytes 14778368 | tf_op jit(solution)/shard_map/pallas_call | solution.py:145
  743.2 10.7 %collective-permute-done.98.refs_1_ = bf16[256,2048]{1,0:T(8,128)(2,1)} collective-permute-done((bf16[256,2048]{1,0:T(8,128)(2,1)S(1)}, bf16[256,2048]{1,0:T(8,128)(2,1)}, u32[]{:S(2)}, u32[]{:S(2)}) %collective-permute-start.98) | collective-permute-done | bytes 1048608 | tf_op jit(solution)/shard_map/ppermute | solution.py:42
  767.7 7.3 reduce-scatter.12.cloned.1.call-done.mine_ref.given_ref.refs_1_
  791.8 6.7 convert_element_type.372.refs_1_
  798.5 10.2 %shard_map.273 = (f32[256,8192]{1,0:T(8,128)}, f32[256,8192]{1,0:T(8,128)}) custom-call(s32[8,4]{1,0:T(8,128)S(1)} %stack.337.places_ref, bf16[256,2048]{1,0:T(8,128)(2,1)} %get-tuple-element.76.refs_2_.refs_0_, bf16[256,2048]{1,0:T(8,128)(2,1)} %collective-permute-done.98.refs_1_, bf16[256,2048]{1,0:T(8,128)(2,1)} %collective-permute-done.99.refs_2_, ...), custom_call_target="tpu_custom_call" | custom-call | bytes 25165824 | tf_op jit(solution)/shard_map/pallas_call | solution.py:96
  813.1 10.4 %collective-permute-done.105.refs_3_.refs_4_.refs_5_ = bf16[256,768]{1,0:T(8,128)(2,1)S(1)} collective-permute-done((bf16[256,768]{1,0:T(8,128)(2,1)}, bf16[256,768]{1,0:T(8,128)(2,1)S(1)}, u32[]{:S(2)}, u32[]{:S(2)}) %collective-permute-start.105) | collective-permute-done | bytes 393248 | tf_op jit(solution)/shard_map/ppermute | solution.py:42
  825.9 7.8 collective-permute-done.107.refs_9_.refs_10_.refs_11_
  (691 shorter events, 417.1 us)
Async XLA Ops:
  7.2 108.6 %all-gather.10.cloned.1.call-start = ((), (), s32[]{:S(2)}) async-start(), calls=%async_computation.11 | async-start | bytes 5406720 | tf_op jit(solution)/shard_map/all_gather | solution.py:539
  23.8 269.2 %all-gather.12.cloned.1.call-start = ((), (), s32[]{:S(2)}) async-start(), calls=%async_computation.12 | async-start | bytes 13107200 | tf_op jit(solution)/shard_map/all_gather | solution.py:539
  23.9 24.6 %collective-permute-start = (bf16[256,2048]{1,0:T(8,128)(2,1)}, bf16[256,2048]{1,0:T(8,128)(2,1)S(1)}, u32[]{:S(2)}, u32[]{:S(2)}) collective-permute-start(bf16[256,2048]{1,0:T(8,128)(2,1)} %param.14), channel_id=1, source_target_pairs={{0,1},{1,0},{2,3},{3,2},{4,5},{5,4},{6,7},{7,6},{8,9},{9,8},{10,11... | collective-permute-start | bytes 3145736 | tf_op jit(solution)/shard_map/ppermute | solution.py:42
  25.7 24.0 %collective-permute-start.2 = (bf16[256,2048]{1,0:T(8,128)(2,1)}, bf16[256,2048]{1,0:T(8,128)(2,1)S(1)}, u32[]{:S(2)}, u32[]{:S(2)}) collective-permute-start(bf16[256,2048]{1,0:T(8,128)(2,1)} %param.14), channel_id=1, source_target_pairs={{0,16},{16,0},{1,17},{17,1},{2,18},{18,2},{3,19},{19,3},{4,20},{20... | collective-permute-start | bytes 3145736 | tf_op jit(solution)/shard_map/ppermute | solution.py:42
  77.5 261.8 %all-gather.14.cloned.1.call-start = ((), (), s32[]{:S(2)}) async-start(), calls=%async_computation.13 | async-start | bytes 2621440 | tf_op jit(solution)/shard_map/all_gather | solution.py:539
  78.2 35.3 %collective-permute-start.8 = (bf16[256,2048]{1,0:T(8,128)(2,1)}, bf16[256,2048]{1,0:T(8,128)(2,1)}, u32[]{:S(2)}, u32[]{:S(2)}) collective-permute-start(bf16[256,2048]{1,0:T(8,128)(2,1)} %param.14), channel_id=1, source_target_pairs={{0,8},{8,0},{1,9},{9,1},{2,10},{10,2},{3,11},{11,3},{4,12},{12,4},... | collective-permute-start | bytes 3145736 | tf_op jit(solution)/shard_map/ppermute | solution.py:42
  183.9 24.6 %collective-permute-start.23 = (bf16[256,2048]{1,0:T(8,128)(2,1)S(1)}, bf16[256,2048]{1,0:T(8,128)(2,1)S(1)}, u32[]{:S(2)}, u32[]{:S(2)}) collective-permute-start(bf16[256,2048]{1,0:T(8,128)(2,1)S(1)} %pad_maximum_fusion.3), channel_id=1, source_target_pairs={{0,16},{16,0},{1,17},{17,1},{2,18},{18,2},{3,19},{19,3},{4,20},{20... | collective-permute-start | bytes 3145736 | tf_op jit(solution)/shard_map/ppermute | solution.py:42
  185.7 24.2 %collective-permute-start.26 = (bf16[256,2048]{1,0:T(8,128)(2,1)S(1)}, bf16[256,2048]{1,0:T(8,128)(2,1)S(1)}, u32[]{:S(2)}, u32[]{:S(2)}) collective-permute-start(bf16[256,2048]{1,0:T(8,128)(2,1)S(1)} %pad_maximum_fusion.4), channel_id=1, source_target_pairs={{0,1},{1,0},{2,3},{3,2},{4,5},{5,4},{6,7},{7,6},{8,9},{9,8},{10,11... | collective-permute-start | bytes 3145736 | tf_op jit(solution)/shard_map/ppermute | solution.py:42
  214.2 23.8 %collective-permute-start.29 = (bf16[256,2048]{1,0:T(8,128)(2,1)S(1)}, bf16[256,2048]{1,0:T(8,128)(2,1)S(1)}, u32[]{:S(2)}, u32[]{:S(2)}) collective-permute-start(bf16[256,2048]{1,0:T(8,128)(2,1)S(1)} %fusion.2), channel_id=1, source_target_pairs={{0,16},{16,0},{1,17},{17,1},{2,18},{18,2},{3,19},{19,3},{4,20},{20... | collective-permute-start | bytes 3145736 | tf_op jit(solution)/shard_map/ppermute | solution.py:42
  250.6 228.5 %reduce-scatter.6.cloned.1.call-start = ((), (), s32[]{:S(2)}) async-start(), calls=%async_computation.5 | async-start | bytes 2621440 | tf_op jit(solution)/shard_map/reduce_scatter | solution.py:659
  346.2 29.1 %collective-permute-start.38 = (bf16[256,1024]{1,0:T(8,128)(2,1)S(1)}, bf16[256,1024]{1,0:T(8,128)(2,1)S(1)}, u32[]{:S(2)}, u32[]{:S(2)}) collective-permute-start(bf16[256,1024]{1,0:T(8,128)(2,1)S(1)} %slice.439), channel_id=1, source_target_pairs={{0,8},{8,0},{1,9},{9,1},{2,10},{10,2},{3,11},{11,3},{4,12},{12,4},... | collective-permute-start | bytes 1572872 | tf_op jit(solution)/shard_map/ppermute | solution.py:42
  346.7 30.2 %collective-permute-start.44 = (bf16[256,1024]{1,0:T(8,128)(2,1)S(1)}, bf16[256,1024]{1,0:T(8,128)(2,1)S(1)}, u32[]{:S(2)}, u32[]{:S(2)}) collective-permute-start(bf16[256,1024]{1,0:T(8,128)(2,1)S(1)} %pad_maximum_fusion.9.refs_3_.refs_4_.refs_5_), channel_id=1, source_target_pairs={{0,1},{1,0},{2,3},{3,2},{4,5},{5,4},{6,7},{7,6},{8,9},{9,8},{10,11... | collective-permute-start | bytes 1572872 | tf_op jit(solution)/shard_map/ppermute | solution.py:42
  348.2 28.7 %collective-permute-start.41 = (bf16[256,1024]{1,0:T(8,128)(2,1)S(1)}, bf16[256,1024]{1,0:T(8,128)(2,1)S(1)}, u32[]{:S(2)}, u32[]{:S(2)}) collective-permute-start(bf16[256,1024]{1,0:T(8,128)(2,1)S(1)} %pad_maximum_fusion.8.refs_2_.refs_3_.refs_4_), channel_id=1, source_target_pairs={{0,16},{16,0},{1,17},{17,1},{2,18},{18,2},{3,19},{19,3},{4,20},{20... | collective-permute-start | bytes 1572872 | tf_op jit(solution)/shard_map/ppermute | solution.py:42
  421.1 198.1 %reduce-scatter.8.cloned.1.call-start = ((), (), s32[]{:S(2)}) async-start(), calls=%async_computation.6 | async-start | bytes 2621440 | tf_op jit(solution)/shard_map/reduce_scatter | solution.py:659
  457.6 197.7 %reduce-scatter.10.cloned.1.call-start = ((), (), s32[]{:S(2)}) async-start(), calls=%async_computation.7 | async-start | bytes 10485760 | tf_op jit(solution)/shard_map/reduce_scatter | solution.py:659
  509.9 186.0 %all-gather.8.cloned.1.call-start = ((), (), s32[]{:S(2)}) async-start(), calls=%async_computation.8 | async-start | bytes 5242880 | tf_op jit(solution)/shard_map/all_gather | solution.py:747
  559.9 24.6 %collective-permute-start.75 = (bf16[256,2048]{1,0:T(8,128)(2,1)S(1)}, bf16[256,2048]{1,0:T(8,128)(2,1)S(1)}, u32[]{:S(2)}, u32[]{:S(2)}) collective-permute-start(bf16[256,2048]{1,0:T(8,128)(2,1)S(1)} %pad_maximum_fusion.5), channel_id=1, source_target_pairs={{0,16},{16,0},{1,17},{17,1},{2,18},{18,2},{3,19},{19,3},{4,20},{20... | collective-permute-start | bytes 3145736 | tf_op jit(solution)/shard_map/ppermute | solution.py:42
  561.7 24.3 %collective-permute-start.78 = (bf16[256,2048]{1,0:T(8,128)(2,1)S(1)}, bf16[256,2048]{1,0:T(8,128)(2,1)S(1)}, u32[]{:S(2)}, u32[]{:S(2)}) collective-permute-start(bf16[256,2048]{1,0:T(8,128)(2,1)S(1)} %pad_maximum_fusion.6), channel_id=1, source_target_pairs={{0,1},{1,0},{2,3},{3,2},{4,5},{5,4},{6,7},{7,6},{8,9},{9,8},{10,11... | collective-permute-start | bytes 3145736 | tf_op jit(solution)/shard_map/ppermute | solution.py:42
  591.7 23.7 %collective-permute-start.82 = (bf16[256,2048]{1,0:T(8,128)(2,1)}, bf16[256,2048]{1,0:T(8,128)(2,1)}, u32[]{:S(2)}, u32[]{:S(2)}) collective-permute-start(bf16[256,2048]{1,0:T(8,128)(2,1)} %subtract_convert_fusion.refs_0_), channel_id=1, source_target_pairs={{0,16},{16,0},{1,17},{17,1},{2,18},{18,2},{3,19},{19,3},{4,20},{20... | collective-permute-start | bytes 3145736 | tf_op jit(solution)/shard_map/ppermute | solution.py:42
  593.4 28.7 %collective-permute-start.80 = (bf16[256,2048]{1,0:T(8,128)(2,1)}, bf16[256,2048]{1,0:T(8,128)(2,1)}, u32[]{:S(2)}, u32[]{:S(2)}) collective-permute-start(bf16[256,2048]{1,0:T(8,128)(2,1)} %subtract_convert_fusion.refs_0_), channel_id=1, source_target_pairs={{0,8},{8,0},{1,9},{9,1},{2,10},{10,2},{3,11},{11,3},{4,12},{12,4},... | collective-permute-start | bytes 3145736 | tf_op jit(solution)/shard_map/ppermute | solution.py:42
  659.1 115.8 %reduce-scatter.12.cloned.1.call-start = ((), (), s32[]{:S(2)}) async-start(), calls=%async_computation.9 | async-start | bytes 4055040 | tf_op jit(solution)/shard_map/reduce_scatter | solution.py:659
  713.0 120.7 %reduce-scatter.14.cloned.1.call-start = ((), (), s32[]{:S(2)}) async-start(), calls=%async_computation.10 | async-start | bytes 1310720 | tf_op jit(solution)/shard_map/reduce_scatter | solution.py:659
  728.4 25.5 %collective-permute-start.98 = (bf16[256,2048]{1,0:T(8,128)(2,1)S(1)}, bf16[256,2048]{1,0:T(8,128)(2,1)}, u32[]{:S(2)}, u32[]{:S(2)}) collective-permute-start(bf16[256,2048]{1,0:T(8,128)(2,1)S(1)} %shard_map.271), channel_id=1, source_target_pairs={{0,1},{1,0},{2,3},{3,2},{4,5},{5,4},{6,7},{7,6},{8,9},{9,8},{10,11... | collective-permute-start | bytes 3145736 | tf_op jit(solution)/shard_map/ppermute | solution.py:42
  734.7 26.1 %collective-permute-start.99 = (bf16[256,2048]{1,0:T(8,128)(2,1)S(1)}, bf16[256,2048]{1,0:T(8,128)(2,1)}, u32[]{:S(2)}, u32[]{:S(2)}) collective-permute-start(bf16[256,2048]{1,0:T(8,128)(2,1)S(1)} %shard_map.272), channel_id=1, source_target_pairs={{0,16},{16,0},{1,17},{17,1},{2,18},{18,2},{3,19},{19,3},{4,20},{20... | collective-permute-start | bytes 3145736 | tf_op jit(solution)/shard_map/ppermute | solution.py:42
  742.8 37.3 %collective-permute-start.96 = (bf16[256,2048]{1,0:T(8,128)(2,1)}, bf16[256,2048]{1,0:T(8,128)(2,1)}, u32[]{:S(2)}, u32[]{:S(2)}) collective-permute-start(bf16[256,2048]{1,0:T(8,128)(2,1)} %get-tuple-element.99), channel_id=1, source_target_pairs={{0,8},{8,0},{1,9},{9,1},{2,10},{10,2},{3,11},{11,3},{4,12},{12,4},... | collective-permute-start | bytes 3145736 | tf_op jit(solution)/shard_map/ppermute | solution.py:42
  753.9 29.0 %collective-permute-start.100 = (bf16[256,2048]{1,0:T(8,128)(2,1)}, bf16[256,2048]{1,0:T(8,128)(2,1)}, u32[]{:S(2)}, u32[]{:S(2)}) collective-permute-start(bf16[256,2048]{1,0:T(8,128)(2,1)} %collective-permute-done.98.refs_1_), channel_id=1, source_target_pairs={{0,16},{16,0},{1,17},{17,1},{2,18},{18,2},{3,19},{19,3},{4,20},{20... | collective-permute-start | bytes 3145736 | tf_op jit(solution)/shard_map/ppermute | solution.py:42
  756.2 27.8 %collective-permute-start.94 = (bf16[256,2048]{1,0:T(8,128)(2,1)}, bf16[256,2048]{1,0:T(8,128)(2,1)}, u32[]{:S(2)}, u32[]{:S(2)}) collective-permute-start(bf16[256,2048]{1,0:T(8,128)(2,1)} %add_convert_fusion.2.refs_2_), channel_id=1, source_target_pairs={{0,1},{1,0},{2,3},{3,2},{4,5},{5,4},{6,7},{7,6},{8,9},{9,8},{10,11... | collective-permute-start | bytes 3145736 | tf_op jit(solution)/shard_map/ppermute | solution.py:42
  760.9 28.8 %collective-permute-start.101 = (bf16[256,2048]{1,0:T(8,128)(2,1)}, bf16[256,2048]{1,0:T(8,128)(2,1)}, u32[]{:S(2)}, u32[]{:S(2)}) collective-permute-start(bf16[256,2048]{1,0:T(8,128)(2,1)} %get-tuple-element.76.refs_2_.refs_0_), channel_id=1, source_target_pairs={{0,8},{8,0},{1,9},{9,1},{2,10},{10,2},{3,11},{11,3},{4,12},{12,4},... | collective-permute-start | bytes 3145736 | tf_op jit(solution)/shard_map/ppermute | solution.py:42
  761.9 27.9 %collective-permute-start.103 = (bf16[256,2048]{1,0:T(8,128)(2,1)}, bf16[256,2048]{1,0:T(8,128)(2,1)}, u32[]{:S(2)}, u32[]{:S(2)}) collective-permute-start(bf16[256,2048]{1,0:T(8,128)(2,1)} %collective-permute-done.99.refs_2_), channel_id=1, source_target_pairs={{0,8},{8,0},{1,9},{9,1},{2,10},{10,2},{3,11},{11,3},{4,12},{12,4},... | collective-permute-start | bytes 3145736 | tf_op jit(solution)/shard_map/ppermute | solution.py:42
  784.0 41.2 %collective-permute-start.92 = (bf16[256,2048]{1,0:T(8,128)(2,1)}, bf16[256,2048]{1,0:T(8,128)(2,1)}, u32[]{:S(2)}, u32[]{:S(2)}) collective-permute-start(bf16[256,2048]{1,0:T(8,128)(2,1)} %slice.497), channel_id=1, source_target_pairs={{0,8},{8,0},{1,9},{9,1},{2,10},{10,2},{3,11},{11,3},{4,12},{12,4},... | collective-permute-start | bytes 3145736 | tf_op jit(solution)/shard_map/ppermute | solution.py:42
  789.7 35.6 %collective-permute-start.95 = (bf16[256,2048]{1,0:T(8,128)(2,1)}, bf16[256,2048]{1,0:T(8,128)(2,1)}, u32[]{:S(2)}, u32[]{:S(2)}) collective-permute-start(bf16[256,2048]{1,0:T(8,128)(2,1)} %get-tuple-element.96), channel_id=1, source_target_pairs={{0,16},{16,0},{1,17},{17,1},{2,18},{18,2},{3,19},{19,3},{4,20},{20... | collective-permute-start | bytes 3145736 | tf_op jit(solution)/shard_map/ppermute | solution.py:42
  789.8 43.8 %collective-permute-start.97 = (bf16[256,2048]{1,0:T(8,128)(2,1)}, bf16[256,2048]{1,0:T(8,128)(2,1)}, u32[]{:S(2)}, u32[]{:S(2)}) collective-permute-start(bf16[256,2048]{1,0:T(8,128)(2,1)} %get-tuple-element.97), channel_id=1, source_target_pairs={{0,1},{1,0},{2,3},{3,2},{4,5},{5,4},{6,7},{7,6},{8,9},{9,8},{10,11... | collective-permute-start | bytes 3145736 | tf_op jit(solution)/shard_map/ppermute | solution.py:42
  (184 other events, 1777.6 us)
Sparse Core Ops, SparseCore 0:
  23.9 84.3 all-gather.9
  110.5 182.4 all-gather.11
  295.1 44.1 all-gather.13
  421.2 41.5 reduce-scatter.5
  465.6 43.1 reduce-scatter.7
  511.5 143.8 reduce-scatter.9
  659.2 36.6 all-gather.7
  713.1 61.7 reduce-scatter.11
  780.2 27.2 reduce-scatter.13
